TPU v7x, 128 devices: a whole 4x4x4 slice. The times are simulated.
128 devices in a mesh: dp: 8 (over y, core), seq: 16 (over z, x).
Axes of the slice: x: 4, y: 4, z: 4, core: 2. Of those that a mesh axis runs over, the one named last changes fastest.
Arguments:
- query: bfloat16 [16, 2048, 32, 128], P('dp', 'seq'), may hold values from -128 to 128
- keys: bfloat16 [16, 2048, 4, 128], P('dp', 'seq'), may hold values from -4.5 to 4.5
- values: bfloat16 [16, 2048, 4, 128], P('dp', 'seq'), may hold values from -6 to 6
- output: bfloat16 [16, 2048, 32, 128], P('dp', 'seq'), may hold values from -6 to 6
- out_grad: bfloat16 [16, 2048, 32, 128], P('dp', 'seq'), may hold values from -6 to 6
- lengths: int32 [16], P('dp'), may hold values from 341 to 2048, as said below
- margins: float32 [8], P('dp'), may hold values from -3 to 3
Outputs:
- query_grad: bfloat16 [16, 2048, 32, 128], P('dp', 'seq')
- key_grad: bfloat16 [16, 2048, 4, 128], P('dp', 'seq')
- value_grad: bfloat16 [16, 2048, 4, 128], P('dp', 'seq')
Inputs may be any that keep to these rules, and one draw needn't show every extreme that they name: `lengths`: sequence 2p is pair p's chosen response and 2p + 1 its rejected one; some sequence has exactly 2048 tokens.
All inputs are finite; a program needn't handle non-finite values.
Results may differ from a plain program's by a relative error of at most 0.009.
Values may be sent and summed in bfloat16 or wider, within the bound.
No kernel may reach another device: no remote copies, remote signals or barrier semaphores. Data moves between devices by JAX's collectives and lax.ppermute only.
A program may use at most 128 MiB of HBM per device.

v0:
```python
import math

import jax
import jax.numpy as jnp
from jax import lax
from jax.sharding import PartitionSpec as P


def sequence_grads(query, scaled, keys, values, delta, length):
    full_len, per_dev, head_dim = query.shape
    slots = keys.shape[1]
    repeat = per_dev // slots
    block = min(512, full_len)
    scale = 1.0 / math.sqrt(head_dim)
    q_four = query.reshape(full_len, slots, repeat, head_dim)
    g_four = scaled.reshape(full_len, slots, repeat, head_dim)
    d_three = delta.reshape(full_len, slots, repeat)

    def make_step(start):
        prefix = start + block

        def one_block(carry):
            query_all, key_acc, value_acc = carry
            q_block = q_four[start:prefix]
            g_block = g_four[start:prefix]
            d_block = jnp.transpose(d_three[start:prefix], (1, 2, 0))[..., None]
            key_pre = keys[:prefix]
            value_pre = values[:prefix]
            scores = (
                jnp.einsum("isrd,jsd->srij", q_block, key_pre, preferred_element_type=jnp.float32)
                * scale
            )
            query_pos = start + jnp.arange(block)
            causal = jnp.arange(prefix)[None, :] <= query_pos[:, None]
            scores = jnp.where(causal, scores, -jnp.inf)
            top = jnp.max(scores, axis=-1, keepdims=True)
            lse = top + jnp.log(jnp.sum(jnp.exp(scores - top), axis=-1, keepdims=True))
            prob = jnp.exp(scores - lse)
            prob_low = prob.astype(jnp.bfloat16)
            value_part = jnp.einsum(
                "srij,isrd->jsd", prob_low, g_block, preferred_element_type=jnp.float32
            )
            dprob = jnp.einsum(
                "isrd,jsd->srij", g_block, value_pre, preferred_element_type=jnp.float32
            )
            dscore = prob * (dprob - d_block)
            dscore_low = dscore.astype(jnp.bfloat16)
            query_part = (
                jnp.einsum(
                    "srij,jsd->isrd", dscore_low, key_pre, preferred_element_type=jnp.float32
                )
                * scale
            )
            query_part = query_part.reshape(block, per_dev, head_dim).astype(jnp.bfloat16)
            query_all = lax.dynamic_update_slice_in_dim(query_all, query_part, start, 0)
            key_part = jnp.einsum(
                "srij,isrd->jsd", dscore_low, q_block, preferred_element_type=jnp.float32
            )
            key_acc = key_acc.at[:prefix].add(key_part)
            value_acc = value_acc.at[:prefix].add(value_part)
            return (query_all, key_acc, value_acc)

        return one_block

    carry = (
        jnp.zeros((full_len, per_dev, head_dim), jnp.bfloat16),
        jnp.zeros((full_len, slots, head_dim), jnp.float32),
        jnp.zeros((full_len, slots, head_dim), jnp.float32),
    )
    for index in range(full_len // block):
        start = index * block
        step_fn = make_step(start)
        carry = step_fn(carry)
    query_all, key_acc, value_acc = carry
    return (query_all, key_acc * scale, value_acc)


def body(query, keys, values, output, out_grad, lengths, margins):
    place = lax.axis_index("seq")
    seqs_dev, toks_dev, heads, head_dim = query.shape
    kv_heads = keys.shape[2]
    group = heads // kv_heads
    total = lax.psum(jnp.sum(lengths), "dp")
    mean_len = total.astype(jnp.float32) / (seqs_dev * lax.axis_size("dp"))
    weight = jax.nn.sigmoid(-margins)
    signs = jnp.tile(jnp.array([-1.0, 1.0], jnp.float32), margins.shape[0])
    coef = jnp.repeat(weight, 2) * signs * 4.0 * mean_len / lengths.astype(jnp.float32)
    positions = place * toks_dev + jnp.arange(toks_dev)
    live = (positions[None, :] < lengths[:, None]).astype(jnp.float32)
    factor = coef[:, None] * live
    scaled = (out_grad.astype(jnp.float32) * factor[:, :, None, None]).astype(jnp.bfloat16)
    key_slots = jnp.repeat(keys, group, axis=2)
    value_slots = jnp.repeat(values, group, axis=2)
    q_heads, g_heads, o_heads, k_heads, v_heads = (
        lax.all_to_all(query, "seq", split_axis=2, concat_axis=1, tiled=True),
        lax.all_to_all(scaled, "seq", split_axis=2, concat_axis=1, tiled=True),
        lax.all_to_all(output, "seq", split_axis=2, concat_axis=1, tiled=True),
        lax.all_to_all(key_slots, "seq", split_axis=2, concat_axis=1, tiled=True),
        lax.all_to_all(value_slots, "seq", split_axis=2, concat_axis=1, tiled=True),
    )
    delta = jnp.sum(g_heads.astype(jnp.float32) * o_heads.astype(jnp.float32), axis=3)
    query_heads, key_heads, value_heads = lax.map(
        lambda items: sequence_grads(*items), (q_heads, g_heads, k_heads, v_heads, delta, lengths)
    )
    query_grad = lax.all_to_all(query_heads, "seq", split_axis=1, concat_axis=2, tiled=True)
    key_rows, value_rows = (
        lax.all_to_all(key_heads, "seq", split_axis=1, concat_axis=2, tiled=True),
        lax.all_to_all(value_heads, "seq", split_axis=1, concat_axis=2, tiled=True),
    )
    key_grad = jnp.sum(
        key_rows.reshape(seqs_dev, toks_dev, kv_heads, group, head_dim), axis=3
    ).astype(jnp.bfloat16)
    value_grad = jnp.sum(
        value_rows.reshape(seqs_dev, toks_dev, kv_heads, group, head_dim), axis=3
    ).astype(jnp.bfloat16)
    return (query_grad, key_grad, value_grad)


def solution(mesh):
    return jax.shard_map(
        body,
        mesh=mesh,
        in_specs=(
            P("dp", "seq", None, None),
            P("dp", "seq", None, None),
            P("dp", "seq", None, None),
            P("dp", "seq", None, None),
            P("dp", "seq", None, None),
            P("dp"),
            P("dp"),
        ),
        out_specs=(
            P("dp", "seq", None, None),
            P("dp", "seq", None, None),
            P("dp", "seq", None, None),
        ),
        check_vma=False,
    )
```

profile of v0, /device:TPU:24, one launch (start us, length us, event | category | flops | bytes accessed | tf_op | source)
XLA Modules:
  0.0 498.7 jit_solution(3425780282088553488)
XLA Ops:
  3.4 8.0 %all-to-all-start.2 = ((bf16[2,128,32,128]{3,1,0,2:T(8,128)(2,1)}), bf16[2,128,32,128]{3,1,0,2:T(8,128)(2,1)S(1)}, u32[]{:S(2)}, u32[]{:S(2)}) async-start(bf16[2,128,32,128]{3,1,0,2:T(8,128)(2,1)} %bitcast.749), calls=%async_computation.2 | async-start | bytes 4194304 | tf_op jit(solution)/shard_map/all_to_all | solution.py:99
  11.5 31.6 %all-to-all-done.2 = bf16[2,128,32,128]{3,1,0,2:T(8,128)(2,1)S(1)} async-done(((bf16[2,128,32,128]{3,1,0,2:T(8,128)(2,1)}), bf16[2,128,32,128]{3,1,0,2:T(8,128)(2,1)S(1)}, u32[]{:S(2)}, u32[]{:S(2)}) %all-to-all-start.2) | async-done | bytes 2097184 | tf_op jit(solution)/shard_map/all_to_all | solution.py:99
  45.1 4.6 all-to-all-start
  50.4 7.7 %psum.7 = s32[]{:T(128)} all-reduce(s32[]{:T(128)} %reduce_sum.96), channel_id=1, replica_groups=mesh['dp'=8,'seq'=16] {'dp'}, use_global_device_ids=true, to_apply=%region_1.0 | all-reduce | flops 1 | bytes 8 | tf_op jit(solution)/shard_map/psum | solution.py:83
  59.6 3.8 multiply_convert_fusion
  63.4 15.7 %all-to-all-done = bf16[2,128,32,128]{3,1,0,2:T(8,128)(2,1)} async-done(((bf16[2,128,32,128]{3,1,0,2:T(8,128)(2,1)}), bf16[2,128,32,128]{3,1,0,2:T(8,128)(2,1)}, u32[]{:S(2)}, u32[]{:S(2)}) %all-to-all-start) | async-done | bytes 2097184 | tf_op jit(solution)/shard_map/all_to_all | solution.py:98
  79.1 3.7 all-to-all-start.3
  82.8 3.7 copy.212
  86.5 26.5 %all-to-all-done.3 = bf16[2,128,32,128]{3,1,0,2:T(8,128)(2,1)S(1)} async-done(((bf16[2,128,32,128]{3,1,0,2:T(8,128)(2,1)}), bf16[2,128,32,128]{3,1,0,2:T(8,128)(2,1)S(1)}, u32[]{:S(2)}, u32[]{:S(2)}) %all-to-all-start.3) | async-done | bytes 2097184 | tf_op jit(solution)/shard_map/all_to_all | solution.py:96
  113.0 4.4 all-to-all-start.1
  117.5 3.7 copy.219
  121.2 25.9 %all-to-all-done.1 = bf16[2,128,32,128]{3,1,0,2:T(8,128)(2,1)} async-done(((bf16[2,128,32,128]{3,1,0,2:T(8,128)(2,1)}), bf16[2,128,32,128]{3,1,0,2:T(8,128)(2,1)}, u32[]{:S(2)}, u32[]{:S(2)}) %all-to-all-start.1) | async-done | bytes 2097184 | tf_op jit(solution)/shard_map/all_to_all | solution.py:95
  147.1 4.4 all-to-all-start.4
  151.6 3.2 copy.216
  154.8 3.1 copy.211
  159.4 3.2 copy.213
  162.6 18.2 %all-to-all-done.4 = bf16[2,128,32,128]{3,1,0,2:T(8,128)(2,1)} async-done(((bf16[2,128,32,128]{3,1,0,2:T(8,128)(2,1)}), bf16[2,128,32,128]{3,1,0,2:T(8,128)(2,1)}, u32[]{:S(2)}, u32[]{:S(2)}) %all-to-all-start.4) | async-done | bytes 2097184 | tf_op jit(solution)/shard_map/all_to_all | solution.py:97
  180.8 2.8 fusion.154
  183.6 154.6 %while.27 = (s32[]{:T(128)}, bf16[2,2048,2,128]{3,2,0,1:T(2,128)(2,1)}, f32[2,2048,2,128]{3,2,0,1:T(2,128)}, f32[2,2048,2,128]{3,2,0,1:T(2,128)}, bf16[2,2048,2,...) while((s32[]{:T(128)}, ...), condition=%wide.region_12.13_spmd, body=%wide.region_3.12_spmd.sunk | while | flops 6793983488 | bytes 198647088 | solution.py:102
  215.2 2.5 fusion.221
  217.7 2.6 fusion.213
  223.8 2.5 fusion.215
  227.2 2.4 fusion.222
  229.6 2.5 fusion.216
  236.1 3.0 fusion.218
  241.1 4.7 fusion.223
  245.9 4.1 fusion.219
  250.0 2.5 fusion.226
  258.8 2.9 copy.379
  279.2 2.5 fusion.221
  281.7 2.6 fusion.213
  287.8 2.5 fusion.215
  291.2 2.4 fusion.222
  293.6 2.5 fusion.216
  300.1 3.0 fusion.218
  305.1 4.7 fusion.223
  309.9 4.1 fusion.219
  314.0 2.5 fusion.226
  322.9 2.9 copy.379
  338.2 31.9 %all_to_all.117 = bf16[2,2048,2,128]{3,2,0,1:T(2,128)(2,1)S(1)} all-to-all(bf16[2,2048,2,128]{3,2,0,1:T(2,128)(2,1)} %get-tuple-element.267), channel_id=1, replica_groups=mesh['dp'=8,'seq'=16] {'seq'}, dimensions={1} | all-to-all | bytes 4194304 | tf_op jit(solution)/shard_map/all_to_all | solution.py:105
  370.1 54.2 %all_to_all.118 = f32[2,2048,2,128]{3,2,0,1:T(2,128)} all-to-all(f32[2,2048,2,128]{3,2,0,1:T(2,128)S(1)} %copy-done.3), channel_id=1, replica_groups=mesh['dp'=8,'seq'=16] {'seq'}, dimensions={1} | all-to-all | bytes 8388608 | tf_op jit(solution)/shard_map/all_to_all | solution.py:108
  424.3 4.5 all-to-all-start.6
  428.9 2.8 copy.222
  431.6 7.6 %reduce_sum.104 = f32[2,2048,128]{2,0,1:T(2,128)S(1)} reduce(f32[2,2048,2,128]{3,2,0,1:T(2,128)} %all_to_all.118, f32[]{:T(128)} %constant.328.clone.1), dimensions={2}, to_apply=%region_15.16 | reduce | flops 524288 | bytes 6291460 | tf_op jit(solution)/shard_map/reduce_sum | solution.py:113
  441.2 3.0 reduce_sum.108
  445.1 40.1 %all-to-all-done.6 = f32[2,2048,2,128]{3,2,0,1:T(2,128)} async-done(((f32[2,2048,2,128]{3,2,0,1:T(2,128)}), f32[2,2048,2,128]{3,2,0,1:T(2,128)}, u32[]{:S(2)}, u32[]{:S(2)}) %all-to-all-start.6) | async-done | bytes 4194336 | tf_op jit(solution)/shard_map/all_to_all | solution.py:107
  485.2 7.6 %reduce_sum.99 = f32[2,2048,128]{2,0,1:T(2,128)S(1)} reduce(f32[2,2048,2,128]{3,2,0,1:T(2,128)} %all-to-all-done.6, f32[]{:T(128)} %constant.328.clone.1), dimensions={2}, to_apply=%region_13.14 | reduce | flops 524288 | bytes 6291460 | tf_op jit(solution)/shard_map/reduce_sum | solution.py:110
  494.7 3.0 reduce_sum.103
  (104 shorter events, 80.6 us)
Async XLA Ops:
  3.4 8.0 %copy-start.4 = (bf16[2,128,4,128]{3,2,1,0:T(4,128)(2,1)S(1)}, bf16[2,128,4,128]{3,2,1,0:T(4,128)(2,1)}, u32[]{:S(2)}) copy-start(bf16[2,128,4,128]{3,2,1,0:T(4,128)(2,1)} %param.31) | copy-start | bytes 786436
  3.4 39.7 %all-to-all-start.2 = ((bf16[2,128,32,128]{3,1,0,2:T(8,128)(2,1)}), bf16[2,128,32,128]{3,1,0,2:T(8,128)(2,1)S(1)}, u32[]{:S(2)}, u32[]{:S(2)}) async-start(bf16[2,128,32,128]{3,1,0,2:T(8,128)(2,1)} %bitcast.749), calls=%async_computation.2 | async-start | bytes 4194304 | tf_op jit(solution)/shard_map/all_to_all | solution.py:99
  43.1 2.0 copy-start.2
  45.1 4.6 copy-start.5
  45.1 14.4 %copy-start.6 = (f32[2]{0:T(128)S(1)}, f32[2]{0:T(128)}, u32[]{:S(2)}) copy-start(f32[2]{0:T(128)} %constant.333.clone) | copy-start | bytes 28
  45.1 34.0 %all-to-all-start = ((bf16[2,128,32,128]{3,1,0,2:T(8,128)(2,1)}), bf16[2,128,32,128]{3,1,0,2:T(8,128)(2,1)}, u32[]{:S(2)}, u32[]{:S(2)}) async-start(bf16[2,128,32,128]{3,1,0,2:T(8,128)(2,1)} %bitcast.747), calls=%async_computation | async-start | bytes 4194304 | tf_op jit(solution)/shard_map/all_to_all | solution.py:98
  79.1 33.9 %all-to-all-start.3 = ((bf16[2,128,32,128]{3,1,0,2:T(8,128)(2,1)}), bf16[2,128,32,128]{3,1,0,2:T(8,128)(2,1)S(1)}, u32[]{:S(2)}, u32[]{:S(2)}) async-start(bf16[2,128,32,128]{3,1,0,2:T(8,128)(2,1)} %multiply_convert_fusion), calls=%async_computation.3 | async-start | bytes 4194304 | tf_op jit(solution)/shard_map/all_to_all | solution.py:96
  113.0 34.1 %all-to-all-start.1 = ((bf16[2,128,32,128]{3,1,0,2:T(8,128)(2,1)}), bf16[2,128,32,128]{3,1,0,2:T(8,128)(2,1)}, u32[]{:S(2)}, u32[]{:S(2)}) async-start(bf16[2,128,32,128]{3,1,0,2:T(8,128)(2,1)} %copy.212), calls=%async_computation.1 | async-start | bytes 4194304 | tf_op jit(solution)/shard_map/all_to_all | solution.py:95
  147.1 33.7 %all-to-all-start.4 = ((bf16[2,128,32,128]{3,1,0,2:T(8,128)(2,1)}), bf16[2,128,32,128]{3,1,0,2:T(8,128)(2,1)}, u32[]{:S(2)}, u32[]{:S(2)}) async-start(bf16[2,128,32,128]{3,1,0,2:T(8,128)(2,1)} %copy.219), calls=%async_computation.4 | async-start | bytes 4194304 | tf_op jit(solution)/shard_map/all_to_all | solution.py:97
  258.8 2.9 copy-start.1
  261.8 1.9 copy-start
  322.9 2.9 copy-start.1
  325.8 1.9 copy-start
  338.2 31.9 %copy-start.3 = (f32[2,2048,2,128]{3,2,0,1:T(2,128)S(1)}, f32[2,2048,2,128]{3,2,0,1:T(2,128)}, u32[]{:S(2)}) copy-start(f32[2,2048,2,128]{3,2,0,1:T(2,128)} %get-tuple-element.269) | copy-start | bytes 12582916
  424.3 60.9 %all-to-all-start.6 = ((f32[2,2048,2,128]{3,2,0,1:T(2,128)}), f32[2,2048,2,128]{3,2,0,1:T(2,128)}, u32[]{:S(2)}, u32[]{:S(2)}) async-start(f32[2,2048,2,128]{3,2,0,1:T(2,128)} %get-tuple-element.268), calls=%async_computation.6 | async-start | bytes 8388608 | tf_op jit(solution)/shard_map/all_to_all | solution.py:107
where the time goes:
time: 506 us; the launch traced here: 499 us
  waiting for transfers between devices  158 us (31%)
  blocking collectives  93.9 us (19%)
  matrix products  91.6 us (18%)
  local copies, waits for them, and re-layouts  55.6 us (11%)
  other arithmetic  40.6 us (8%)
  starting transfers between devices  29.7 us (6%)
  loops' own time  26.9 us (5%)
    all_to_all x1, blocking collectives, body(): lax.all_to_all(value_heads, 'seq', split_axis=1, concat_axis=2, tiled=True)  54.2 us
    all_to_all x1, waiting for transfers between devices, body(): lax.all_to_all(key_heads, 'seq', split_axis=1, concat_axis=2, tiled=True)  40.1 us
    all_to_all x1, blocking collectives, body(): lax.all_to_all(query_heads, 'seq', split_axis=1, concat_axis=2, tiled=True)  31.9 us
    all_to_all x1, waiting for transfers between devices, body(): lax.all_to_all(value_slots, 'seq', split_axis=2, concat_axis=1, tiled=True)  31.6 us
    another operation x1, loops' own time, body(): lax.map(lambda items: sequence_grads(*items), (q_heads, g_heads, k_heads,...  26.9 us
    all_to_all x1, waiting for transfers between devices, body(): lax.all_to_all(scaled, 'seq', split_axis=2, concat_axis=1, tiled=True)  26.5 us
    all_to_all x1, waiting for transfers between devices, body(): lax.all_to_all(query, 'seq', split_axis=2, concat_axis=1, tiled=True)  25.9 us
    dot_general x8, matrix products, one_block(): jnp.einsum('srij,isrd->jsd', prob_low, g_block, preferred_element_type=jn...  22.3 us
  transfers between devices with their start and end apart: 6, of which 6 were waited for; matrix products, arithmetic and copies ran while one was open for 8% of the time, Pallas kernels for 0%

commit v1 on v0

v1 whole, which is shorter than its diff:
```python
import functools
import math

import jax
import jax.numpy as jnp
from jax import lax
from jax.experimental import pallas as pl
from jax.experimental.pallas import tpu as pltpu
from jax.sharding import PartitionSpec as P

f32, bf16 = jnp.float32, jnp.bfloat16
NT = (((1,), (1,)), ((), ()))
NN = (((1,), (0,)), ((), ()))

SIDE = 4
TOK = 128
GROUP = 8
DIM = 128
ROWS = TOK * GROUP
EXTRA = 16
FULL = TOK * SIDE * SIDE
CHUNK = 512
SCALE = 1.0 / math.sqrt(DIM)
EXP2 = SCALE * math.log2(math.e)
VMEM_BYTES = 56 * 1024 * 1024


def shift_pairs(kind, by):
    pairs = []
    for z in range(SIDE):
        for x in range(SIDE):
            to = ((z + by) % SIDE) * SIDE + x if kind == 0 else z * SIDE + (x + by) % SIDE
            pairs.append((z * SIDE + x, to))
    return pairs


def shift(value, kind, by):
    return lax.ppermute(value, "seq", shift_pairs(kind, by % SIDE))


def any_spec():
    return pl.BlockSpec(memory_space=pl.ANY)


def vmem_spec():
    return pl.BlockSpec(memory_space=pltpu.VMEM)


def smem_spec():
    return pl.BlockSpec(memory_space=pltpu.SMEM)


def params():
    return pltpu.CompilerParams(vmem_limit_bytes=VMEM_BYTES)


def pack_kv_kernel(place, kv_ref, *outs):
    for s in range(2):
        for d in range(SIDE):
            head = lax.rem(place[s] + d, SIDE)
            outs[s * SIDE + d][...] = kv_ref[s, head]


def pack_kernel(place, q_ref, g_ref, o_ref, *outs):
    for s in range(2):
        for d in range(SIDE):
            head = lax.rem(place[s] + d, SIDE)
            out = outs[s * SIDE + d]
            g = g_ref[s, :, head].reshape(ROWS, DIM)
            o = o_ref[s, :, head].reshape(ROWS, DIM)
            out[0:ROWS, :] = q_ref[s, :, head].reshape(ROWS, DIM)
            out[ROWS:2 * ROWS, :] = g
            prod = g.astype(f32) * o.astype(f32)
            high = prod.astype(bf16)
            low = (prod - high.astype(f32)).astype(bf16)
            ones = jnp.ones((8, DIM), bf16)
            delta = lax.dot_general(ones, high, NT, preferred_element_type=f32)
            delta += lax.dot_general(ones, low, NT, preferred_element_type=f32)
            rows = jnp.concatenate(
                [delta[0:1, a * DIM:(a + 1) * DIM] for a in range(ROWS // DIM)], axis=0
            )
            d_high = rows.astype(bf16)
            d_low = (rows - d_high.astype(f32)).astype(bf16)
            out[2 * ROWS:, :] = jnp.concatenate([d_high, d_low], axis=0)


def attention_kernel(meta, coef, *refs):
    packs, kvs = refs[0:SIDE], refs[SIDE:2 * SIDE]
    dqs, dkvs = refs[2 * SIDE:3 * SIDE], refs[3 * SIDE:4 * SIDE]
    pk, k_s, v_s, kt_s, p_s, m_s, dka, dva, gm_s, dqt_s, dq_s, sem_p, sem_kv, sem_o = refs[4 * SIDE:]
    length = meta[SIDE * SIDE]
    copies = []
    for d in range(SIDE):
        copies.append(pltpu.make_async_copy(packs[d], pk.at[d], sem_p.at[d]))
    for e in range(SIDE):
        for d in range(SIDE):
            at = pl.ds(pl.multiple_of(meta[e * SIDE + d] * TOK, TOK), TOK)
            slot = e * SIDE + d
            copies.append(
                pltpu.make_async_copy(kvs[e].at[d, pl.ds(0, TOK)], k_s.at[at], sem_kv.at[0, slot])
            )
            copies.append(
                pltpu.make_async_copy(kvs[e].at[d, pl.ds(TOK, TOK)], v_s.at[at], sem_kv.at[1, slot])
            )
    for copy in copies:
        copy.start()
    dka[...] = jnp.zeros_like(dka)
    dva[...] = jnp.zeros_like(dva)
    for copy in copies:
        copy.wait()
    kt_s[...] = k_s[...].T
    factor = coef[0]

    def one_block(d, _):
        block = meta[d]
        first = block * TOK

        @pl.when(first >= length)
        def _():
            dq_s[d] = jnp.zeros((ROWS, DIM), bf16)

        @pl.when(first < length)
        def _():
            token = lax.broadcasted_iota(jnp.int32, (ROWS, DIM), 0) // GROUP + first
            gm_s[...] = jnp.where(token < length, pk[d, ROWS:2 * ROWS, :], jnp.zeros((), bf16))
            lane_token = lax.broadcasted_iota(jnp.int32, (1, ROWS), 1) // GROUP + first
            tail = pk[d, 2 * ROWS:, :].astype(f32)
            tail = tail[0:8] + tail[8:16]
            delta = jnp.concatenate([tail[a:a + 1, :] for a in range(8)], axis=1)
            delta = jnp.where(lane_token < length, delta, 0.0)
            steps = (first + TOK + CHUNK - 1) // CHUNK

            def scores_step(c, carry, masked):
                top, total = carry
                k0 = pl.multiple_of(c * CHUNK, CHUNK)
                s = lax.dot_general(
                    k_s[pl.ds(k0, CHUNK), :], pk[d, 0:ROWS, :], NT, preferred_element_type=f32
                )
                if masked:
                    key = lax.broadcasted_iota(jnp.int32, (CHUNK, ROWS), 0) + k0
                    s = jnp.where(key <= lane_token, s, -jnp.inf)
                new = jnp.maximum(top, jnp.max(s, axis=0, keepdims=True))
                p = jnp.exp2((s - new) * EXP2)
                p_s[pl.ds(k0, CHUNK), :] = p
                m_s[c] = jnp.broadcast_to(new, (8, ROWS))
                total = total * jnp.exp2((top - new) * EXP2) + jnp.sum(p, axis=0, keepdims=True)
                return new, total

            carry = (jnp.full((1, ROWS), -1e30, f32), jnp.zeros((1, ROWS), f32))
            carry = lax.fori_loop(0, steps - 1, lambda c, x: scores_step(c, x, False), carry)
            top, total = scores_step(steps - 1, carry, True)
            inverse = 1.0 / total
            dqt_s[...] = jnp.zeros_like(dqt_s)

            def grads_step(c, _):
                k0 = pl.multiple_of(c * CHUNK, CHUNK)
                at = pl.ds(k0, CHUNK)
                g = gm_s[...]
                weight = jnp.exp2((m_s[c][0:1] - top) * EXP2) * inverse
                dp = lax.dot_general(v_s[at, :], g, NT, preferred_element_type=f32)
                prob = p_s[at, :] * weight
                ds = (prob * (dp - delta)).astype(bf16)
                dva[at, :] += lax.dot_general(prob.astype(bf16), g, NN, preferred_element_type=f32)
                dka[at, :] += lax.dot_general(ds, pk[d, 0:ROWS, :], NN, preferred_element_type=f32)
                dqt_s[...] += lax.dot_general(kt_s[:, at], ds, NN, preferred_element_type=f32)
                return 0

            lax.fori_loop(0, steps, grads_step, 0)
            dq_s[d] = (dqt_s[...].T * (factor * SCALE)).astype(bf16)

        return 0

    lax.fori_loop(0, SIDE, one_block, 0)
    outs = [pltpu.make_async_copy(dq_s.at[d], dqs[d], sem_o.at[d]) for d in range(SIDE)]
    for copy in outs:
        copy.start()
    for e in range(SIDE):
        for d in range(SIDE):
            at = pl.ds(pl.multiple_of(meta[e * SIDE + d] * TOK, TOK), TOK)
            dkvs[e][d, 0] = (dka[at, :] * (factor * SCALE)).astype(bf16)
            dkvs[e][d, 1] = (dva[at, :] * factor).astype(bf16)
    for copy in outs:
        copy.wait()


def attention(meta, coef, packs, kvs):
    flops = 2 * ROWS * FULL * DIM * 5 * SIDE // 2
    return pl.pallas_call(
        attention_kernel,
        in_specs=[smem_spec(), smem_spec()] + [any_spec()] * (2 * SIDE),
        out_specs=[any_spec()] * SIDE + [vmem_spec()] * SIDE,
        out_shape=[jax.ShapeDtypeStruct((ROWS, DIM), bf16)] * SIDE
        + [jax.ShapeDtypeStruct((SIDE, 2, TOK, DIM), bf16)] * SIDE,
        scratch_shapes=[
            pltpu.VMEM((SIDE, 2 * ROWS + EXTRA, DIM), bf16),
            pltpu.VMEM((FULL, DIM), bf16),
            pltpu.VMEM((FULL, DIM), bf16),
            pltpu.VMEM((DIM, FULL), bf16),
            pltpu.VMEM((FULL, ROWS), f32),
            pltpu.VMEM((FULL // CHUNK, 8, ROWS), f32),
            pltpu.VMEM((FULL, DIM), f32),
            pltpu.VMEM((FULL, DIM), f32),
            pltpu.VMEM((ROWS, DIM), bf16),
            pltpu.VMEM((DIM, ROWS), f32),
            pltpu.VMEM((SIDE, ROWS, DIM), bf16),
            pltpu.SemaphoreType.DMA((SIDE,)),
            pltpu.SemaphoreType.DMA((2, SIDE * SIDE)),
            pltpu.SemaphoreType.DMA((SIDE,)),
        ],
        compiler_params=params(),
        cost_estimate=pl.CostEstimate(flops=flops, bytes_accessed=8 << 20, transcendentals=ROWS * FULL * 2),
    )(meta, coef, *packs, *kvs)


def sum_kernel(a, b, c, d, *outs):
    for i in range(SIDE):
        total = a[i].astype(f32) + b[i].astype(f32) + (c[i].astype(f32) + d[i].astype(f32))
        outs[i][...] = total.astype(bf16)


def place_kernel(place, *refs):
    rows, out = refs[:-1], refs[-1]
    for s in range(2):
        for d in range(SIDE):
            head = lax.rem(place[s] + d, SIDE)
            out[s, :, head] = rows[s * SIDE + d][...].reshape(TOK, GROUP, DIM)


def place_kv_kernel(place, *refs):
    parts, out = refs[:-1], refs[-1]
    for s in range(2):
        for d in range(SIDE):
            out[s, lax.rem(place[s] + d, SIDE)] = parts[s * SIDE + d][...]


def body(query, keys, values, output, out_grad, lengths, margins):
    index = lax.axis_index("seq")
    z, x = index // SIDE, index % SIDE
    place = jnp.stack([z, x]).astype(jnp.int32)
    cross = [x, z]
    total = lax.psum(jnp.sum(lengths), "dp")
    mean_len = total.astype(f32) / (2 * lax.axis_size("dp"))
    weight = jax.nn.sigmoid(-margins)
    signs = jnp.array([-1.0, 1.0], f32)
    coef = jnp.repeat(weight, 2) * signs * 4.0 * mean_len / lengths.astype(f32)

    kv = jnp.stack([keys, values], axis=0)
    kv = jnp.transpose(kv, (1, 3, 0, 2, 4)).reshape(2, SIDE, 2 * TOK, DIM)
    kv_parts = pl.pallas_call(
        pack_kv_kernel,
        in_specs=[smem_spec(), vmem_spec()],
        out_specs=[vmem_spec()] * (2 * SIDE),
        out_shape=[jax.ShapeDtypeStruct((2 * TOK, DIM), bf16)] * (2 * SIDE),
        compiler_params=params(),
    )(place, kv)
    five = (2, TOK, SIDE, GROUP, DIM)
    packs = pl.pallas_call(
        pack_kernel,
        in_specs=[smem_spec()] + [vmem_spec()] * 3,
        out_specs=[vmem_spec()] * (2 * SIDE),
        out_shape=[jax.ShapeDtypeStruct((2 * ROWS + EXTRA, DIM), bf16)] * (2 * SIDE),
        compiler_params=params(),
    )(place, query.reshape(five), out_grad.reshape(five), output.reshape(five))

    gathered, moved = [], []
    for s in range(2):
        kv_in = [kv_parts[s * SIDE]] + [shift(kv_parts[s * SIDE + d], s, d) for d in range(1, SIDE)]
        mine = jnp.stack(kv_in, axis=0)
        gathered.append([mine] + [shift(mine, 1 - s, e) for e in range(1, SIDE)])
        moved.append([packs[s * SIDE]] + [shift(packs[s * SIDE + d], s, d) for d in range(1, SIDE)])

    dq_rows, kv_grads = [], []
    for s in range(2):
        order = []
        for e in range(SIDE):
            for d in range(SIDE):
                along, across = (place[s] - d) % SIDE, (cross[s] - e) % SIDE
                order.append(along * SIDE + across if s == 0 else across * SIDE + along)
        meta = jnp.stack(order + [lengths[s]]).astype(jnp.int32)
        res = attention(meta, coef[s].reshape(1), moved[s], gathered[s])
        dqs, dkvs = res[:SIDE], res[SIDE:]
        dq_rows += [dqs[0]] + [shift(dqs[d], s, -d) for d in range(1, SIDE)]
        sums = [dkvs[0]] + [shift(dkvs[e], 1 - s, -e) for e in range(1, SIDE)]
        parts = pl.pallas_call(
            sum_kernel,
            in_specs=[vmem_spec()] * SIDE,
            out_specs=[vmem_spec()] * SIDE,
            out_shape=[jax.ShapeDtypeStruct((2, TOK, DIM), bf16)] * SIDE,
            compiler_params=params(),
        )(*sums)
        kv_grads += [parts[0]] + [shift(parts[d], s, -d) for d in range(1, SIDE)]

    query_grad = pl.pallas_call(
        place_kernel,
        in_specs=[smem_spec()] + [vmem_spec()] * (2 * SIDE),
        out_specs=vmem_spec(),
        out_shape=jax.ShapeDtypeStruct(five, bf16),
        compiler_params=params(),
    )(place, *dq_rows).reshape(query.shape)
    kv_grad = pl.pallas_call(
        place_kv_kernel,
        in_specs=[smem_spec()] + [vmem_spec()] * (2 * SIDE),
        out_specs=vmem_spec(),
        out_shape=jax.ShapeDtypeStruct((2, SIDE, 2, TOK, DIM), bf16),
        compiler_params=params(),
    )(place, *kv_grads)
    kv_grad = jnp.transpose(kv_grad, (2, 0, 3, 1, 4))
    return (query_grad, kv_grad[0], kv_grad[1])


def solution(mesh):
    spec = P("dp", "seq", None, None)
    return jax.shard_map(
        body,
        mesh=mesh,
        in_specs=(spec,) * 5 + (P("dp"), P("dp")),
        out_specs=(spec,) * 3,
        check_vma=False,
    )
```

time: 506 us -> 170 us (0.34); the launches traced: 499 us -> 168 us
  waiting for transfers between devices: 158 us -> 24.9 us
  matrix products: 91.6 us -> 0 us
  blocking collectives: 93.9 us -> 7.73 us
  Pallas kernels: 0 us -> 51.6 us
  local copies, waits for them, and re-layouts: 55.6 us -> 9.85 us
  starting transfers between devices: 29.7 us -> 67.8 us
  other arithmetic: 40.6 us -> 3.54 us
  loops' own time: 26.9 us -> 0 us
    all_to_all x6 -> x0, waiting for transfers between devices: 158 us -> none  [the longest x1 40.1 us: body(): lax.all_to_all(key_heads, 'seq', split_axis=1, concat_axis=2, tiled=True)]
    dot_general x40 -> x0, matrix products: 91.6 us -> none  [the longest x8 22.3 us: one_block(): jnp.einsum('srij,isrd->jsd', prob_low, g_block, preferred_element_type=jn...]
    all_to_all x2 -> x0, blocking collectives: 86.1 us -> none  [the longest x1 54.2 us: body(): lax.all_to_all(value_heads, 'seq', split_axis=1, concat_axis=2, tiled=True)]
    ppermute x0 -> x36, starting transfers between devices: none -> 67.8 us  [shift(): return lax.ppermute(value, 'seq', shift_pairs(kind, by % SIDE))]
    pallas_call x0 -> x8, Pallas kernels: none -> 51.6 us  [the longest x2 34.3 us: attention(): pl.pallas_call(attention_kernel, in_specs=[smem_spec(), smem_spec()] + [a...]
    reduce_sum x13 -> x0, other arithmetic: 32.2 us -> none  [the longest x2 10.6 us: body(): jnp.sum(key_rows.reshape(seqs_dev, toks_dev, kv_heads, group, head_dim),...]
    all_to_all x6 -> x0, starting transfers between devices: 29.7 us -> none  [the longest x1 8.01 us: body(): lax.all_to_all(value_slots, 'seq', split_axis=2, concat_axis=1, tiled=True)]
    another operation x1 -> x0, loops' own time: 26.9 us -> none  [body(): lax.map(lambda items: sequence_grads(*items), (q_heads, g_heads, k_heads,...]
  transfers between devices with their start and end apart: 6 -> 36, of which waited for: 6 -> 10; matrix products, arithmetic and copies ran while one was open for 8% -> 3% of each run, Pallas kernels for 0% -> 28%
where the time goes in v1:
time: 170 us; the launch traced here: 168 us
  starting transfers between devices  67.8 us (40%)
  Pallas kernels  51.6 us (30%)
  waiting for transfers between devices  24.9 us (15%)
  local copies, waits for them, and re-layouts  9.85 us (6%)
  blocking collectives  7.73 us (5%)
  other arithmetic  3.54 us (2%)
  between operations  2.4 us (1%)
    ppermute x36, starting transfers between devices, shift(): return lax.ppermute(value, 'seq', shift_pairs(kind, by % SIDE))  67.8 us
    pallas_call x2, Pallas kernels, attention(): pl.pallas_call(attention_kernel, in_specs=[smem_spec(), smem_spec()] + [a...  34.3 us
    ppermute x36, waiting for transfers between devices, shift(): return lax.ppermute(value, 'seq', shift_pairs(kind, by % SIDE))  24.9 us
    psum x1, blocking collectives, body(): total = lax.psum(jnp.sum(lengths), 'dp')  7.73 us
    pallas_call x1, Pallas kernels, body(): pl.pallas_call(pack_kernel, in_specs=[smem_spec()] + [vmem_spec()] * 3, o...  6.22 us
    unnamed x80, local copies, waits for them, and re-layouts  4.06 us
    pallas_call x2, Pallas kernels, body(): pl.pallas_call(sum_kernel, in_specs=[vmem_spec()] * SIDE, out_specs=[vmem...  3.89 us
  transfers between devices with their start and end apart: 36, of which 10 were waited for; matrix products, arithmetic and copies ran while one was open for 3% of the time, Pallas kernels for 28%

profile of v1, /device:TPU:24, one launch (start us, length us, event | category | flops | bytes accessed | tf_op | source)
XLA Modules:
  0.0 167.8 jit_solution(119310957327078192)
XLA Ops:
  0.6 1.4 maximum_bitcast_fusion
  2.1 0.9 copy.11
  3.5 1.9 %shard_map.104 = (bf16[256,128]{1,0:T(8,128)(2,1)}, bf16[256,128]{1,0:T(8,128)(2,1)}, bf16[256,128]{1,0:T(8,128)(2,1)}, bf16[256,128]{1,0:T(8,128)(2,1)}, bf16[2...) custom-call(s32[2]{0:T(128)} %pad_add_fusion.place, ...), custom_call_target="tpu_custom_call" | custom-call | tf_op jit(solution)/shard_map/pallas_call | solution.py:249
  5.4 1.5 collective-permute-start.15
  6.9 2.7 %collective-permute-start.16 = (bf16[256,128]{1,0:T(8,128)(2,1)}, bf16[256,128]{1,0:T(8,128)(2,1)S(1)}, u32[]{:S(2)}, u32[]{:S(2)}) collective-permute-start(bf16[256,128]{1,0:T(8,128)(2,1)} %get-tuple-element.61), channel_id=1, source_target_pairs={{0,2},{1,3},{2,0},{3,1},{4,6},{5,7},{6,4},{7,5},{8,10},{9,11},{10,... | collective-permute-start | bytes 196616 | tf_op jit(solution)/shard_map/ppermute | solution.py:38
  9.6 1.4 collective-permute-start.17
  11.7 1.4 collective-permute-done.16
  13.1 1.1 collective-permute-done.17
  14.1 0.9 pad_maximum_fusion.1.refs_4_
  15.0 2.0 %collective-permute-start.18 = (bf16[4,256,128]{2,1,0:T(8,128)(2,1)S(1)}, bf16[4,256,128]{2,1,0:T(8,128)(2,1)S(1)}, u32[]{:S(2)}, u32[]{:S(2)}) collective-permute-start(bf16[4,256,128]{2,1,0:T(8,128)(2,1)S(1)} %pad_maximum_fusion.1.refs_4_), channel_id=1, source_target_pairs={{0,4},{1,5},{2,6},{3,7},{4,8},{5,9},{6,10},{7,11},{8,12},{9,13},{1... | collective-permute-start | bytes 786440 | tf_op jit(solution)/shard_map/ppermute | solution.py:38
  17.0 3.6 %collective-permute-start.19 = (bf16[4,256,128]{2,1,0:T(8,128)(2,1)S(1)}, bf16[4,256,128]{2,1,0:T(8,128)(2,1)S(1)}, u32[]{:S(2)}, u32[]{:S(2)}) collective-permute-start(bf16[4,256,128]{2,1,0:T(8,128)(2,1)S(1)} %pad_maximum_fusion.1.refs_4_), channel_id=1, source_target_pairs={{0,8},{1,9},{2,10},{3,11},{4,12},{5,13},{6,14},{7,15},{8,0},{9,1},... | collective-permute-start | bytes 786440 | tf_op jit(solution)/shard_map/ppermute | solution.py:38
  20.6 6.2 %shard_map.103 = (bf16[2064,128]{1,0:T(8,128)(2,1)}, bf16[2064,128]{1,0:T(8,128)(2,1)}, bf16[2064,128]{1,0:T(8,128)(2,1)}, bf16[2064,128]{1,0:T(8,128)(2,1)}, bf...) custom-call(s32[2]{0:T(128)} %pad_add_fusion.place, ...), custom_call_target="tpu_custom_call" | custom-call | tf_op jit(solution)/shard_map/pallas_call | solution.py:257
  27.4 2.4 %collective-permute-start.4 = (bf16[256,128]{1,0:T(8,128)(2,1)S(1)}, bf16[256,128]{1,0:T(8,128)(2,1)S(1)}, u32[]{:S(2)}, u32[]{:S(2)}) collective-permute-start(bf16[256,128]{1,0:T(8,128)(2,1)S(1)} %copy-done.38), channel_id=1, source_target_pairs={{0,8},{1,9},{2,10},{3,11},{4,12},{5,13},{6,14},{7,15},{8,0},{9,1},... | collective-permute-start | bytes 196616 | tf_op jit(solution)/shard_map/ppermute | solution.py:38
  29.8 3.9 %collective-permute-start.5 = (bf16[256,128]{1,0:T(8,128)(2,1)S(1)}, bf16[256,128]{1,0:T(8,128)(2,1)S(1)}, u32[]{:S(2)}, u32[]{:S(2)}) collective-permute-start(bf16[256,128]{1,0:T(8,128)(2,1)S(1)} %copy-done.37), channel_id=1, source_target_pairs={{0,12},{1,13},{2,14},{3,15},{4,0},{5,1},{6,2},{7,3},{8,4},{9,5},{1... | collective-permute-start | bytes 196616 | tf_op jit(solution)/shard_map/ppermute | solution.py:38
  34.4 2.4 %collective-permute-start.13 = (bf16[2064,128]{1,0:T(8,128)(2,1)}, bf16[2064,128]{1,0:T(8,128)(2,1)S(1)}, u32[]{:S(2)}, u32[]{:S(2)}) collective-permute-start(bf16[2064,128]{1,0:T(8,128)(2,1)} %get-tuple-element.57), channel_id=1, source_target_pairs={{0,2},{1,3},{2,0},{3,1},{4,6},{5,7},{6,4},{7,5},{8,10},{9,11},{10,... | collective-permute-start | bytes 1585160 | tf_op jit(solution)/shard_map/ppermute | solution.py:38
  36.7 1.9 %collective-permute-start.14 = (bf16[2064,128]{1,0:T(8,128)(2,1)}, bf16[2064,128]{1,0:T(8,128)(2,1)S(1)}, u32[]{:S(2)}, u32[]{:S(2)}) collective-permute-start(bf16[2064,128]{1,0:T(8,128)(2,1)} %get-tuple-element.58), channel_id=1, source_target_pairs={{0,3},{1,0},{2,1},{3,2},{4,7},{5,4},{6,5},{7,6},{8,11},{9,8},{10,9... | collective-permute-start | bytes 1585160 | tf_op jit(solution)/shard_map/ppermute | solution.py:38
  38.7 3.8 %collective-permute-start.20 = (bf16[4,256,128]{2,1,0:T(8,128)(2,1)S(1)}, bf16[4,256,128]{2,1,0:T(8,128)(2,1)S(1)}, u32[]{:S(2)}, u32[]{:S(2)}) collective-permute-start(bf16[4,256,128]{2,1,0:T(8,128)(2,1)S(1)} %pad_maximum_fusion.1.refs_4_), channel_id=1, source_target_pairs={{0,12},{1,13},{2,14},{3,15},{4,0},{5,1},{6,2},{7,3},{8,4},{9,5},{1... | collective-permute-start | bytes 786440 | tf_op jit(solution)/shard_map/ppermute | solution.py:38
  43.1 7.7 %psum.7 = s32[]{:T(128)} all-reduce(s32[]{:T(128)} %reduce_sum.9), channel_id=1, replica_groups=mesh['dp'=8,'seq'=16] {'dp'}, use_global_device_ids=true, to_apply=%region_1.2 | all-reduce | flops 1 | bytes 8 | tf_op jit(solution)/shard_map/psum | solution.py:241
  52.4 4.8 %collective-permute-done.6.refs_5_ = bf16[4,256,128]{2,1,0:T(8,128)(2,1)S(1)} collective-permute-done((bf16[4,256,128]{2,1,0:T(8,128)(2,1)S(1)}, bf16[4,256,128]{2,1,0:T(8,128)(2,1)S(1)}, u32[]{:S(2)}, u32[]{:S(2)}) %collective-permute-start.6) | collective-permute-done | bytes 262176 | tf_op jit(solution)/shard_map/ppermute | solution.py:38
  57.9 2.1 %collective-permute-start.1 = (bf16[2064,128]{1,0:T(8,128)(2,1)}, bf16[2064,128]{1,0:T(8,128)(2,1)S(1)}, u32[]{:S(2)}, u32[]{:S(2)}) collective-permute-start(bf16[2064,128]{1,0:T(8,128)(2,1)} %get-tuple-element.45), channel_id=1, source_target_pairs={{0,8},{1,9},{2,10},{3,11},{4,12},{5,13},{6,14},{7,15},{8,0},{9,1},... | collective-permute-start | bytes 1585160 | tf_op jit(solution)/shard_map/ppermute | solution.py:38
  60.1 0.8 collective-permute-start.2
  61.5 1.3 stack.146.meta
  62.8 1.2 stack.137.meta
  64.3 1.6 collective-permute-start.8
  65.9 15.2 %shard_map.106 = (bf16[1024,128]{1,0:T(8,128)(2,1)}, bf16[1024,128]{1,0:T(8,128)(2,1)}, bf16[1024,128]{1,0:T(8,128)(2,1)}, bf16[1024,128]{1,0:T(8,128)(2,1)}, bf...) custom-call(s32[17]{0:T(128)} %stack.146.meta, ...), custom_call_target="tpu_custom_call" | custom-call | flops 5368709120 | bytes 8388608 | tf_op jit(solution)/shard_map/pallas_call | solution.py:188
  81.4 18.9 %collective-permute-start.31 = (bf16[4,2,128,128]{3,2,1,0:T(8,128)(2,1)}, bf16[4,2,128,128]{3,2,1,0:T(8,128)(2,1)S(1)}, u32[]{:S(2)}, u32[]{:S(2)}) collective-permute-start(bf16[4,2,128,128]{3,2,1,0:T(8,128)(2,1)} %get-tuple-element.77), channel_id=1, source_target_pairs={{0,8},{1,9},{2,10},{3,11},{4,12},{5,13},{6,14},{7,15},{8,0},{9,1},... | collective-permute-start | bytes 786440 | tf_op jit(solution)/shard_map/ppermute | solution.py:38
  100.3 1.3 collective-permute-start.32
  101.6 0.8 copy-done.27
  102.4 19.1 %shard_map.105 = (bf16[1024,128]{1,0:T(8,128)(2,1)}, bf16[1024,128]{1,0:T(8,128)(2,1)}, bf16[1024,128]{1,0:T(8,128)(2,1)}, bf16[1024,128]{1,0:T(8,128)(2,1)}, bf...) custom-call(s32[17]{0:T(128)} %stack.137.meta, ...), custom_call_target="tpu_custom_call" | custom-call | flops 5368709120 | bytes 8388608 | tf_op jit(solution)/shard_map/pallas_call | solution.py:188
  121.7 2.0 %collective-permute-start.26 = (bf16[4,2,128,128]{3,2,1,0:T(8,128)(2,1)}, bf16[4,2,128,128]{3,2,1,0:T(8,128)(2,1)S(1)}, u32[]{:S(2)}, u32[]{:S(2)}) collective-permute-start(bf16[4,2,128,128]{3,2,1,0:T(8,128)(2,1)} %get-tuple-element.70), channel_id=1, source_target_pairs={{0,1},{1,2},{2,3},{3,0},{4,5},{5,6},{6,7},{7,4},{8,9},{9,10},{10,1... | collective-permute-start | bytes 786440 | tf_op jit(solution)/shard_map/ppermute | solution.py:38
  123.7 2.7 %collective-permute-start.21 = (bf16[1024,128]{1,0:T(8,128)(2,1)S(1)}, bf16[1024,128]{1,0:T(8,128)(2,1)S(1)}, u32[]{:S(2)}, u32[]{:S(2)}) collective-permute-start(bf16[1024,128]{1,0:T(8,128)(2,1)S(1)} %copy-done.34), channel_id=1, source_target_pairs={{0,3},{1,0},{2,1},{3,2},{4,7},{5,4},{6,5},{7,6},{8,11},{9,8},{10,9... | collective-permute-start | bytes 786440 | tf_op jit(solution)/shard_map/ppermute | solution.py:38
  126.4 1.5 collective-permute-start.22
  127.9 4.4 %collective-permute-done.24.b = bf16[4,2,128,128]{3,2,1,0:T(8,128)(2,1)S(1)} collective-permute-done((bf16[4,2,128,128]{3,2,1,0:T(8,128)(2,1)}, bf16[4,2,128,128]{3,2,1,0:T(8,128)(2,1)S(1)}, u32[]{:S(2)}, u32[]{:S(2)}) %collective-permute-start.24) | collective-permute-done | bytes 262176 | tf_op jit(solution)/shard_map/ppermute | solution.py:38
  132.6 0.7 collective-permute-start.10
  133.3 5.0 %collective-permute-done.26.d = bf16[4,2,128,128]{3,2,1,0:T(8,128)(2,1)S(1)} collective-permute-done((bf16[4,2,128,128]{3,2,1,0:T(8,128)(2,1)}, bf16[4,2,128,128]{3,2,1,0:T(8,128)(2,1)S(1)}, u32[]{:S(2)}, u32[]{:S(2)}) %collective-permute-start.26) | collective-permute-done | bytes 262176 | tf_op jit(solution)/shard_map/ppermute | solution.py:38
  138.5 5.2 %collective-permute-done.21.refs_5_ = bf16[1024,128]{1,0:T(8,128)(2,1)S(1)} collective-permute-done((bf16[1024,128]{1,0:T(8,128)(2,1)S(1)}, bf16[1024,128]{1,0:T(8,128)(2,1)S(1)}, u32[]{:S(2)}, u32[]{:S(2)}) %collective-permute-start.21) | collective-permute-done | bytes 262176 | tf_op jit(solution)/shard_map/ppermute | solution.py:38
  143.7 2.2 %collective-permute-start.9 = (bf16[1024,128]{1,0:T(8,128)(2,1)}, bf16[1024,128]{1,0:T(8,128)(2,1)S(1)}, u32[]{:S(2)}, u32[]{:S(2)}) collective-permute-start(bf16[1024,128]{1,0:T(8,128)(2,1)} %get-tuple-element.52), channel_id=1, source_target_pairs={{0,12},{1,13},{2,14},{3,15},{4,0},{5,1},{6,2},{7,3},{8,4},{9,5},{1... | collective-permute-start | bytes 786440 | tf_op jit(solution)/shard_map/ppermute | solution.py:38
  145.9 1.9 %shard_map.109 = (bf16[2,128,128]{2,1,0:T(8,128)(2,1)}, bf16[2,128,128]{2,1,0:T(8,128)(2,1)}, bf16[2,128,128]{2,1,0:T(8,128)(2,1)}, bf16[2,128,128]{2,1,0:T(8,128)(2,1)}) custom-call(bf16[4,2,128,128]{3,2,1,0:T(8,128)(2,1)} %get-tuple-element.75.a, bf16[4,2,128,128]{3,2,1,0:T(8,128)(2,1)} %copy-done.8, bf16[4,2,128,128]{3,2,1,0:T(8,128)(2,1)} %copy-done.9, ...), custom_call_target="tpu_custom_call" | custom-call | tf_op jit(solution)/shard_map/pallas_call | solution.py:284
  147.9 3.7 %collective-permute-start.33 = (bf16[2,128,128]{2,1,0:T(8,128)(2,1)}, bf16[2,128,128]{2,1,0:T(8,128)(2,1)S(1)}, u32[]{:S(2)}, u32[]{:S(2)}) collective-permute-start(bf16[2,128,128]{2,1,0:T(8,128)(2,1)} %get-tuple-element.80), channel_id=1, source_target_pairs={{0,3},{1,0},{2,1},{3,2},{4,7},{5,4},{6,5},{7,6},{8,11},{9,8},{10,9... | collective-permute-start | bytes 196616 | tf_op jit(solution)/shard_map/ppermute | solution.py:38
  151.6 1.9 %shard_map.108 = (bf16[2,128,128]{2,1,0:T(8,128)(2,1)}, bf16[2,128,128]{2,1,0:T(8,128)(2,1)}, bf16[2,128,128]{2,1,0:T(8,128)(2,1)}, bf16[2,128,128]{2,1,0:T(8,128)(2,1)}) custom-call(bf16[4,2,128,128]{3,2,1,0:T(8,128)(2,1)} %get-tuple-element.67.a, bf16[4,2,128,128]{3,2,1,0:T(8,128)(2,1)} %copy-done.11, bf16[4,2,128,128]{3,2,1,0:T(8,128)(2,1)} %copy-done.12, ...), custom_call_target="tpu_custom_call" | custom-call | tf_op jit(solution)/shard_map/pallas_call | solution.py:284
  153.9 0.9 collective-permute-start.35
  154.9 1.8 %collective-permute-start.28 = (bf16[2,128,128]{2,1,0:T(8,128)(2,1)}, bf16[2,128,128]{2,1,0:T(8,128)(2,1)S(1)}, u32[]{:S(2)}, u32[]{:S(2)}) collective-permute-start(bf16[2,128,128]{2,1,0:T(8,128)(2,1)} %get-tuple-element.73), channel_id=1, source_target_pairs={{0,8},{1,9},{2,10},{3,11},{4,12},{5,13},{6,14},{7,15},{8,0},{9,1},... | collective-permute-start | bytes 196616 | tf_op jit(solution)/shard_map/ppermute | solution.py:38
  156.9 3.4 %shard_map.107 = bf16[2,128,4,8,128]{4,3,2,1,0:T(8,128)(2,1)} custom-call(s32[2]{0:T(128)} %pad_add_fusion.place, bf16[1024,128]{1,0:T(8,128)(2,1)} %get-tuple-element.51.refs_0_, bf16[1024,128]{1,0:T(8,128)(2,1)} %copy-done.5, bf16[1024,128]{1,0:T(8,128)(2,1)} %copy-done.3, bf16[1024,128]{1,0:T(8,128)(2,1)} %copy-done.4, ...), custom_call_target="tpu_custom_call" | custom-call | tf_op jit(solution)/shard_map/pallas_call | solution.py:293
  160.8 1.5 collective-permute-done.29.refs_3_
  163.0 1.9 %shard_map.110 = bf16[2,4,2,128,128]{4,3,2,1,0:T(8,128)(2,1)} custom-call(s32[2]{0:T(128)} %pad_add_fusion.place, bf16[2,128,128]{2,1,0:T(8,128)(2,1)} %get-tuple-element.71.refs_0_, bf16[2,128,128]{2,1,0:T(8,128)(2,1)} %copy-done.18, bf16[2,128,128]{2,1,0:T(8,128)(2,1)} %copy-done.19, bf16[2,128,128]{2,1,0:T(8,128)(2,1)} %copy-done.20, ...), custom_call_target="tpu_custom_call" | custom-call | tf_op jit(solution)/shard_map/pallas_call | solution.py:300
  164.9 1.1 slice_bitcast_fusion
  166.0 0.9 copy.12
  166.9 0.9 copy.13
  (125 shorter events, 7.5 us)
Async XLA Ops:
  5.4 6.3 %collective-permute-start.15 = (bf16[256,128]{1,0:T(8,128)(2,1)}, bf16[256,128]{1,0:T(8,128)(2,1)S(1)}, u32[]{:S(2)}, u32[]{:S(2)}) collective-permute-start(bf16[256,128]{1,0:T(8,128)(2,1)} %get-tuple-element.60), channel_id=1, source_target_pairs={{0,1},{1,2},{2,3},{3,0},{4,5},{5,6},{6,7},{7,4},{8,9},{9,10},{10,1... | collective-permute-start | bytes 196616 | tf_op jit(solution)/shard_map/ppermute | solution.py:38
  6.9 6.2 %collective-permute-start.16 = (bf16[256,128]{1,0:T(8,128)(2,1)}, bf16[256,128]{1,0:T(8,128)(2,1)S(1)}, u32[]{:S(2)}, u32[]{:S(2)}) collective-permute-start(bf16[256,128]{1,0:T(8,128)(2,1)} %get-tuple-element.61), channel_id=1, source_target_pairs={{0,2},{1,3},{2,0},{3,1},{4,6},{5,7},{6,4},{7,5},{8,10},{9,11},{10,... | collective-permute-start | bytes 196616 | tf_op jit(solution)/shard_map/ppermute | solution.py:38
  9.6 4.5 %collective-permute-start.17 = (bf16[256,128]{1,0:T(8,128)(2,1)}, bf16[256,128]{1,0:T(8,128)(2,1)S(1)}, u32[]{:S(2)}, u32[]{:S(2)}) collective-permute-start(bf16[256,128]{1,0:T(8,128)(2,1)} %get-tuple-element.62), channel_id=1, source_target_pairs={{0,3},{1,0},{2,1},{3,2},{4,7},{5,4},{6,5},{7,6},{8,11},{9,8},{10,9... | collective-permute-start | bytes 196616 | tf_op jit(solution)/shard_map/ppermute | solution.py:38
  15.0 23.6 %copy-start.6 = (bf16[4,256,128]{2,1,0:T(8,128)(2,1)}, bf16[4,256,128]{2,1,0:T(8,128)(2,1)S(1)}, u32[]{:S(2)}) copy-start(bf16[4,256,128]{2,1,0:T(8,128)(2,1)S(1)} %pad_maximum_fusion.1.refs_4_) | copy-start | bytes 786436
  15.0 23.6 %collective-permute-start.18 = (bf16[4,256,128]{2,1,0:T(8,128)(2,1)S(1)}, bf16[4,256,128]{2,1,0:T(8,128)(2,1)S(1)}, u32[]{:S(2)}, u32[]{:S(2)}) collective-permute-start(bf16[4,256,128]{2,1,0:T(8,128)(2,1)S(1)} %pad_maximum_fusion.1.refs_4_), channel_id=1, source_target_pairs={{0,4},{1,5},{2,6},{3,7},{4,8},{5,9},{6,10},{7,11},{8,12},{9,13},{1... | collective-permute-start | bytes 786440 | tf_op jit(solution)/shard_map/ppermute | solution.py:38
  17.0 25.4 %collective-permute-start.19 = (bf16[4,256,128]{2,1,0:T(8,128)(2,1)S(1)}, bf16[4,256,128]{2,1,0:T(8,128)(2,1)S(1)}, u32[]{:S(2)}, u32[]{:S(2)}) collective-permute-start(bf16[4,256,128]{2,1,0:T(8,128)(2,1)S(1)} %pad_maximum_fusion.1.refs_4_), channel_id=1, source_target_pairs={{0,8},{1,9},{2,10},{3,11},{4,12},{5,13},{6,14},{7,15},{8,0},{9,1},... | collective-permute-start | bytes 786440 | tf_op jit(solution)/shard_map/ppermute | solution.py:38
  20.6 9.3 %collective-permute-start.3 = (bf16[256,128]{1,0:T(8,128)(2,1)}, bf16[256,128]{1,0:T(8,128)(2,1)S(1)}, u32[]{:S(2)}, u32[]{:S(2)}) collective-permute-start(bf16[256,128]{1,0:T(8,128)(2,1)} %get-tuple-element.48), channel_id=1, source_target_pairs={{0,4},{1,5},{2,6},{3,7},{4,8},{5,9},{6,10},{7,11},{8,12},{9,13},{1... | collective-permute-start | bytes 196616 | tf_op jit(solution)/shard_map/ppermute | solution.py:38
  20.6 31.6 %copy-start.22 = (f32[2]{0:T(128)S(1)}, f32[2]{0:T(128)}, u32[]{:S(2)}) copy-start(f32[2]{0:T(128)} %constant.195.clone) | copy-start | bytes 28
  26.8 33.2 %collective-permute-start.12 = (bf16[2064,128]{1,0:T(8,128)(2,1)}, bf16[2064,128]{1,0:T(8,128)(2,1)S(1)}, u32[]{:S(2)}, u32[]{:S(2)}) collective-permute-start(bf16[2064,128]{1,0:T(8,128)(2,1)} %get-tuple-element.56), channel_id=1, source_target_pairs={{0,1},{1,2},{2,3},{3,0},{4,5},{5,6},{6,7},{7,4},{8,9},{9,10},{10,1... | collective-permute-start | bytes 1585160 | tf_op jit(solution)/shard_map/ppermute | solution.py:38
  27.4 6.9 %collective-permute-start.4 = (bf16[256,128]{1,0:T(8,128)(2,1)S(1)}, bf16[256,128]{1,0:T(8,128)(2,1)S(1)}, u32[]{:S(2)}, u32[]{:S(2)}) collective-permute-start(bf16[256,128]{1,0:T(8,128)(2,1)S(1)} %copy-done.38), channel_id=1, source_target_pairs={{0,8},{1,9},{2,10},{3,11},{4,12},{5,13},{6,14},{7,15},{8,0},{9,1},... | collective-permute-start | bytes 196616 | tf_op jit(solution)/shard_map/ppermute | solution.py:38
  29.8 6.9 %collective-permute-start.5 = (bf16[256,128]{1,0:T(8,128)(2,1)S(1)}, bf16[256,128]{1,0:T(8,128)(2,1)S(1)}, u32[]{:S(2)}, u32[]{:S(2)}) collective-permute-start(bf16[256,128]{1,0:T(8,128)(2,1)S(1)} %copy-done.37), channel_id=1, source_target_pairs={{0,12},{1,13},{2,14},{3,15},{4,0},{5,1},{6,2},{7,3},{8,4},{9,5},{1... | collective-permute-start | bytes 196616 | tf_op jit(solution)/shard_map/ppermute | solution.py:38
  34.4 29.7 %collective-permute-start.13 = (bf16[2064,128]{1,0:T(8,128)(2,1)}, bf16[2064,128]{1,0:T(8,128)(2,1)S(1)}, u32[]{:S(2)}, u32[]{:S(2)}) collective-permute-start(bf16[2064,128]{1,0:T(8,128)(2,1)} %get-tuple-element.57), channel_id=1, source_target_pairs={{0,2},{1,3},{2,0},{3,1},{4,6},{5,7},{6,4},{7,5},{8,10},{9,11},{10,... | collective-permute-start | bytes 1585160 | tf_op jit(solution)/shard_map/ppermute | solution.py:38
  36.7 27.5 %collective-permute-start.14 = (bf16[2064,128]{1,0:T(8,128)(2,1)}, bf16[2064,128]{1,0:T(8,128)(2,1)S(1)}, u32[]{:S(2)}, u32[]{:S(2)}) collective-permute-start(bf16[2064,128]{1,0:T(8,128)(2,1)} %get-tuple-element.58), channel_id=1, source_target_pairs={{0,3},{1,0},{2,1},{3,2},{4,7},{5,4},{6,5},{7,6},{8,11},{9,8},{10,9... | collective-permute-start | bytes 1585160 | tf_op jit(solution)/shard_map/ppermute | solution.py:38
  38.6 42.5 %copy-start.7 = (bf16[4,256,128]{2,1,0:T(8,128)(2,1)}, bf16[4,256,128]{2,1,0:T(8,128)(2,1)S(1)}, u32[]{:S(2)}) copy-start(bf16[4,256,128]{2,1,0:T(8,128)(2,1)S(1)} %pad_maximum_fusion.refs_4_) | copy-start | bytes 786436
  38.7 13.6 %collective-permute-start.20 = (bf16[4,256,128]{2,1,0:T(8,128)(2,1)S(1)}, bf16[4,256,128]{2,1,0:T(8,128)(2,1)S(1)}, u32[]{:S(2)}, u32[]{:S(2)}) collective-permute-start(bf16[4,256,128]{2,1,0:T(8,128)(2,1)S(1)} %pad_maximum_fusion.1.refs_4_), channel_id=1, source_target_pairs={{0,12},{1,13},{2,14},{3,15},{4,0},{5,1},{6,2},{7,3},{8,4},{9,5},{1... | collective-permute-start | bytes 786440 | tf_op jit(solution)/shard_map/ppermute | solution.py:38
  42.4 14.8 %collective-permute-start.6 = (bf16[4,256,128]{2,1,0:T(8,128)(2,1)S(1)}, bf16[4,256,128]{2,1,0:T(8,128)(2,1)S(1)}, u32[]{:S(2)}, u32[]{:S(2)}) collective-permute-start(bf16[4,256,128]{2,1,0:T(8,128)(2,1)S(1)} %pad_maximum_fusion.refs_4_), channel_id=1, source_target_pairs={{0,1},{1,2},{2,3},{3,0},{4,5},{5,6},{6,7},{7,4},{8,9},{9,10},{10,1... | collective-permute-start | bytes 786440 | tf_op jit(solution)/shard_map/ppermute | solution.py:38
  52.3 48.0 %collective-permute-start = (bf16[2064,128]{1,0:T(8,128)(2,1)}, bf16[2064,128]{1,0:T(8,128)(2,1)S(1)}, u32[]{:S(2)}, u32[]{:S(2)}) collective-permute-start(bf16[2064,128]{1,0:T(8,128)(2,1)} %get-tuple-element.44), channel_id=1, source_target_pairs={{0,4},{1,5},{2,6},{3,7},{4,8},{5,9},{6,10},{7,11},{8,12},{9,13},{1... | collective-permute-start | bytes 1585160 | tf_op jit(solution)/shard_map/ppermute | solution.py:38
  57.9 43.6 %collective-permute-start.1 = (bf16[2064,128]{1,0:T(8,128)(2,1)}, bf16[2064,128]{1,0:T(8,128)(2,1)S(1)}, u32[]{:S(2)}, u32[]{:S(2)}) collective-permute-start(bf16[2064,128]{1,0:T(8,128)(2,1)} %get-tuple-element.45), channel_id=1, source_target_pairs={{0,8},{1,9},{2,10},{3,11},{4,12},{5,13},{6,14},{7,15},{8,0},{9,1},... | collective-permute-start | bytes 1585160 | tf_op jit(solution)/shard_map/ppermute | solution.py:38
  60.1 41.5 %collective-permute-start.2 = (bf16[2064,128]{1,0:T(8,128)(2,1)}, bf16[2064,128]{1,0:T(8,128)(2,1)}, u32[]{:S(2)}, u32[]{:S(2)}) collective-permute-start(bf16[2064,128]{1,0:T(8,128)(2,1)} %get-tuple-element.46), channel_id=1, source_target_pairs={{0,12},{1,13},{2,14},{3,15},{4,0},{5,1},{6,2},{7,3},{8,4},{9,5},{1... | collective-permute-start | bytes 1585160 | tf_op jit(solution)/shard_map/ppermute | solution.py:38
  64.1 17.0 %collective-permute-start.7 = (bf16[4,256,128]{2,1,0:T(8,128)(2,1)S(1)}, bf16[4,256,128]{2,1,0:T(8,128)(2,1)S(1)}, u32[]{:S(2)}, u32[]{:S(2)}) collective-permute-start(bf16[4,256,128]{2,1,0:T(8,128)(2,1)S(1)} %pad_maximum_fusion.refs_4_), channel_id=1, source_target_pairs={{0,2},{1,3},{2,0},{3,1},{4,6},{5,7},{6,4},{7,5},{8,10},{9,11},{10,... | collective-permute-start | bytes 786440 | tf_op jit(solution)/shard_map/ppermute | solution.py:38
  64.3 17.1 %collective-permute-start.8 = (bf16[4,256,128]{2,1,0:T(8,128)(2,1)S(1)}, bf16[4,256,128]{2,1,0:T(8,128)(2,1)S(1)}, u32[]{:S(2)}, u32[]{:S(2)}) collective-permute-start(bf16[4,256,128]{2,1,0:T(8,128)(2,1)S(1)} %pad_maximum_fusion.refs_4_), channel_id=1, source_target_pairs={{0,3},{1,0},{2,1},{3,2},{4,7},{5,4},{6,5},{7,6},{8,11},{9,8},{10,9... | collective-permute-start | bytes 786440 | tf_op jit(solution)/shard_map/ppermute | solution.py:38
  81.1 20.5 %copy-start.35 = (bf16[4,256,128]{2,1,0:T(8,128)(2,1)}, bf16[4,256,128]{2,1,0:T(8,128)(2,1)S(1)}, u32[]{:S(2)}) copy-start(bf16[4,256,128]{2,1,0:T(8,128)(2,1)S(1)} %collective-permute-done.7.refs_6_) | copy-start | bytes 786436
  81.1 40.5 %collective-permute-start.30 = (bf16[4,2,128,128]{3,2,1,0:T(8,128)(2,1)}, bf16[4,2,128,128]{3,2,1,0:T(8,128)(2,1)S(1)}, u32[]{:S(2)}, u32[]{:S(2)}) collective-permute-start(bf16[4,2,128,128]{3,2,1,0:T(8,128)(2,1)} %get-tuple-element.76), channel_id=1, source_target_pairs={{0,12},{1,13},{2,14},{3,15},{4,0},{5,1},{6,2},{7,3},{8,4},{9,5},{1... | collective-permute-start | bytes 786440 | tf_op jit(solution)/shard_map/ppermute | solution.py:38
  81.4 20.2 %copy-start.36 = (bf16[4,256,128]{2,1,0:T(8,128)(2,1)}, bf16[4,256,128]{2,1,0:T(8,128)(2,1)S(1)}, u32[]{:S(2)}) copy-start(bf16[4,256,128]{2,1,0:T(8,128)(2,1)S(1)} %collective-permute-done.8.refs_7_) | copy-start | bytes 786436
  81.4 42.3 %collective-permute-start.31 = (bf16[4,2,128,128]{3,2,1,0:T(8,128)(2,1)}, bf16[4,2,128,128]{3,2,1,0:T(8,128)(2,1)S(1)}, u32[]{:S(2)}, u32[]{:S(2)}) collective-permute-start(bf16[4,2,128,128]{3,2,1,0:T(8,128)(2,1)} %get-tuple-element.77), channel_id=1, source_target_pairs={{0,8},{1,9},{2,10},{3,11},{4,12},{5,13},{6,14},{7,15},{8,0},{9,1},... | collective-permute-start | bytes 786440 | tf_op jit(solution)/shard_map/ppermute | solution.py:38
  100.3 26.1 %collective-permute-start.32 = (bf16[4,2,128,128]{3,2,1,0:T(8,128)(2,1)}, bf16[4,2,128,128]{3,2,1,0:T(8,128)(2,1)S(1)}, u32[]{:S(2)}, u32[]{:S(2)}) collective-permute-start(bf16[4,2,128,128]{3,2,1,0:T(8,128)(2,1)} %get-tuple-element.78), channel_id=1, source_target_pairs={{0,4},{1,5},{2,6},{3,7},{4,8},{5,9},{6,10},{7,11},{8,12},{9,13},{1... | collective-permute-start | bytes 786440 | tf_op jit(solution)/shard_map/ppermute | solution.py:38
  102.4 21.3 %copy-start.34 = (bf16[1024,128]{1,0:T(8,128)(2,1)S(1)}, bf16[1024,128]{1,0:T(8,128)(2,1)}, u32[]{:S(2)}) copy-start(bf16[1024,128]{1,0:T(8,128)(2,1)} %get-tuple-element.64) | copy-start | bytes 786436
  102.4 24.0 %copy-start.33 = (bf16[1024,128]{1,0:T(8,128)(2,1)S(1)}, bf16[1024,128]{1,0:T(8,128)(2,1)}, u32[]{:S(2)}) copy-start(bf16[1024,128]{1,0:T(8,128)(2,1)} %get-tuple-element.65) | copy-start | bytes 786436
  102.4 29.9 %copy-start.32 = (bf16[1024,128]{1,0:T(8,128)(2,1)S(1)}, bf16[1024,128]{1,0:T(8,128)(2,1)}, u32[]{:S(2)}) copy-start(bf16[1024,128]{1,0:T(8,128)(2,1)} %get-tuple-element.66) | copy-start | bytes 786436
  121.5 10.8 %collective-permute-start.24 = (bf16[4,2,128,128]{3,2,1,0:T(8,128)(2,1)}, bf16[4,2,128,128]{3,2,1,0:T(8,128)(2,1)S(1)}, u32[]{:S(2)}, u32[]{:S(2)}) collective-permute-start(bf16[4,2,128,128]{3,2,1,0:T(8,128)(2,1)} %get-tuple-element.68), channel_id=1, source_target_pairs={{0,3},{1,0},{2,1},{3,2},{4,7},{5,4},{6,5},{7,6},{8,11},{9,8},{10,9... | collective-permute-start | bytes 786440 | tf_op jit(solution)/shard_map/ppermute | solution.py:38
  121.6 11.1 %collective-permute-start.25 = (bf16[4,2,128,128]{3,2,1,0:T(8,128)(2,1)}, bf16[4,2,128,128]{3,2,1,0:T(8,128)(2,1)S(1)}, u32[]{:S(2)}, u32[]{:S(2)}) collective-permute-start(bf16[4,2,128,128]{3,2,1,0:T(8,128)(2,1)} %get-tuple-element.69), channel_id=1, source_target_pairs={{0,2},{1,3},{2,0},{3,1},{4,6},{5,7},{6,4},{7,5},{8,10},{9,11},{10,... | collective-permute-start | bytes 786440 | tf_op jit(solution)/shard_map/ppermute | solution.py:38
  121.7 24.2 %copy-start.8 = (bf16[4,2,128,128]{3,2,1,0:T(8,128)(2,1)}, bf16[4,2,128,128]{3,2,1,0:T(8,128)(2,1)S(1)}, u32[]{:S(2)}) copy-start(bf16[4,2,128,128]{3,2,1,0:T(8,128)(2,1)S(1)} %collective-permute-done.30.b) | copy-start | bytes 786436
  121.7 16.6 %collective-permute-start.26 = (bf16[4,2,128,128]{3,2,1,0:T(8,128)(2,1)}, bf16[4,2,128,128]{3,2,1,0:T(8,128)(2,1)S(1)}, u32[]{:S(2)}, u32[]{:S(2)}) collective-permute-start(bf16[4,2,128,128]{3,2,1,0:T(8,128)(2,1)} %get-tuple-element.70), channel_id=1, source_target_pairs={{0,1},{1,2},{2,3},{3,0},{4,5},{5,6},{6,7},{7,4},{8,9},{9,10},{10,1... | collective-permute-start | bytes 786440 | tf_op jit(solution)/shard_map/ppermute | solution.py:38
  123.7 22.2 %copy-start.9 = (bf16[4,2,128,128]{3,2,1,0:T(8,128)(2,1)}, bf16[4,2,128,128]{3,2,1,0:T(8,128)(2,1)S(1)}, u32[]{:S(2)}) copy-start(bf16[4,2,128,128]{3,2,1,0:T(8,128)(2,1)S(1)} %collective-permute-done.31.c) | copy-start | bytes 786436
  123.7 20.0 %collective-permute-start.21 = (bf16[1024,128]{1,0:T(8,128)(2,1)S(1)}, bf16[1024,128]{1,0:T(8,128)(2,1)S(1)}, u32[]{:S(2)}, u32[]{:S(2)}) collective-permute-start(bf16[1024,128]{1,0:T(8,128)(2,1)S(1)} %copy-done.34), channel_id=1, source_target_pairs={{0,3},{1,0},{2,1},{3,2},{4,7},{5,4},{6,5},{7,6},{8,11},{9,8},{10,9... | collective-permute-start | bytes 786440 | tf_op jit(solution)/shard_map/ppermute | solution.py:38
  126.4 19.5 %copy-start.10 = (bf16[4,2,128,128]{3,2,1,0:T(8,128)(2,1)}, bf16[4,2,128,128]{3,2,1,0:T(8,128)(2,1)S(1)}, u32[]{:S(2)}) copy-start(bf16[4,2,128,128]{3,2,1,0:T(8,128)(2,1)S(1)} %collective-permute-done.32.d) | copy-start | bytes 786436
  126.4 21.5 %collective-permute-start.22 = (bf16[1024,128]{1,0:T(8,128)(2,1)S(1)}, bf16[1024,128]{1,0:T(8,128)(2,1)S(1)}, u32[]{:S(2)}, u32[]{:S(2)}) collective-permute-start(bf16[1024,128]{1,0:T(8,128)(2,1)S(1)} %copy-done.33), channel_id=1, source_target_pairs={{0,2},{1,3},{2,0},{3,1},{4,6},{5,7},{6,4},{7,5},{8,10},{9,11},{10,... | collective-permute-start | bytes 786440 | tf_op jit(solution)/shard_map/ppermute | solution.py:38
  132.3 19.3 %copy-start.11 = (bf16[4,2,128,128]{3,2,1,0:T(8,128)(2,1)}, bf16[4,2,128,128]{3,2,1,0:T(8,128)(2,1)S(1)}, u32[]{:S(2)}) copy-start(bf16[4,2,128,128]{3,2,1,0:T(8,128)(2,1)S(1)} %collective-permute-done.24.b) | copy-start | bytes 786436
  132.3 21.2 %collective-permute-start.23 = (bf16[1024,128]{1,0:T(8,128)(2,1)S(1)}, bf16[1024,128]{1,0:T(8,128)(2,1)S(1)}, u32[]{:S(2)}, u32[]{:S(2)}) collective-permute-start(bf16[1024,128]{1,0:T(8,128)(2,1)S(1)} %copy-done.32), channel_id=1, source_target_pairs={{0,1},{1,2},{2,3},{3,0},{4,5},{5,6},{6,7},{7,4},{8,9},{9,10},{10,1... | collective-permute-start | bytes 786440 | tf_op jit(solution)/shard_map/ppermute | solution.py:38
  132.6 21.2 %collective-permute-start.10 = (bf16[1024,128]{1,0:T(8,128)(2,1)}, bf16[1024,128]{1,0:T(8,128)(2,1)S(1)}, u32[]{:S(2)}, u32[]{:S(2)}) collective-permute-start(bf16[1024,128]{1,0:T(8,128)(2,1)} %get-tuple-element.53), channel_id=1, source_target_pairs={{0,8},{1,9},{2,10},{3,11},{4,12},{5,13},{6,14},{7,15},{8,0},{9,1},... | collective-permute-start | bytes 786440 | tf_op jit(solution)/shard_map/ppermute | solution.py:38
  138.3 16.4 %collective-permute-start.11 = (bf16[1024,128]{1,0:T(8,128)(2,1)}, bf16[1024,128]{1,0:T(8,128)(2,1)S(1)}, u32[]{:S(2)}, u32[]{:S(2)}) collective-permute-start(bf16[1024,128]{1,0:T(8,128)(2,1)} %get-tuple-element.54), channel_id=1, source_target_pairs={{0,4},{1,5},{2,6},{3,7},{4,8},{5,9},{6,10},{7,11},{8,12},{9,13},{1... | collective-permute-start | bytes 786440 | tf_op jit(solution)/shard_map/ppermute | solution.py:38
  143.7 11.1 %collective-permute-start.9 = (bf16[1024,128]{1,0:T(8,128)(2,1)}, bf16[1024,128]{1,0:T(8,128)(2,1)S(1)}, u32[]{:S(2)}, u32[]{:S(2)}) collective-permute-start(bf16[1024,128]{1,0:T(8,128)(2,1)} %get-tuple-element.52), channel_id=1, source_target_pairs={{0,12},{1,13},{2,14},{3,15},{4,0},{5,1},{6,2},{7,3},{8,4},{9,5},{1... | collective-permute-start | bytes 786440 | tf_op jit(solution)/shard_map/ppermute | solution.py:38
  147.9 8.8 %collective-permute-start.33 = (bf16[2,128,128]{2,1,0:T(8,128)(2,1)}, bf16[2,128,128]{2,1,0:T(8,128)(2,1)S(1)}, u32[]{:S(2)}, u32[]{:S(2)}) collective-permute-start(bf16[2,128,128]{2,1,0:T(8,128)(2,1)} %get-tuple-element.80), channel_id=1, source_target_pairs={{0,3},{1,0},{2,1},{3,2},{4,7},{5,4},{6,5},{7,6},{8,11},{9,8},{10,9... | collective-permute-start | bytes 196616 | tf_op jit(solution)/shard_map/ppermute | solution.py:38
  153.5 6.7 %collective-permute-start.34 = (bf16[2,128,128]{2,1,0:T(8,128)(2,1)}, bf16[2,128,128]{2,1,0:T(8,128)(2,1)S(1)}, u32[]{:S(2)}, u32[]{:S(2)}) collective-permute-start(bf16[2,128,128]{2,1,0:T(8,128)(2,1)} %get-tuple-element.81), channel_id=1, source_target_pairs={{0,2},{1,3},{2,0},{3,1},{4,6},{5,7},{6,4},{7,5},{8,10},{9,11},{10,... | collective-permute-start | bytes 196616 | tf_op jit(solution)/shard_map/ppermute | solution.py:38
  153.9 6.5 %collective-permute-start.35 = (bf16[2,128,128]{2,1,0:T(8,128)(2,1)}, bf16[2,128,128]{2,1,0:T(8,128)(2,1)S(1)}, u32[]{:S(2)}, u32[]{:S(2)}) collective-permute-start(bf16[2,128,128]{2,1,0:T(8,128)(2,1)} %get-tuple-element.82), channel_id=1, source_target_pairs={{0,1},{1,2},{2,3},{3,0},{4,5},{5,6},{6,7},{7,4},{8,9},{9,10},{10,1... | collective-permute-start | bytes 196616 | tf_op jit(solution)/shard_map/ppermute | solution.py:38
  154.8 5.6 %collective-permute-start.27 = (bf16[2,128,128]{2,1,0:T(8,128)(2,1)}, bf16[2,128,128]{2,1,0:T(8,128)(2,1)S(1)}, u32[]{:S(2)}, u32[]{:S(2)}) collective-permute-start(bf16[2,128,128]{2,1,0:T(8,128)(2,1)} %get-tuple-element.72), channel_id=1, source_target_pairs={{0,12},{1,13},{2,14},{3,15},{4,0},{5,1},{6,2},{7,3},{8,4},{9,5},{1... | collective-permute-start | bytes 196616 | tf_op jit(solution)/shard_map/ppermute | solution.py:38
  154.9 6.0 %collective-permute-start.28 = (bf16[2,128,128]{2,1,0:T(8,128)(2,1)}, bf16[2,128,128]{2,1,0:T(8,128)(2,1)S(1)}, u32[]{:S(2)}, u32[]{:S(2)}) collective-permute-start(bf16[2,128,128]{2,1,0:T(8,128)(2,1)} %get-tuple-element.73), channel_id=1, source_target_pairs={{0,8},{1,9},{2,10},{3,11},{4,12},{5,13},{6,14},{7,15},{8,0},{9,1},... | collective-permute-start | bytes 196616 | tf_op jit(solution)/shard_map/ppermute | solution.py:38
  156.7 5.7 %collective-permute-start.29 = (bf16[2,128,128]{2,1,0:T(8,128)(2,1)}, bf16[2,128,128]{2,1,0:T(8,128)(2,1)S(1)}, u32[]{:S(2)}, u32[]{:S(2)}) collective-permute-start(bf16[2,128,128]{2,1,0:T(8,128)(2,1)} %get-tuple-element.74), channel_id=1, source_target_pairs={{0,4},{1,5},{2,6},{3,7},{4,8},{5,9},{6,10},{7,11},{8,12},{9,13},{1... | collective-permute-start | bytes 196616 | tf_op jit(solution)/shard_map/ppermute | solution.py:38
  (27 other events, 164.6 us)

commit v2 on v1

v2 whole, which is shorter than its diff:
```python
import functools
import math

import jax
import jax.numpy as jnp
from jax import lax
from jax.experimental import pallas as pl
from jax.experimental.pallas import tpu as pltpu
from jax.sharding import PartitionSpec as P

f32, bf16 = jnp.float32, jnp.bfloat16
NT = (((1,), (1,)), ((), ()))
NN = (((1,), (0,)), ((), ()))

SIDE = 4
TOK = 128
GROUP = 8
DIM = 128
ROWS = TOK * GROUP
EXTRA = 16
FULL = TOK * SIDE * SIDE
CHUNK = 512
SCALE = 1.0 / math.sqrt(DIM)
EXP2 = SCALE * math.log2(math.e)
VMEM_BYTES = 56 * 1024 * 1024


def shift_pairs(kind, by):
    pairs = []
    for z in range(SIDE):
        for x in range(SIDE):
            to = ((z + by) % SIDE) * SIDE + x if kind == 0 else z * SIDE + (x + by) % SIDE
            pairs.append((z * SIDE + x, to))
    return pairs


def shift(value, kind, by):
    return lax.ppermute(value, "seq", shift_pairs(kind, by % SIDE))


def any_spec():
    return pl.BlockSpec(memory_space=pl.ANY)


def vmem_spec():
    return pl.BlockSpec(memory_space=pltpu.VMEM)


def smem_spec():
    return pl.BlockSpec(memory_space=pltpu.SMEM)


def params():
    return pltpu.CompilerParams(vmem_limit_bytes=VMEM_BYTES)


def pack_kernel(place, q_ref, g_ref, o_ref, *outs):
    for d in range(SIDE):
        head = lax.rem(place[0] + d, SIDE)
        out = outs[d]
        g = g_ref[:, head].reshape(ROWS, DIM)
        o = o_ref[:, head].reshape(ROWS, DIM)
        out[0:ROWS, :] = q_ref[:, head].reshape(ROWS, DIM)
        out[ROWS:2 * ROWS, :] = g
        prod = g.astype(f32) * o.astype(f32)
        high = prod.astype(bf16)
        low = (prod - high.astype(f32)).astype(bf16)
        ones = jnp.ones((8, DIM), bf16)
        delta = lax.dot_general(ones, high, NT, preferred_element_type=f32)
        delta += lax.dot_general(ones, low, NT, preferred_element_type=f32)
        rows = jnp.concatenate(
            [delta[0:1, a * DIM:(a + 1) * DIM] for a in range(ROWS // DIM)], axis=0
        )
        d_high = rows.astype(bf16)
        d_low = (rows - d_high.astype(f32)).astype(bf16)
        out[2 * ROWS:, :] = jnp.concatenate([d_high, d_low], axis=0)


def pack(place, s, query, out_grad, output):
    block = (None, TOK, SIDE, GROUP, DIM)
    spec = pl.BlockSpec(block, lambda i: (s, 0, 0, 0, 0))
    return pl.pallas_call(
        pack_kernel,
        grid=(1,),
        in_specs=[smem_spec()] + [spec] * 3,
        out_specs=[vmem_spec()] * SIDE,
        out_shape=[jax.ShapeDtypeStruct((2 * ROWS + EXTRA, DIM), bf16)] * SIDE,
        compiler_params=params(),
    )(place, query, out_grad, output)


def token_block(z, x, d, e):
    return lax.rem(z - d + SIDE, SIDE) * SIDE + lax.rem(x - e + SIDE, SIDE)


def attention_kernel(seq, shifts, first_call, last_call, *refs):
    count = len(shifts)
    refs = list(refs)
    meta, coef = refs[:2]
    packs = refs[2:2 + count]
    kvs = refs[2 + count:2 + count + SIDE]
    refs = refs[2 + count + SIDE:]
    if not first_call:
        acc_in, refs = refs[:2], refs[2:]
    dqs, refs = refs[:count], refs[count:]
    if last_call:
        dkv, refs = refs[0], refs[1:]
        dka, dva = refs[:2]
        refs = refs[2:]
    else:
        dka, dva = refs[:2]
        refs = refs[2:]
    pk, k_s, v_s, kt_s, p_s, m_s, gm_s, dqt_s, dq_s, sem_p, sem_kv, sem_o = refs
    z, x, length = meta[0], meta[1], meta[2 + seq]
    copies = []
    for e in range(SIDE):
        for d in range(SIDE):
            at, slot = token_block(z, x, d, e), e * SIDE + d
            copies.append(pltpu.make_async_copy(kvs[e].at[d, 0], k_s.at[at], sem_kv.at[0, slot]))
            copies.append(pltpu.make_async_copy(kvs[e].at[d, 1], v_s.at[at], sem_kv.at[1, slot]))
    for d in range(count):
        copies.append(pltpu.make_async_copy(packs[d], pk.at[d], sem_p.at[d]))
    for copy in copies:
        copy.start()
    if first_call:
        dka[...] = jnp.zeros_like(dka)
        dva[...] = jnp.zeros_like(dva)
    else:
        dka[...] = acc_in[0][...]
        dva[...] = acc_in[1][...]
    for copy in copies:
        copy.wait()
    kt_s[...] = k_s[...].reshape(FULL, DIM).T
    factor = coef[seq]
    along = [token_block(z, x, d, 0) for d in shifts]

    def one_block(d, _):
        block = along[0]
        for n in range(1, count):
            block = jnp.where(d == n, along[n], block)
        first = block * TOK

        @pl.when(first >= length)
        def _():
            dq_s[d] = jnp.zeros((ROWS, DIM), bf16)

        @pl.when(first < length)
        def _():
            token = lax.broadcasted_iota(jnp.int32, (ROWS, DIM), 0) // GROUP + first
            gm_s[...] = jnp.where(token < length, pk[d, ROWS:2 * ROWS, :], jnp.zeros((), bf16))
            lane_token = lax.broadcasted_iota(jnp.int32, (1, ROWS), 1) // GROUP + first
            tail = pk[d, 2 * ROWS:, :].astype(f32)
            tail = tail[0:8] + tail[8:16]
            delta = jnp.concatenate([tail[a:a + 1, :] for a in range(8)], axis=1)
            delta = jnp.where(lane_token < length, delta, 0.0)
            steps = (first + TOK + CHUNK - 1) // CHUNK

            def blocks(c):
                return pl.ds(c * (CHUNK // TOK), CHUNK // TOK)

            def scores_step(c, carry, masked):
                top, total = carry
                k0 = pl.multiple_of(c * CHUNK, CHUNK)
                s = lax.dot_general(
                    k_s[blocks(c)].reshape(CHUNK, DIM),
                    pk[d, 0:ROWS, :],
                    NT,
                    preferred_element_type=f32,
                )
                if masked:
                    key = lax.broadcasted_iota(jnp.int32, (CHUNK, ROWS), 0) + k0
                    s = jnp.where(key <= lane_token, s, -jnp.inf)
                new = jnp.maximum(top, jnp.max(s, axis=0, keepdims=True))
                p = jnp.exp2((s - new) * EXP2)
                p_s[pl.ds(k0, CHUNK), :] = p
                m_s[c] = jnp.broadcast_to(new, (8, ROWS))
                total = total * jnp.exp2((top - new) * EXP2) + jnp.sum(p, axis=0, keepdims=True)
                return new, total

            carry = (jnp.full((1, ROWS), -1e30, f32), jnp.zeros((1, ROWS), f32))
            carry = lax.fori_loop(0, steps - 1, lambda c, x: scores_step(c, x, False), carry)
            top, total = scores_step(steps - 1, carry, True)
            inverse = 1.0 / total
            dqt_s[...] = jnp.zeros_like(dqt_s)

            def grads_step(c, _):
                k0 = pl.multiple_of(c * CHUNK, CHUNK)
                at = pl.ds(k0, CHUNK)
                g = gm_s[...]
                weight = jnp.exp2((m_s[c][0:1] - top) * EXP2) * inverse
                dp = lax.dot_general(
                    v_s[blocks(c)].reshape(CHUNK, DIM), g, NT, preferred_element_type=f32
                )
                prob = p_s[at, :] * weight
                ds = (prob * (dp - delta)).astype(bf16)
                dva[at, :] += lax.dot_general(prob.astype(bf16), g, NN, preferred_element_type=f32)
                dka[at, :] += lax.dot_general(ds, pk[d, 0:ROWS, :], NN, preferred_element_type=f32)
                dqt_s[...] += lax.dot_general(kt_s[:, at], ds, NN, preferred_element_type=f32)
                return 0

            lax.fori_loop(0, steps, grads_step, 0)
            dq_s[d] = (dqt_s[...].T * (factor * SCALE)).astype(bf16)

        return 0

    lax.fori_loop(0, count, one_block, 0)
    outs = [pltpu.make_async_copy(dq_s.at[d], dqs[d], sem_o.at[d]) for d in range(count)]
    for copy in outs:
        copy.start()
    if last_call:
        for b in range(FULL // TOK):
            at = pl.ds(b * TOK, TOK)
            dkv[b, 0] = (dka[at, :] * (factor * SCALE)).astype(bf16)
            dkv[b, 1] = (dva[at, :] * factor).astype(bf16)
    for copy in outs:
        copy.wait()


def attention(meta, coef, seq, shifts, packs, kvs, acc_in=None, last_call=True):
    count = len(packs)
    first_call = acc_in is None
    acc = jax.ShapeDtypeStruct((FULL, DIM), f32)
    acc_scratch = [pltpu.VMEM((FULL, DIM), f32)] * 2
    out_shape = [jax.ShapeDtypeStruct((ROWS, DIM), bf16)] * count
    out_specs = [any_spec()] * count
    if last_call:
        out_shape += [jax.ShapeDtypeStruct((FULL // TOK, 2, TOK, DIM), bf16)]
        out_specs += [vmem_spec()]
    else:
        out_shape += [acc, acc]
        out_specs += [vmem_spec()] * 2
    return pl.pallas_call(
        functools.partial(attention_kernel, seq, shifts, first_call, last_call),
        in_specs=[smem_spec(), smem_spec()]
        + [any_spec()] * (count + SIDE)
        + [vmem_spec()] * (0 if first_call else 2),
        out_specs=out_specs,
        out_shape=out_shape,
        scratch_shapes=(acc_scratch if last_call else [])
        + [
            pltpu.VMEM((count, 2 * ROWS + EXTRA, DIM), bf16),
            pltpu.VMEM((FULL // TOK, TOK, DIM), bf16),
            pltpu.VMEM((FULL // TOK, TOK, DIM), bf16),
            pltpu.VMEM((DIM, FULL), bf16),
            pltpu.VMEM((FULL, ROWS), f32),
            pltpu.VMEM((FULL // CHUNK, 8, ROWS), f32),
            pltpu.VMEM((ROWS, DIM), bf16),
            pltpu.VMEM((DIM, ROWS), f32),
            pltpu.VMEM((count, ROWS, DIM), bf16),
            pltpu.SemaphoreType.DMA((count,)),
            pltpu.SemaphoreType.DMA((2, SIDE * SIDE)),
            pltpu.SemaphoreType.DMA((count,)),
        ],
        compiler_params=params(),
        cost_estimate=pl.CostEstimate(
            flops=2 * ROWS * FULL * DIM * 5 * count,
            bytes_accessed=8 << 20,
            transcendentals=ROWS * FULL * count,
        ),
    )(meta, coef, *packs, *kvs, *(() if first_call else acc_in))


def place_kernel(place, mean_len, *refs):
    rows, out = refs[:-1], refs[-1]
    for s in range(2):
        for d in range(SIDE):
            head = lax.rem(place[0] + d, SIDE)
            grad = rows[s * SIDE + d][...].astype(f32) * mean_len[0]
            out[s, :, head] = grad.astype(bf16).reshape(TOK, GROUP, DIM)


ROUNDS = (((3, 0, 1, 2),), ((2, 1, 3, 0),))


def after(value, other):
    return lax.optimization_barrier((value, other))[0]


def pack_kv_kernel(place, kv_ref, *outs):
    for d in range(SIDE):
        outs[d][...] = kv_ref[lax.rem(place[0] + d, SIDE)]


def body(query, keys, values, output, out_grad, lengths, margins):
    index = lax.axis_index("seq")
    z, x = index // SIDE, index % SIDE
    place = jnp.concatenate([jnp.stack([z, x]).astype(jnp.int32), lengths])
    weight = jax.nn.sigmoid(-margins)
    signs = jnp.array([-1.0, 1.0], f32)
    coef = jnp.repeat(weight, 2) * signs * 4.0 / lengths.astype(f32)

    kv = jnp.stack([keys, values], axis=1)
    kv = jnp.transpose(kv, (3, 0, 1, 2, 4))
    kv_parts = pl.pallas_call(
        pack_kv_kernel,
        in_specs=[smem_spec(), vmem_spec()],
        out_specs=[vmem_spec()] * SIDE,
        out_shape=[jax.ShapeDtypeStruct((2, 2, TOK, DIM), bf16)] * SIDE,
        compiler_params=params(),
    )(place, kv)
    kv_in = [kv_parts[0]] + [shift(kv_parts[d], 0, d) for d in range(1, SIDE)]
    five = (2, TOK, SIDE, GROUP, DIM)
    query, out_grad, output = (a.reshape(five) for a in (query, out_grad, output))
    query = after(query, kv_parts)
    packs = [pack(place, s, query, out_grad, output) for s in range(2)]
    kv_in = after(kv_in, packs[0])
    gathered = []
    for s in range(2):
        mine = jnp.stack([part[s] for part in kv_in], axis=0)
        gathered.append([mine] + [shift(mine, 1, e) for e in (1, 2, 3)])

    moved = []
    for s in range(2):
        mine = packs[s] if s == 0 else after(packs[s], gathered[0])
        moved.append([mine[0]] + [shift(mine[d], 0, d) for d in range(1, SIDE)])

    dq_rows, kv_grads, prev = [], [], None
    for s in range(2):
        meta = place if s == 0 else after(place, prev)
        acc, dqs = None, {}
        for n, shifts in enumerate(ROUNDS[s]):
            last = n == len(ROUNDS[s]) - 1
            packs_now = [moved[s][d] for d in shifts]
            res = attention(meta, coef, s, shifts, packs_now, gathered[s], acc, last)
            if last:
                prev = after(res[len(shifts)], list(dqs.values()) + dq_rows)
            else:
                acc = res[len(shifts):]
            for d, dq in zip(shifts, res):
                dqs[d] = dq if d == 0 else shift(dq, 0, -d)
        dq_rows += [dqs[d] for d in range(SIDE)]
        parts = lax.all_to_all(prev, "seq", 0, 0, tiled=True)
        parts = parts.reshape(SIDE, SIDE, 2, TOK, DIM).astype(f32)
        kv_grads.append(jnp.sum(parts, axis=1))

    total = lax.psum(jnp.sum(after(lengths, prev)), "dp")
    mean_len = total.astype(f32) / (2 * lax.axis_size("dp"))
    query_grad = pl.pallas_call(
        place_kernel,
        in_specs=[smem_spec()] * 2 + [vmem_spec()] * (2 * SIDE),
        out_specs=vmem_spec(),
        out_shape=jax.ShapeDtypeStruct(five, bf16),
        compiler_params=params(),
    )(place, mean_len.reshape(1), *dq_rows).reshape(2, TOK, SIDE * GROUP, DIM)
    kv_grad = jnp.transpose(jnp.stack(kv_grads, axis=0) * mean_len, (2, 0, 3, 1, 4)).astype(bf16)
    return (query_grad, kv_grad[0], kv_grad[1])


def solution(mesh):
    spec = P("dp", "seq", None, None)
    return jax.shard_map(
        body,
        mesh=mesh,
        in_specs=(spec,) * 5 + (P("dp"), P("dp")),
        out_specs=(spec,) * 3,
        check_vma=False,
    )
```

time: 170 us -> 148 us (0.87)
  starting transfers between devices: 67.8 us -> 43.8 us
  Pallas kernels: 51.6 us -> 67.7 us
  local copies, waits for them, and re-layouts: 9.85 us -> 3.11 us
  waiting for transfers between devices: 24.9 us -> 21 us
    ppermute x36 -> x21, starting transfers between devices: 67.8 us -> 35.4 us  [shift(): return lax.ppermute(value, 'seq', shift_pairs(kind, by % SIDE))]
    pallas_call x7 -> x5, Pallas kernels: 49.7 us -> 65.8 us  [the longest x2 54.7 us: attention(): pl.pallas_call(functools.partial(attention_kernel, seq, shifts, first_cal...]
    all_to_all x0 -> x2, starting transfers between devices: none -> 8.43 us  [body(): parts = lax.all_to_all(prev, 'seq', 0, 0, tiled=True)]
    ppermute x36 -> x21, waiting for transfers between devices: 24.9 us -> 21 us  [shift(): return lax.ppermute(value, 'seq', shift_pairs(kind, by % SIDE))]
    unnamed x80 -> x42, local copies, waits for them, and re-layouts: 4.06 us -> 1.9 us
  transfers between devices with their start and end apart: 36 -> 23, of which waited for: 10 -> 7; matrix products, arithmetic and copies ran while one was open for 3% -> 1% of each run, Pallas kernels for 28% -> 45%
where the time goes in v2:
time: 148 us
  Pallas kernels  67.7 us (46%)
  starting transfers between devices  43.8 us (30%)
  waiting for transfers between devices  21 us (14%)
  blocking collectives  6.41 us (4%)
  local copies, waits for them, and re-layouts  3.11 us (2%)
  other arithmetic  3.1 us (2%)
  between operations  2.36 us (2%)
    pallas_call x2, Pallas kernels, attention(): pl.pallas_call(functools.partial(attention_kernel, seq, shifts, first_cal...  54.7 us
    ppermute x21, starting transfers between devices, shift(): return lax.ppermute(value, 'seq', shift_pairs(kind, by % SIDE))  35.4 us
    ppermute x21, waiting for transfers between devices, shift(): return lax.ppermute(value, 'seq', shift_pairs(kind, by % SIDE))  21 us
    all_to_all x2, starting transfers between devices, body(): parts = lax.all_to_all(prev, 'seq', 0, 0, tiled=True)  8.43 us
    pallas_call x2, Pallas kernels, pack(): pl.pallas_call(pack_kernel, grid=(1,), in_specs=[smem_spec()] + [spec] *...  7.74 us
    psum x1, blocking collectives, body(): total = lax.psum(jnp.sum(after(lengths, prev)), 'dp')  6.41 us
    pallas_call x1, Pallas kernels, body(): pl.pallas_call(place_kernel, in_specs=[smem_spec()] * 2 + [vmem_spec()] *...  3.38 us
  transfers between devices with their start and end apart: 23, of which 7 were waited for; matrix products, arithmetic and copies ran while one was open for 1% of the time, Pallas kernels for 45%

profile of v2, /device:TPU:24, one launch (start us, length us, event | category | flops | bytes accessed | tf_op | source)
XLA Modules:
  0.0 147.5 jit_solution(7401774271437629239)
XLA Ops:
  0.7 1.1 copy_bitcast_fusion
  1.8 0.8 maximum_bitcast_fusion.kv_ref
  2.6 0.6 pad_add_fusion.place.refs_0_
  3.2 1.9 %shard_map.103 = (bf16[2,2,128,128]{3,2,1,0:T(8,128)(2,1)}, bf16[2,2,128,128]{3,2,1,0:T(8,128)(2,1)}, bf16[2,2,128,128]{3,2,1,0:T(8,128)(2,1)}, bf16[2,2,128,128]{3,2,1,0:T(8,128)(2,1)}) custom-call(s32[4]{0:T(128)} %pad_add_fusion.place.refs_0_, bf16[4,2,2,128,128]{4,3,2,1,0:T(8,128)(2,1)} %maximum_bitcast_fusion.kv_ref), custom_call_target="tpu_custom_call" | custom-call | tf_op jit(solution)/shard_map/pallas_call | solution.py:294
  5.1 1.9 %collective-permute-start.3 = (bf16[2,2,128,128]{3,2,1,0:T(8,128)(2,1)}, bf16[2,2,128,128]{3,2,1,0:T(8,128)(2,1)S(1)}, u32[]{:S(2)}, u32[]{:S(2)}) collective-permute-start(bf16[2,2,128,128]{3,2,1,0:T(8,128)(2,1)} %get-tuple-element.38), channel_id=1, source_target_pairs={{0,4},{1,5},{2,6},{3,7},{4,8},{5,9},{6,10},{7,11},{8,12},{9,13},{1... | collective-permute-start | bytes 393224 | tf_op jit(solution)/shard_map/ppermute | solution.py:38
  7.0 3.6 %collective-permute-start.4 = (bf16[2,2,128,128]{3,2,1,0:T(8,128)(2,1)}, bf16[2,2,128,128]{3,2,1,0:T(8,128)(2,1)S(1)}, u32[]{:S(2)}, u32[]{:S(2)}) collective-permute-start(bf16[2,2,128,128]{3,2,1,0:T(8,128)(2,1)} %get-tuple-element.39), channel_id=1, source_target_pairs={{0,8},{1,9},{2,10},{3,11},{4,12},{5,13},{6,14},{7,15},{8,0},{9,1},... | collective-permute-start | bytes 393224 | tf_op jit(solution)/shard_map/ppermute | solution.py:38
  10.6 1.0 collective-permute-start.5
  11.6 3.9 %shard_map.104 = (bf16[2064,128]{1,0:T(8,128)(2,1)}, bf16[2064,128]{1,0:T(8,128)(2,1)}, bf16[2064,128]{1,0:T(8,128)(2,1)}, bf16[2064,128]{1,0:T(8,128)(2,1)}) custom-call(s32[4]{0:T(128)} %pad_add_fusion.place.refs_0_, bf16[2,128,4,8,128]{4,3,2,1,0:T(8,128)(2,1)} %bitcast.28, bf16[2,128,4,8,128]{4,3,2,1,0:T(8,128)(2,1)} %bitcast.30, ...), custom_call_target="tpu_custom_call" | custom-call | tf_op jit(solution)/shard_map/pallas_call | solution.py:82
  15.5 1.3 collective-permute-done.4
  17.0 1.6 %collective-permute-start.6 = (bf16[4,2,128,128]{3,2,1,0:T(8,128)(2,1)S(1)}, bf16[4,2,128,128]{3,2,1,0:T(8,128)(2,1)S(1)}, u32[]{:S(2)}, u32[]{:S(2)}) collective-permute-start(bf16[4,2,128,128]{3,2,1,0:T(8,128)(2,1)S(1)} %pad_maximum_fusion.refs_6_), channel_id=1, source_target_pairs={{0,1},{1,2},{2,3},{3,0},{4,5},{5,6},{6,7},{7,4},{8,9},{9,10},{10,1... | collective-permute-start | bytes 786440 | tf_op jit(solution)/shard_map/ppermute | solution.py:38
  18.5 2.1 %collective-permute-start = (bf16[2064,128]{1,0:T(8,128)(2,1)}, bf16[2064,128]{1,0:T(8,128)(2,1)S(1)}, u32[]{:S(2)}, u32[]{:S(2)}) collective-permute-start(bf16[2064,128]{1,0:T(8,128)(2,1)} %get-tuple-element.42), channel_id=1, source_target_pairs={{0,12},{1,13},{2,14},{3,15},{4,0},{5,1},{6,2},{7,3},{8,4},{9,5},{1... | collective-permute-start | bytes 1585160 | tf_op jit(solution)/shard_map/ppermute | solution.py:38
  20.6 2.2 %collective-permute-start.2 = (bf16[2064,128]{1,0:T(8,128)(2,1)}, bf16[2064,128]{1,0:T(8,128)(2,1)S(1)}, u32[]{:S(2)}, u32[]{:S(2)}) collective-permute-start(bf16[2064,128]{1,0:T(8,128)(2,1)} %get-tuple-element.45), channel_id=1, source_target_pairs={{0,8},{1,9},{2,10},{3,11},{4,12},{5,13},{6,14},{7,15},{8,0},{9,1},... | collective-permute-start | bytes 1585160 | tf_op jit(solution)/shard_map/ppermute | solution.py:38
  22.8 2.7 %collective-permute-start.7 = (bf16[4,2,128,128]{3,2,1,0:T(8,128)(2,1)S(1)}, bf16[4,2,128,128]{3,2,1,0:T(8,128)(2,1)S(1)}, u32[]{:S(2)}, u32[]{:S(2)}) collective-permute-start(bf16[4,2,128,128]{3,2,1,0:T(8,128)(2,1)S(1)} %pad_maximum_fusion.refs_6_), channel_id=1, source_target_pairs={{0,2},{1,3},{2,0},{3,1},{4,6},{5,7},{6,4},{7,5},{8,10},{9,11},{10,... | collective-permute-start | bytes 786440 | tf_op jit(solution)/shard_map/ppermute | solution.py:38
  25.5 0.5 collective-permute-done.6.refs_7_
  26.0 2.5 %collective-permute-start.8 = (bf16[4,2,128,128]{3,2,1,0:T(8,128)(2,1)S(1)}, bf16[4,2,128,128]{3,2,1,0:T(8,128)(2,1)S(1)}, u32[]{:S(2)}, u32[]{:S(2)}) collective-permute-start(bf16[4,2,128,128]{3,2,1,0:T(8,128)(2,1)S(1)} %pad_maximum_fusion.refs_6_), channel_id=1, source_target_pairs={{0,3},{1,0},{2,1},{3,2},{4,7},{5,4},{6,5},{7,6},{8,11},{9,8},{10,9... | collective-permute-start | bytes 786440 | tf_op jit(solution)/shard_map/ppermute | solution.py:38
  28.6 0.0 copy-start.9
  28.6 4.1 %collective-permute-done.7.refs_8_ = bf16[4,2,128,128]{3,2,1,0:T(8,128)(2,1)S(1)} collective-permute-done((bf16[4,2,128,128]{3,2,1,0:T(8,128)(2,1)S(1)}, bf16[4,2,128,128]{3,2,1,0:T(8,128)(2,1)S(1)}, u32[]{:S(2)}, u32[]{:S(2)}) %collective-permute-start.7) | collective-permute-done | bytes 262176 | tf_op jit(solution)/shard_map/ppermute | solution.py:38
  32.7 2.0 %collective-permute-start.12 = (bf16[4,2,128,128]{3,2,1,0:T(8,128)(2,1)S(1)}, bf16[4,2,128,128]{3,2,1,0:T(8,128)(2,1)S(1)}, u32[]{:S(2)}, u32[]{:S(2)}) collective-permute-start(bf16[4,2,128,128]{3,2,1,0:T(8,128)(2,1)S(1)} %pad_maximum_fusion.1.refs_6_), channel_id=1, source_target_pairs={{0,1},{1,2},{2,3},{3,0},{4,5},{5,6},{6,7},{7,4},{8,9},{9,10},{10,1... | collective-permute-start | bytes 786440 | tf_op jit(solution)/shard_map/ppermute | solution.py:38
  34.8 3.8 %shard_map.106 = (bf16[2064,128]{1,0:T(8,128)(2,1)}, bf16[2064,128]{1,0:T(8,128)(2,1)}, bf16[2064,128]{1,0:T(8,128)(2,1)}, bf16[2064,128]{1,0:T(8,128)(2,1)}) custom-call(s32[4]{0:T(128)} %pad_add_fusion.place.refs_0_, bf16[2,128,4,8,128]{4,3,2,1,0:T(8,128)(2,1)} %bitcast.29, bf16[2,128,4,8,128]{4,3,2,1,0:T(8,128)(2,1)} %bitcast.31, ...), custom_call_target="tpu_custom_call" | custom-call | tf_op jit(solution)/shard_map/pallas_call | solution.py:82
  39.3 0.5 convert_divide_fusion.refs_1_
  39.9 1.7 %collective-permute-start.13 = (bf16[4,2,128,128]{3,2,1,0:T(8,128)(2,1)S(1)}, bf16[4,2,128,128]{3,2,1,0:T(8,128)(2,1)}, u32[]{:S(2)}, u32[]{:S(2)}) collective-permute-start(bf16[4,2,128,128]{3,2,1,0:T(8,128)(2,1)S(1)} %pad_maximum_fusion.1.refs_6_), channel_id=1, source_target_pairs={{0,2},{1,3},{2,0},{3,1},{4,6},{5,7},{6,4},{7,5},{8,10},{9,11},{10,... | collective-permute-start | bytes 786440 | tf_op jit(solution)/shard_map/ppermute | solution.py:38
  41.6 1.2 collective-permute-start.14
  42.7 6.0 %collective-permute-done.refs_2_ = bf16[2064,128]{1,0:T(8,128)(2,1)S(1)} collective-permute-done((bf16[2064,128]{1,0:T(8,128)(2,1)}, bf16[2064,128]{1,0:T(8,128)(2,1)S(1)}, u32[]{:S(2)}, u32[]{:S(2)}) %collective-permute-start) | collective-permute-done | bytes 528416 | tf_op jit(solution)/shard_map/ppermute | solution.py:38
  48.7 4.4 %collective-permute-done.1.refs_4_ = bf16[2064,128]{1,0:T(8,128)(2,1)S(1)} collective-permute-done((bf16[2064,128]{1,0:T(8,128)(2,1)}, bf16[2064,128]{1,0:T(8,128)(2,1)S(1)}, u32[]{:S(2)}, u32[]{:S(2)}) %collective-permute-start.1) | collective-permute-done | bytes 528416 | tf_op jit(solution)/shard_map/ppermute | solution.py:38
  53.1 0.2 collective-permute-start.10
  53.3 3.1 %collective-permute-start.11 = (bf16[2064,128]{1,0:T(8,128)(2,1)}, bf16[2064,128]{1,0:T(8,128)(2,1)}, u32[]{:S(2)}, u32[]{:S(2)}) collective-permute-start(bf16[2064,128]{1,0:T(8,128)(2,1)} %get-tuple-element.58), channel_id=1, source_target_pairs={{0,12},{1,13},{2,14},{3,15},{4,0},{5,1},{6,2},{7,3},{8,4},{9,5},{1... | collective-permute-start | bytes 1585160 | tf_op jit(solution)/shard_map/ppermute | solution.py:38
  56.4 27.4 %shard_map.105 = (bf16[1024,128]{1,0:T(8,128)(2,1)}, bf16[1024,128]{1,0:T(8,128)(2,1)}, bf16[1024,128]{1,0:T(8,128)(2,1)}, bf16[1024,128]{1,0:T(8,128)(2,1)}, bf16[16,2,128,128]{3,2,1,0:T(8,128)(2,1)}) custom-call(s32[4]{0:T(128)} %pad_add_fusion.place.refs_0_, f32[2]{0:T(128)} %convert_divide_fusion.refs_1_, bf16[2064,128]{1,0:T(8,128)(2,1)} %copy-done.10, ...), custom_call_target="tpu_custom_call" | custom-call | flops 10737418240 | bytes 8388608 | tf_op jit(solution)/shard_map/pallas_call | solution.py:232
  83.8 3.8 %all-to-all-start = ((bf16[16,2,128,128]{3,2,1,0:T(8,128)(2,1)}), bf16[16,2,128,128]{3,2,1,0:T(8,128)(2,1)S(1)}, u32[]{:S(2)}, u32[]{:S(2)}) async-start(bf16[16,2,128,128]{3,2,1,0:T(8,128)(2,1)} %get-tuple-element.50), calls=%async_computation | async-start | bytes 2097152 | tf_op jit(solution)/shard_map/all_to_all | solution.py:332
  87.6 3.2 %collective-permute-start.15 = (bf16[1024,128]{1,0:T(8,128)(2,1)S(1)}, bf16[1024,128]{1,0:T(8,128)(2,1)S(1)}, u32[]{:S(2)}, u32[]{:S(2)}) collective-permute-start(bf16[1024,128]{1,0:T(8,128)(2,1)S(1)} %copy-done.19), channel_id=1, source_target_pairs={{0,12},{1,13},{2,14},{3,15},{4,0},{5,1},{6,2},{7,3},{8,4},{9,5},{1... | collective-permute-start | bytes 786440 | tf_op jit(solution)/shard_map/ppermute | solution.py:38
  90.8 0.8 collective-permute-start.16
  91.6 0.9 collective-permute-start.17
  92.5 27.3 %shard_map.107 = (bf16[1024,128]{1,0:T(8,128)(2,1)}, bf16[1024,128]{1,0:T(8,128)(2,1)}, bf16[1024,128]{1,0:T(8,128)(2,1)}, bf16[1024,128]{1,0:T(8,128)(2,1)}, bf16[16,2,128,128]{3,2,1,0:T(8,128)(2,1)}) custom-call(s32[4]{0:T(128)} %pad_add_fusion.place.refs_0_, f32[2]{0:T(128)} %convert_divide_fusion.refs_1_, ...), custom_call_target="tpu_custom_call" | custom-call | flops 10737418240 | bytes 8388608 | tf_op jit(solution)/shard_map/pallas_call | solution.py:232
  119.8 0.0 copy-start
  119.9 4.6 %all-to-all-start.1 = ((bf16[16,2,128,128]{3,2,1,0:T(8,128)(2,1)}), bf16[16,2,128,128]{3,2,1,0:T(8,128)(2,1)S(1)}, u32[]{:S(2)}, u32[]{:S(2)}) async-start(bf16[16,2,128,128]{3,2,1,0:T(8,128)(2,1)} %get-tuple-element.65), calls=%async_computation.1 | async-start | bytes 2097152 | tf_op jit(solution)/shard_map/all_to_all | solution.py:332
  124.5 3.1 %collective-permute-start.18 = (bf16[1024,128]{1,0:T(8,128)(2,1)}, bf16[1024,128]{1,0:T(8,128)(2,1)S(1)}, u32[]{:S(2)}, u32[]{:S(2)}) collective-permute-start(bf16[1024,128]{1,0:T(8,128)(2,1)} %get-tuple-element.68), channel_id=1, source_target_pairs={{0,12},{1,13},{2,14},{3,15},{4,0},{5,1},{6,2},{7,3},{8,4},{9,5},{1... | collective-permute-start | bytes 786440 | tf_op jit(solution)/shard_map/ppermute | solution.py:38
  127.7 0.9 collective-permute-start.19
  128.5 0.9 collective-permute-start.20
  129.4 0.6 reduce_sum.27
  130.0 6.4 %psum.7 = s32[]{:T(128)} all-reduce(s32[]{:T(128)} %reduce_sum.27), channel_id=1, replica_groups=mesh['dp'=8,'seq'=16] {'dp'}, use_global_device_ids=true, to_apply=%region_1.2 | all-reduce | flops 1 | bytes 8 | tf_op jit(solution)/shard_map/psum | solution.py:336
  137.1 1.9 %collective-permute-done.18.refs_5_ = bf16[1024,128]{1,0:T(8,128)(2,1)S(1)} collective-permute-done((bf16[1024,128]{1,0:T(8,128)(2,1)}, bf16[1024,128]{1,0:T(8,128)(2,1)S(1)}, u32[]{:S(2)}, u32[]{:S(2)}) %collective-permute-start.18) | collective-permute-done | bytes 262176 | tf_op jit(solution)/shard_map/ppermute | solution.py:38
  138.9 0.0 collective-permute-done.19.refs_6_
  139.0 2.8 %collective-permute-done.20.refs_7_ = bf16[1024,128]{1,0:T(8,128)(2,1)} collective-permute-done((bf16[1024,128]{1,0:T(8,128)(2,1)}, bf16[1024,128]{1,0:T(8,128)(2,1)}, u32[]{:S(2)}, u32[]{:S(2)}) %collective-permute-start.20) | collective-permute-done | bytes 262176 | tf_op jit(solution)/shard_map/ppermute | solution.py:38
  141.8 3.4 %shard_map.108 = bf16[2,128,4,8,128]{4,3,2,1,0:T(8,128)(2,1)} custom-call(s32[4]{0:T(128)} %pad_add_fusion.place.refs_0_, f32[1]{0:T(128)} %bitcast.9.mean_len, bf16[1024,128]{1,0:T(8,128)(2,1)} %get-tuple-element.61.refs_0_, bf16[1024,128]{1,0:T(8,128)(2,1)} %copy-done, bf16[1024,128]{1,0:T(8,128)(2,1)} %copy-done.1, bf16[1024,128]{1,0:T(8,128)(2,1)} %copy-done.2, ...), custom_call_target="tpu_custom_call" | custom-call | tf_op jit(solution)/shard_map/pallas_call | solution.py:338
  145.2 0.2 convert_reduce_fusion.1
  145.4 0.2 convert_reduce_fusion
  145.5 0.1 fusion.1
  145.7 0.9 copy.15
  146.6 0.9 copy.16
  (62 shorter events, 0.3 us)
Async XLA Ops:
  0.6 2.0 %copy-start.8 = (s32[2]{0:T(128)S(1)}, s32[2]{0:T(128)}, u32[]{:S(2)}) copy-start(s32[2]{0:T(128)} %param.13) | copy-start | bytes 28
  5.1 10.4 %collective-permute-start.3 = (bf16[2,2,128,128]{3,2,1,0:T(8,128)(2,1)}, bf16[2,2,128,128]{3,2,1,0:T(8,128)(2,1)S(1)}, u32[]{:S(2)}, u32[]{:S(2)}) collective-permute-start(bf16[2,2,128,128]{3,2,1,0:T(8,128)(2,1)} %get-tuple-element.38), channel_id=1, source_target_pairs={{0,4},{1,5},{2,6},{3,7},{4,8},{5,9},{6,10},{7,11},{8,12},{9,13},{1... | collective-permute-start | bytes 393224 | tf_op jit(solution)/shard_map/ppermute | solution.py:38
  7.0 9.8 %collective-permute-start.4 = (bf16[2,2,128,128]{3,2,1,0:T(8,128)(2,1)}, bf16[2,2,128,128]{3,2,1,0:T(8,128)(2,1)S(1)}, u32[]{:S(2)}, u32[]{:S(2)}) collective-permute-start(bf16[2,2,128,128]{3,2,1,0:T(8,128)(2,1)} %get-tuple-element.39), channel_id=1, source_target_pairs={{0,8},{1,9},{2,10},{3,11},{4,12},{5,13},{6,14},{7,15},{8,0},{9,1},... | collective-permute-start | bytes 393224 | tf_op jit(solution)/shard_map/ppermute | solution.py:38
  10.6 6.2 %collective-permute-start.5 = (bf16[2,2,128,128]{3,2,1,0:T(8,128)(2,1)}, bf16[2,2,128,128]{3,2,1,0:T(8,128)(2,1)S(1)}, u32[]{:S(2)}, u32[]{:S(2)}) collective-permute-start(bf16[2,2,128,128]{3,2,1,0:T(8,128)(2,1)} %get-tuple-element.40), channel_id=1, source_target_pairs={{0,12},{1,13},{2,14},{3,15},{4,0},{5,1},{6,2},{7,3},{8,4},{9,5},{1... | collective-permute-start | bytes 393224 | tf_op jit(solution)/shard_map/ppermute | solution.py:38
  11.6 5.3 %copy-start.7 = (bf16[2,2,128,128]{3,2,1,0:T(8,128)(2,1)S(1)}, bf16[2,2,128,128]{3,2,1,0:T(8,128)(2,1)}, u32[]{:S(2)}) copy-start(bf16[2,2,128,128]{3,2,1,0:T(8,128)(2,1)} %get-tuple-element.46) | copy-start | bytes 393220
  17.0 21.6 %copy-start.6 = (bf16[4,2,128,128]{3,2,1,0:T(8,128)(2,1)}, bf16[4,2,128,128]{3,2,1,0:T(8,128)(2,1)S(1)}, u32[]{:S(2)}) copy-start(bf16[4,2,128,128]{3,2,1,0:T(8,128)(2,1)S(1)} %pad_maximum_fusion.refs_6_) | copy-start | bytes 786436
  17.0 9.1 %collective-permute-start.6 = (bf16[4,2,128,128]{3,2,1,0:T(8,128)(2,1)S(1)}, bf16[4,2,128,128]{3,2,1,0:T(8,128)(2,1)S(1)}, u32[]{:S(2)}, u32[]{:S(2)}) collective-permute-start(bf16[4,2,128,128]{3,2,1,0:T(8,128)(2,1)S(1)} %pad_maximum_fusion.refs_6_), channel_id=1, source_target_pairs={{0,1},{1,2},{2,3},{3,0},{4,5},{5,6},{6,7},{7,4},{8,9},{9,10},{10,1... | collective-permute-start | bytes 786440 | tf_op jit(solution)/shard_map/ppermute | solution.py:38
  18.5 30.2 %collective-permute-start = (bf16[2064,128]{1,0:T(8,128)(2,1)}, bf16[2064,128]{1,0:T(8,128)(2,1)S(1)}, u32[]{:S(2)}, u32[]{:S(2)}) collective-permute-start(bf16[2064,128]{1,0:T(8,128)(2,1)} %get-tuple-element.42), channel_id=1, source_target_pairs={{0,12},{1,13},{2,14},{3,15},{4,0},{5,1},{6,2},{7,3},{8,4},{9,5},{1... | collective-permute-start | bytes 1585160 | tf_op jit(solution)/shard_map/ppermute | solution.py:38
  20.6 32.5 %collective-permute-start.1 = (bf16[2064,128]{1,0:T(8,128)(2,1)}, bf16[2064,128]{1,0:T(8,128)(2,1)S(1)}, u32[]{:S(2)}, u32[]{:S(2)}) collective-permute-start(bf16[2064,128]{1,0:T(8,128)(2,1)} %get-tuple-element.44), channel_id=1, source_target_pairs={{0,4},{1,5},{2,6},{3,7},{4,8},{5,9},{6,10},{7,11},{8,12},{9,13},{1... | collective-permute-start | bytes 1585160 | tf_op jit(solution)/shard_map/ppermute | solution.py:38
  20.6 32.7 %collective-permute-start.2 = (bf16[2064,128]{1,0:T(8,128)(2,1)}, bf16[2064,128]{1,0:T(8,128)(2,1)S(1)}, u32[]{:S(2)}, u32[]{:S(2)}) collective-permute-start(bf16[2064,128]{1,0:T(8,128)(2,1)} %get-tuple-element.45), channel_id=1, source_target_pairs={{0,8},{1,9},{2,10},{3,11},{4,12},{5,13},{6,14},{7,15},{8,0},{9,1},... | collective-permute-start | bytes 1585160 | tf_op jit(solution)/shard_map/ppermute | solution.py:38
  22.8 9.9 %collective-permute-start.7 = (bf16[4,2,128,128]{3,2,1,0:T(8,128)(2,1)S(1)}, bf16[4,2,128,128]{3,2,1,0:T(8,128)(2,1)S(1)}, u32[]{:S(2)}, u32[]{:S(2)}) collective-permute-start(bf16[4,2,128,128]{3,2,1,0:T(8,128)(2,1)S(1)} %pad_maximum_fusion.refs_6_), channel_id=1, source_target_pairs={{0,2},{1,3},{2,0},{3,1},{4,6},{5,7},{6,4},{7,5},{8,10},{9,11},{10,... | collective-permute-start | bytes 786440 | tf_op jit(solution)/shard_map/ppermute | solution.py:38
  26.0 12.6 %copy-start.14 = (bf16[4,2,128,128]{3,2,1,0:T(8,128)(2,1)}, bf16[4,2,128,128]{3,2,1,0:T(8,128)(2,1)S(1)}, u32[]{:S(2)}) copy-start(bf16[4,2,128,128]{3,2,1,0:T(8,128)(2,1)S(1)} %collective-permute-done.6.refs_7_) | copy-start | bytes 786436
  26.0 13.8 %collective-permute-start.8 = (bf16[4,2,128,128]{3,2,1,0:T(8,128)(2,1)S(1)}, bf16[4,2,128,128]{3,2,1,0:T(8,128)(2,1)S(1)}, u32[]{:S(2)}, u32[]{:S(2)}) collective-permute-start(bf16[4,2,128,128]{3,2,1,0:T(8,128)(2,1)S(1)} %pad_maximum_fusion.refs_6_), channel_id=1, source_target_pairs={{0,3},{1,0},{2,1},{3,2},{4,7},{5,4},{6,5},{7,6},{8,11},{9,8},{10,9... | collective-permute-start | bytes 786440 | tf_op jit(solution)/shard_map/ppermute | solution.py:38
  28.6 12.9 %copy-start.5 = (bf16[4,2,128,128]{3,2,1,0:T(8,128)(2,1)}, bf16[4,2,128,128]{3,2,1,0:T(8,128)(2,1)S(1)}, u32[]{:S(2)}) copy-start(bf16[4,2,128,128]{3,2,1,0:T(8,128)(2,1)S(1)} %pad_maximum_fusion.1.refs_6_) | copy-start | bytes 786436
  28.6 10.7 %copy-start.9 = (f32[2]{0:T(128)S(1)}, f32[2]{0:T(128)}, u32[]{:S(2)}) copy-start(f32[2]{0:T(128)} %constant.42.clone) | copy-start | bytes 28
  32.7 5.9 %copy-start.15 = (bf16[4,2,128,128]{3,2,1,0:T(8,128)(2,1)}, bf16[4,2,128,128]{3,2,1,0:T(8,128)(2,1)S(1)}, u32[]{:S(2)}) copy-start(bf16[4,2,128,128]{3,2,1,0:T(8,128)(2,1)S(1)} %collective-permute-done.7.refs_8_) | copy-start | bytes 786436
  32.7 8.8 %collective-permute-start.12 = (bf16[4,2,128,128]{3,2,1,0:T(8,128)(2,1)S(1)}, bf16[4,2,128,128]{3,2,1,0:T(8,128)(2,1)S(1)}, u32[]{:S(2)}, u32[]{:S(2)}) collective-permute-start(bf16[4,2,128,128]{3,2,1,0:T(8,128)(2,1)S(1)} %pad_maximum_fusion.1.refs_6_), channel_id=1, source_target_pairs={{0,1},{1,2},{2,3},{3,0},{4,5},{5,6},{6,7},{7,4},{8,9},{9,10},{10,1... | collective-permute-start | bytes 786440 | tf_op jit(solution)/shard_map/ppermute | solution.py:38
  39.9 16.5 %copy-start.16 = (bf16[4,2,128,128]{3,2,1,0:T(8,128)(2,1)}, bf16[4,2,128,128]{3,2,1,0:T(8,128)(2,1)S(1)}, u32[]{:S(2)}) copy-start(bf16[4,2,128,128]{3,2,1,0:T(8,128)(2,1)S(1)} %collective-permute-done.8.refs_9_) | copy-start | bytes 786436
  39.9 47.7 %collective-permute-start.13 = (bf16[4,2,128,128]{3,2,1,0:T(8,128)(2,1)S(1)}, bf16[4,2,128,128]{3,2,1,0:T(8,128)(2,1)}, u32[]{:S(2)}, u32[]{:S(2)}) collective-permute-start(bf16[4,2,128,128]{3,2,1,0:T(8,128)(2,1)S(1)} %pad_maximum_fusion.1.refs_6_), channel_id=1, source_target_pairs={{0,2},{1,3},{2,0},{3,1},{4,6},{5,7},{6,4},{7,5},{8,10},{9,11},{10,... | collective-permute-start | bytes 786440 | tf_op jit(solution)/shard_map/ppermute | solution.py:38
  41.5 42.2 %copy-start.13 = (bf16[4,2,128,128]{3,2,1,0:T(8,128)(2,1)}, bf16[4,2,128,128]{3,2,1,0:T(8,128)(2,1)S(1)}, u32[]{:S(2)}) copy-start(bf16[4,2,128,128]{3,2,1,0:T(8,128)(2,1)S(1)} %collective-permute-done.12.refs_7_) | copy-start | bytes 786436
  41.6 49.2 %collective-permute-start.14 = (bf16[4,2,128,128]{3,2,1,0:T(8,128)(2,1)S(1)}, bf16[4,2,128,128]{3,2,1,0:T(8,128)(2,1)}, u32[]{:S(2)}, u32[]{:S(2)}) collective-permute-start(bf16[4,2,128,128]{3,2,1,0:T(8,128)(2,1)S(1)} %pad_maximum_fusion.1.refs_6_), channel_id=1, source_target_pairs={{0,3},{1,0},{2,1},{3,2},{4,7},{5,4},{6,5},{7,6},{8,11},{9,8},{10,9... | collective-permute-start | bytes 786440 | tf_op jit(solution)/shard_map/ppermute | solution.py:38
  48.7 7.7 %copy-start.10 = (bf16[2064,128]{1,0:T(8,128)(2,1)}, bf16[2064,128]{1,0:T(8,128)(2,1)S(1)}, u32[]{:S(2)}) copy-start(bf16[2064,128]{1,0:T(8,128)(2,1)S(1)} %collective-permute-done.refs_2_) | copy-start | bytes 1585156
  48.7 42.9 %collective-permute-start.9 = (bf16[2064,128]{1,0:T(8,128)(2,1)}, bf16[2064,128]{1,0:T(8,128)(2,1)}, u32[]{:S(2)}, u32[]{:S(2)}) collective-permute-start(bf16[2064,128]{1,0:T(8,128)(2,1)} %get-tuple-element.56), channel_id=1, source_target_pairs={{0,8},{1,9},{2,10},{3,11},{4,12},{5,13},{6,14},{7,15},{8,0},{9,1},... | collective-permute-start | bytes 1585160 | tf_op jit(solution)/shard_map/ppermute | solution.py:38
  53.1 3.3 %copy-start.11 = (bf16[2064,128]{1,0:T(8,128)(2,1)}, bf16[2064,128]{1,0:T(8,128)(2,1)S(1)}, u32[]{:S(2)}) copy-start(bf16[2064,128]{1,0:T(8,128)(2,1)S(1)} %collective-permute-done.1.refs_4_) | copy-start | bytes 1585156
  53.1 39.4 %collective-permute-start.10 = (bf16[2064,128]{1,0:T(8,128)(2,1)}, bf16[2064,128]{1,0:T(8,128)(2,1)}, u32[]{:S(2)}, u32[]{:S(2)}) collective-permute-start(bf16[2064,128]{1,0:T(8,128)(2,1)} %get-tuple-element.57), channel_id=1, source_target_pairs={{0,4},{1,5},{2,6},{3,7},{4,8},{5,9},{6,10},{7,11},{8,12},{9,13},{1... | collective-permute-start | bytes 1585160 | tf_op jit(solution)/shard_map/ppermute | solution.py:38
  53.3 3.1 %copy-start.12 = (bf16[2064,128]{1,0:T(8,128)(2,1)}, bf16[2064,128]{1,0:T(8,128)(2,1)S(1)}, u32[]{:S(2)}) copy-start(bf16[2064,128]{1,0:T(8,128)(2,1)S(1)} %collective-permute-done.2.refs_5_) | copy-start | bytes 1585156
  53.3 39.2 %collective-permute-start.11 = (bf16[2064,128]{1,0:T(8,128)(2,1)}, bf16[2064,128]{1,0:T(8,128)(2,1)}, u32[]{:S(2)}, u32[]{:S(2)}) collective-permute-start(bf16[2064,128]{1,0:T(8,128)(2,1)} %get-tuple-element.58), channel_id=1, source_target_pairs={{0,12},{1,13},{2,14},{3,15},{4,0},{5,1},{6,2},{7,3},{8,4},{9,5},{1... | collective-permute-start | bytes 1585160 | tf_op jit(solution)/shard_map/ppermute | solution.py:38
  83.8 3.8 %copy-start.19 = (bf16[1024,128]{1,0:T(8,128)(2,1)S(1)}, bf16[1024,128]{1,0:T(8,128)(2,1)}, u32[]{:S(2)}) copy-start(bf16[1024,128]{1,0:T(8,128)(2,1)} %get-tuple-element.62) | copy-start | bytes 786436
  83.8 7.0 %copy-start.18 = (bf16[1024,128]{1,0:T(8,128)(2,1)S(1)}, bf16[1024,128]{1,0:T(8,128)(2,1)}, u32[]{:S(2)}) copy-start(bf16[1024,128]{1,0:T(8,128)(2,1)} %get-tuple-element.63) | copy-start | bytes 786436
  83.8 7.8 %copy-start.17 = (bf16[1024,128]{1,0:T(8,128)(2,1)S(1)}, bf16[1024,128]{1,0:T(8,128)(2,1)}, u32[]{:S(2)}) copy-start(bf16[1024,128]{1,0:T(8,128)(2,1)} %get-tuple-element.64) | copy-start | bytes 786436
  83.8 36.1 %all-to-all-start = ((bf16[16,2,128,128]{3,2,1,0:T(8,128)(2,1)}), bf16[16,2,128,128]{3,2,1,0:T(8,128)(2,1)S(1)}, u32[]{:S(2)}, u32[]{:S(2)}) async-start(bf16[16,2,128,128]{3,2,1,0:T(8,128)(2,1)} %get-tuple-element.50), calls=%async_computation | async-start | bytes 2097152 | tf_op jit(solution)/shard_map/all_to_all | solution.py:332
  87.6 32.2 %collective-permute-start.15 = (bf16[1024,128]{1,0:T(8,128)(2,1)S(1)}, bf16[1024,128]{1,0:T(8,128)(2,1)S(1)}, u32[]{:S(2)}, u32[]{:S(2)}) collective-permute-start(bf16[1024,128]{1,0:T(8,128)(2,1)S(1)} %copy-done.19), channel_id=1, source_target_pairs={{0,12},{1,13},{2,14},{3,15},{4,0},{5,1},{6,2},{7,3},{8,4},{9,5},{1... | collective-permute-start | bytes 786440 | tf_op jit(solution)/shard_map/ppermute | solution.py:38
  90.8 29.1 %collective-permute-start.16 = (bf16[1024,128]{1,0:T(8,128)(2,1)S(1)}, bf16[1024,128]{1,0:T(8,128)(2,1)S(1)}, u32[]{:S(2)}, u32[]{:S(2)}) collective-permute-start(bf16[1024,128]{1,0:T(8,128)(2,1)S(1)} %copy-done.18), channel_id=1, source_target_pairs={{0,8},{1,9},{2,10},{3,11},{4,12},{5,13},{6,14},{7,15},{8,0},{9,1},... | collective-permute-start | bytes 786440 | tf_op jit(solution)/shard_map/ppermute | solution.py:38
  91.6 28.3 %collective-permute-start.17 = (bf16[1024,128]{1,0:T(8,128)(2,1)S(1)}, bf16[1024,128]{1,0:T(8,128)(2,1)S(1)}, u32[]{:S(2)}, u32[]{:S(2)}) collective-permute-start(bf16[1024,128]{1,0:T(8,128)(2,1)S(1)} %copy-done.17), channel_id=1, source_target_pairs={{0,4},{1,5},{2,6},{3,7},{4,8},{5,9},{6,10},{7,11},{8,12},{9,13},{1... | collective-permute-start | bytes 786440 | tf_op jit(solution)/shard_map/ppermute | solution.py:38
  119.8 21.9 %copy-start = (bf16[1024,128]{1,0:T(8,128)(2,1)}, bf16[1024,128]{1,0:T(8,128)(2,1)S(1)}, u32[]{:S(2)}) copy-start(bf16[1024,128]{1,0:T(8,128)(2,1)S(1)} %collective-permute-done.15.refs_1_) | copy-start | bytes 786436
  119.9 21.9 %copy-start.1 = (bf16[1024,128]{1,0:T(8,128)(2,1)}, bf16[1024,128]{1,0:T(8,128)(2,1)S(1)}, u32[]{:S(2)}) copy-start(bf16[1024,128]{1,0:T(8,128)(2,1)S(1)} %collective-permute-done.16.refs_2_) | copy-start | bytes 786436
  119.9 21.9 %copy-start.2 = (bf16[1024,128]{1,0:T(8,128)(2,1)}, bf16[1024,128]{1,0:T(8,128)(2,1)S(1)}, u32[]{:S(2)}) copy-start(bf16[1024,128]{1,0:T(8,128)(2,1)S(1)} %collective-permute-done.17.refs_3_) | copy-start | bytes 786436
  119.9 25.4 %all-to-all-start.1 = ((bf16[16,2,128,128]{3,2,1,0:T(8,128)(2,1)}), bf16[16,2,128,128]{3,2,1,0:T(8,128)(2,1)S(1)}, u32[]{:S(2)}, u32[]{:S(2)}) async-start(bf16[16,2,128,128]{3,2,1,0:T(8,128)(2,1)} %get-tuple-element.65), calls=%async_computation.1 | async-start | bytes 2097152 | tf_op jit(solution)/shard_map/all_to_all | solution.py:332
  124.5 14.4 %collective-permute-start.18 = (bf16[1024,128]{1,0:T(8,128)(2,1)}, bf16[1024,128]{1,0:T(8,128)(2,1)S(1)}, u32[]{:S(2)}, u32[]{:S(2)}) collective-permute-start(bf16[1024,128]{1,0:T(8,128)(2,1)} %get-tuple-element.68), channel_id=1, source_target_pairs={{0,12},{1,13},{2,14},{3,15},{4,0},{5,1},{6,2},{7,3},{8,4},{9,5},{1... | collective-permute-start | bytes 786440 | tf_op jit(solution)/shard_map/ppermute | solution.py:38
  127.7 11.3 %collective-permute-start.19 = (bf16[1024,128]{1,0:T(8,128)(2,1)}, bf16[1024,128]{1,0:T(8,128)(2,1)S(1)}, u32[]{:S(2)}, u32[]{:S(2)}) collective-permute-start(bf16[1024,128]{1,0:T(8,128)(2,1)} %get-tuple-element.69), channel_id=1, source_target_pairs={{0,8},{1,9},{2,10},{3,11},{4,12},{5,13},{6,14},{7,15},{8,0},{9,1},... | collective-permute-start | bytes 786440 | tf_op jit(solution)/shard_map/ppermute | solution.py:38
  128.5 13.2 %collective-permute-start.20 = (bf16[1024,128]{1,0:T(8,128)(2,1)}, bf16[1024,128]{1,0:T(8,128)(2,1)}, u32[]{:S(2)}, u32[]{:S(2)}) collective-permute-start(bf16[1024,128]{1,0:T(8,128)(2,1)} %get-tuple-element.70), channel_id=1, source_target_pairs={{0,4},{1,5},{2,6},{3,7},{4,8},{5,9},{6,10},{7,11},{8,12},{9,13},{1... | collective-permute-start | bytes 786440 | tf_op jit(solution)/shard_map/ppermute | solution.py:38
  138.9 2.8 %copy-start.3 = (bf16[1024,128]{1,0:T(8,128)(2,1)}, bf16[1024,128]{1,0:T(8,128)(2,1)S(1)}, u32[]{:S(2)}) copy-start(bf16[1024,128]{1,0:T(8,128)(2,1)S(1)} %collective-permute-done.18.refs_5_) | copy-start | bytes 786436
  139.0 2.8 %copy-start.4 = (bf16[1024,128]{1,0:T(8,128)(2,1)}, bf16[1024,128]{1,0:T(8,128)(2,1)S(1)}, u32[]{:S(2)}) copy-start(bf16[1024,128]{1,0:T(8,128)(2,1)S(1)} %collective-permute-done.19.refs_6_) | copy-start | bytes 786436

commit v3 on v2

--- a/solution.py
+++ b/solution.py
@@ -110,7 +110,7 @@
     else:
         dka, dva = refs[:2]
         refs = refs[2:]
-    pk, k_s, v_s, kt_s, p_s, m_s, gm_s, dqt_s, dq_s, sem_p, sem_kv, sem_o = refs
+    pk, k_s, v_s, kt_s, p_s, m_s, gm_s, dqt_s, stat, dq_s, sem_p, sem_kv, sem_o = refs
     z, x, length = meta[0], meta[1], meta[2 + seq]
     copies = []
     for e in range(SIDE):
@@ -128,7 +128,7 @@
     else:
         dka[...] = acc_in[0][...]
         dva[...] = acc_in[1][...]
-    for copy in copies:
+    for copy in copies[:2 * SIDE * SIDE]:
         copy.wait()
     kt_s[...] = k_s[...].reshape(FULL, DIM).T
     factor = coef[seq]
@@ -139,6 +139,7 @@
         for n in range(1, count):
             block = jnp.where(d == n, along[n], block)
         first = block * TOK
+        pltpu.make_async_copy(pk.at[d], pk.at[d], sem_p.at[d]).wait()
 
         @pl.when(first >= length)
         def _():
@@ -155,50 +156,69 @@
             delta = jnp.where(lane_token < length, delta, 0.0)
             steps = (first + TOK + CHUNK - 1) // CHUNK
 
-            def blocks(c):
-                return pl.ds(c * (CHUNK // TOK), CHUNK // TOK)
-
-            def scores_step(c, carry, masked):
+            per = CHUNK // TOK
+            rest = lax.rem(block, per) + 1
+
+            def scores_step(c, width, carry, masked):
                 top, total = carry
                 k0 = pl.multiple_of(c * CHUNK, CHUNK)
                 s = lax.dot_general(
-                    k_s[blocks(c)].reshape(CHUNK, DIM),
+                    k_s[pl.ds(c * per, width)].reshape(width * TOK, DIM),
                     pk[d, 0:ROWS, :],
                     NT,
                     preferred_element_type=f32,
                 )
                 if masked:
-                    key = lax.broadcasted_iota(jnp.int32, (CHUNK, ROWS), 0) + k0
+                    key = lax.broadcasted_iota(jnp.int32, (width * TOK, ROWS), 0) + k0
                     s = jnp.where(key <= lane_token, s, -jnp.inf)
                 new = jnp.maximum(top, jnp.max(s, axis=0, keepdims=True))
                 p = jnp.exp2((s - new) * EXP2)
-                p_s[pl.ds(k0, CHUNK), :] = p
+                p_s[pl.ds(k0, width * TOK), :] = p
                 m_s[c] = jnp.broadcast_to(new, (8, ROWS))
                 total = total * jnp.exp2((top - new) * EXP2) + jnp.sum(p, axis=0, keepdims=True)
                 return new, total
 
             carry = (jnp.full((1, ROWS), -1e30, f32), jnp.zeros((1, ROWS), f32))
-            carry = lax.fori_loop(0, steps - 1, lambda c, x: scores_step(c, x, False), carry)
-            top, total = scores_step(steps - 1, carry, True)
+            carry = lax.fori_loop(
+                0, steps - 1, lambda c, held: scores_step(c, per, held, False), carry
+            )
+            for width in range(1, per + 1):
+
+                @pl.when(rest == width)
+                def _():
+                    row_top, row_total = scores_step(steps - 1, width, carry, True)
+                    stat[0:1, :] = row_top
+                    stat[8:9, :] = row_total
+
+            top, total = stat[0:1, :], stat[8:9, :]
             inverse = 1.0 / total
             dqt_s[...] = jnp.zeros_like(dqt_s)
 
-            def grads_step(c, _):
+            def grads_step(c, width):
                 k0 = pl.multiple_of(c * CHUNK, CHUNK)
-                at = pl.ds(k0, CHUNK)
+                at = pl.ds(k0, width * TOK)
                 g = gm_s[...]
                 weight = jnp.exp2((m_s[c][0:1] - top) * EXP2) * inverse
                 dp = lax.dot_general(
-                    v_s[blocks(c)].reshape(CHUNK, DIM), g, NT, preferred_element_type=f32
+                    v_s[pl.ds(c * per, width)].reshape(width * TOK, DIM), g, NT, preferred_element_type=f32
                 )
                 prob = p_s[at, :] * weight
                 ds = (prob * (dp - delta)).astype(bf16)
                 dva[at, :] += lax.dot_general(prob.astype(bf16), g, NN, preferred_element_type=f32)
                 dka[at, :] += lax.dot_general(ds, pk[d, 0:ROWS, :], NN, preferred_element_type=f32)
                 dqt_s[...] += lax.dot_general(kt_s[:, at], ds, NN, preferred_element_type=f32)
+
+            def full_step(c, _):
+                grads_step(c, per)
                 return 0
 
-            lax.fori_loop(0, steps, grads_step, 0)
+            lax.fori_loop(0, steps - 1, full_step, 0)
+            for width in range(1, per + 1):
+
+                @pl.when(rest == width)
+                def _():
+                    grads_step(steps - 1, width)
+
             dq_s[d] = (dqt_s[...].T * (factor * SCALE)).astype(bf16)
 
         return 0
@@ -246,6 +266,7 @@
             pltpu.VMEM((FULL // CHUNK, 8, ROWS), f32),
             pltpu.VMEM((ROWS, DIM), bf16),
             pltpu.VMEM((DIM, ROWS), f32),
+            pltpu.VMEM((16, ROWS), f32),
             pltpu.VMEM((count, ROWS, DIM), bf16),
             pltpu.SemaphoreType.DMA((count,)),
             pltpu.SemaphoreType.DMA((2, SIDE * SIDE)),

time: 148 us -> 140 us (0.946); the launches traced: 148 us -> 142 us
  Pallas kernels: 67.7 us -> 56.7 us
  starting transfers between devices: 43.8 us -> 49 us
    pallas_call x2, Pallas kernels: 54.7 us -> 43.7 us  [attention(): pl.pallas_call(functools.partial(attention_kernel, seq, shifts, first_cal...]
    all_to_all x2, starting transfers between devices: 8.43 us -> 13.6 us  [body(): parts = lax.all_to_all(prev, 'seq', 0, 0, tiled=True)]
  transfers between devices with their start and end apart: 23 -> 23, of which waited for: 7 -> 7; matrix products, arithmetic and copies ran while one was open for 1% -> 1% of each run, Pallas kernels for 45% -> 39%
where the time goes in v3:
time: 140 us; the launch traced here: 142 us
  Pallas kernels  56.7 us (40%)
  starting transfers between devices  49 us (35%)
  waiting for transfers between devices  21 us (15%)
  blocking collectives  6.41 us (5%)
  local copies, waits for them, and re-layouts  3.11 us (2%)
  other arithmetic  3.1 us (2%)
  between operations  2.36 us (2%)
    pallas_call x2, Pallas kernels, attention(): pl.pallas_call(functools.partial(attention_kernel, seq, shifts, first_cal...  43.7 us
    ppermute x21, starting transfers between devices, shift(): return lax.ppermute(value, 'seq', shift_pairs(kind, by % SIDE))  35.4 us
    ppermute x21, waiting for transfers between devices, shift(): return lax.ppermute(value, 'seq', shift_pairs(kind, by % SIDE))  21 us
    all_to_all x2, starting transfers between devices, body(): parts = lax.all_to_all(prev, 'seq', 0, 0, tiled=True)  13.6 us
    pallas_call x2, Pallas kernels, pack(): pl.pallas_call(pack_kernel, grid=(1,), in_specs=[smem_spec()] + [spec] *...  7.74 us
    psum x1, blocking collectives, body(): total = lax.psum(jnp.sum(after(lengths, prev)), 'dp')  6.41 us
    pallas_call x1, Pallas kernels, body(): pl.pallas_call(place_kernel, in_specs=[smem_spec()] * 2 + [vmem_spec()] *...  3.38 us
  transfers between devices with their start and end apart: 23, of which 7 were waited for; matrix products, arithmetic and copies ran while one was open for 1% of the time, Pallas kernels for 39%

profile of v3, /device:TPU:24, one launch (start us, length us, event | category | flops | bytes accessed | tf_op | source)
XLA Modules:
  0.0 141.7 jit_solution(10430692614576337402)
XLA Ops:
  0.7 1.1 copy_bitcast_fusion
  1.8 0.8 maximum_bitcast_fusion.kv_ref
  2.6 0.6 pad_add_fusion.place.refs_0_
  3.2 1.9 %shard_map.103 = (bf16[2,2,128,128]{3,2,1,0:T(8,128)(2,1)}, bf16[2,2,128,128]{3,2,1,0:T(8,128)(2,1)}, bf16[2,2,128,128]{3,2,1,0:T(8,128)(2,1)}, bf16[2,2,128,128]{3,2,1,0:T(8,128)(2,1)}) custom-call(s32[4]{0:T(128)} %pad_add_fusion.place.refs_0_, bf16[4,2,2,128,128]{4,3,2,1,0:T(8,128)(2,1)} %maximum_bitcast_fusion.kv_ref), custom_call_target="tpu_custom_call" | custom-call | tf_op jit(solution)/shard_map/pallas_call | solution.py:315
  5.1 1.9 %collective-permute-start.3 = (bf16[2,2,128,128]{3,2,1,0:T(8,128)(2,1)}, bf16[2,2,128,128]{3,2,1,0:T(8,128)(2,1)S(1)}, u32[]{:S(2)}, u32[]{:S(2)}) collective-permute-start(bf16[2,2,128,128]{3,2,1,0:T(8,128)(2,1)} %get-tuple-element.38), channel_id=1, source_target_pairs={{0,4},{1,5},{2,6},{3,7},{4,8},{5,9},{6,10},{7,11},{8,12},{9,13},{1... | collective-permute-start | bytes 393224 | tf_op jit(solution)/shard_map/ppermute | solution.py:38
  7.0 3.6 %collective-permute-start.4 = (bf16[2,2,128,128]{3,2,1,0:T(8,128)(2,1)}, bf16[2,2,128,128]{3,2,1,0:T(8,128)(2,1)S(1)}, u32[]{:S(2)}, u32[]{:S(2)}) collective-permute-start(bf16[2,2,128,128]{3,2,1,0:T(8,128)(2,1)} %get-tuple-element.39), channel_id=1, source_target_pairs={{0,8},{1,9},{2,10},{3,11},{4,12},{5,13},{6,14},{7,15},{8,0},{9,1},... | collective-permute-start | bytes 393224 | tf_op jit(solution)/shard_map/ppermute | solution.py:38
  10.6 1.0 collective-permute-start.5
  11.6 3.9 %shard_map.104 = (bf16[2064,128]{1,0:T(8,128)(2,1)}, bf16[2064,128]{1,0:T(8,128)(2,1)}, bf16[2064,128]{1,0:T(8,128)(2,1)}, bf16[2064,128]{1,0:T(8,128)(2,1)}) custom-call(s32[4]{0:T(128)} %pad_add_fusion.place.refs_0_, bf16[2,128,4,8,128]{4,3,2,1,0:T(8,128)(2,1)} %bitcast.28, bf16[2,128,4,8,128]{4,3,2,1,0:T(8,128)(2,1)} %bitcast.30, ...), custom_call_target="tpu_custom_call" | custom-call | tf_op jit(solution)/shard_map/pallas_call | solution.py:82
  15.5 1.3 collective-permute-done.4
  17.0 1.6 %collective-permute-start.6 = (bf16[4,2,128,128]{3,2,1,0:T(8,128)(2,1)S(1)}, bf16[4,2,128,128]{3,2,1,0:T(8,128)(2,1)S(1)}, u32[]{:S(2)}, u32[]{:S(2)}) collective-permute-start(bf16[4,2,128,128]{3,2,1,0:T(8,128)(2,1)S(1)} %pad_maximum_fusion.refs_6_), channel_id=1, source_target_pairs={{0,1},{1,2},{2,3},{3,0},{4,5},{5,6},{6,7},{7,4},{8,9},{9,10},{10,1... | collective-permute-start | bytes 786440 | tf_op jit(solution)/shard_map/ppermute | solution.py:38
  18.5 2.1 %collective-permute-start = (bf16[2064,128]{1,0:T(8,128)(2,1)}, bf16[2064,128]{1,0:T(8,128)(2,1)S(1)}, u32[]{:S(2)}, u32[]{:S(2)}) collective-permute-start(bf16[2064,128]{1,0:T(8,128)(2,1)} %get-tuple-element.42), channel_id=1, source_target_pairs={{0,12},{1,13},{2,14},{3,15},{4,0},{5,1},{6,2},{7,3},{8,4},{9,5},{1... | collective-permute-start | bytes 1585160 | tf_op jit(solution)/shard_map/ppermute | solution.py:38
  20.6 2.2 %collective-permute-start.2 = (bf16[2064,128]{1,0:T(8,128)(2,1)}, bf16[2064,128]{1,0:T(8,128)(2,1)S(1)}, u32[]{:S(2)}, u32[]{:S(2)}) collective-permute-start(bf16[2064,128]{1,0:T(8,128)(2,1)} %get-tuple-element.45), channel_id=1, source_target_pairs={{0,8},{1,9},{2,10},{3,11},{4,12},{5,13},{6,14},{7,15},{8,0},{9,1},... | collective-permute-start | bytes 1585160 | tf_op jit(solution)/shard_map/ppermute | solution.py:38
  22.8 2.7 %collective-permute-start.7 = (bf16[4,2,128,128]{3,2,1,0:T(8,128)(2,1)S(1)}, bf16[4,2,128,128]{3,2,1,0:T(8,128)(2,1)S(1)}, u32[]{:S(2)}, u32[]{:S(2)}) collective-permute-start(bf16[4,2,128,128]{3,2,1,0:T(8,128)(2,1)S(1)} %pad_maximum_fusion.refs_6_), channel_id=1, source_target_pairs={{0,2},{1,3},{2,0},{3,1},{4,6},{5,7},{6,4},{7,5},{8,10},{9,11},{10,... | collective-permute-start | bytes 786440 | tf_op jit(solution)/shard_map/ppermute | solution.py:38
  25.5 0.5 collective-permute-done.6.refs_7_
  26.0 2.5 %collective-permute-start.8 = (bf16[4,2,128,128]{3,2,1,0:T(8,128)(2,1)S(1)}, bf16[4,2,128,128]{3,2,1,0:T(8,128)(2,1)S(1)}, u32[]{:S(2)}, u32[]{:S(2)}) collective-permute-start(bf16[4,2,128,128]{3,2,1,0:T(8,128)(2,1)S(1)} %pad_maximum_fusion.refs_6_), channel_id=1, source_target_pairs={{0,3},{1,0},{2,1},{3,2},{4,7},{5,4},{6,5},{7,6},{8,11},{9,8},{10,9... | collective-permute-start | bytes 786440 | tf_op jit(solution)/shard_map/ppermute | solution.py:38
  28.6 0.0 copy-start.9
  28.6 4.1 %collective-permute-done.7.refs_8_ = bf16[4,2,128,128]{3,2,1,0:T(8,128)(2,1)S(1)} collective-permute-done((bf16[4,2,128,128]{3,2,1,0:T(8,128)(2,1)S(1)}, bf16[4,2,128,128]{3,2,1,0:T(8,128)(2,1)S(1)}, u32[]{:S(2)}, u32[]{:S(2)}) %collective-permute-start.7) | collective-permute-done | bytes 262176 | tf_op jit(solution)/shard_map/ppermute | solution.py:38
  32.7 2.0 %collective-permute-start.12 = (bf16[4,2,128,128]{3,2,1,0:T(8,128)(2,1)S(1)}, bf16[4,2,128,128]{3,2,1,0:T(8,128)(2,1)S(1)}, u32[]{:S(2)}, u32[]{:S(2)}) collective-permute-start(bf16[4,2,128,128]{3,2,1,0:T(8,128)(2,1)S(1)} %pad_maximum_fusion.1.refs_6_), channel_id=1, source_target_pairs={{0,1},{1,2},{2,3},{3,0},{4,5},{5,6},{6,7},{7,4},{8,9},{9,10},{10,1... | collective-permute-start | bytes 786440 | tf_op jit(solution)/shard_map/ppermute | solution.py:38
  34.8 3.8 %shard_map.106 = (bf16[2064,128]{1,0:T(8,128)(2,1)}, bf16[2064,128]{1,0:T(8,128)(2,1)}, bf16[2064,128]{1,0:T(8,128)(2,1)}, bf16[2064,128]{1,0:T(8,128)(2,1)}) custom-call(s32[4]{0:T(128)} %pad_add_fusion.place.refs_0_, bf16[2,128,4,8,128]{4,3,2,1,0:T(8,128)(2,1)} %bitcast.29, bf16[2,128,4,8,128]{4,3,2,1,0:T(8,128)(2,1)} %bitcast.31, ...), custom_call_target="tpu_custom_call" | custom-call | tf_op jit(solution)/shard_map/pallas_call | solution.py:82
  39.3 0.5 convert_divide_fusion.refs_1_
  39.9 1.7 %collective-permute-start.13 = (bf16[4,2,128,128]{3,2,1,0:T(8,128)(2,1)S(1)}, bf16[4,2,128,128]{3,2,1,0:T(8,128)(2,1)}, u32[]{:S(2)}, u32[]{:S(2)}) collective-permute-start(bf16[4,2,128,128]{3,2,1,0:T(8,128)(2,1)S(1)} %pad_maximum_fusion.1.refs_6_), channel_id=1, source_target_pairs={{0,2},{1,3},{2,0},{3,1},{4,6},{5,7},{6,4},{7,5},{8,10},{9,11},{10,... | collective-permute-start | bytes 786440 | tf_op jit(solution)/shard_map/ppermute | solution.py:38
  41.6 1.2 collective-permute-start.14
  42.7 6.0 %collective-permute-done.refs_2_ = bf16[2064,128]{1,0:T(8,128)(2,1)S(1)} collective-permute-done((bf16[2064,128]{1,0:T(8,128)(2,1)}, bf16[2064,128]{1,0:T(8,128)(2,1)S(1)}, u32[]{:S(2)}, u32[]{:S(2)}) %collective-permute-start) | collective-permute-done | bytes 528416 | tf_op jit(solution)/shard_map/ppermute | solution.py:38
  48.7 4.4 %collective-permute-done.1.refs_4_ = bf16[2064,128]{1,0:T(8,128)(2,1)S(1)} collective-permute-done((bf16[2064,128]{1,0:T(8,128)(2,1)}, bf16[2064,128]{1,0:T(8,128)(2,1)S(1)}, u32[]{:S(2)}, u32[]{:S(2)}) %collective-permute-start.1) | collective-permute-done | bytes 528416 | tf_op jit(solution)/shard_map/ppermute | solution.py:38
  53.1 0.2 collective-permute-start.10
  53.3 3.1 %collective-permute-start.11 = (bf16[2064,128]{1,0:T(8,128)(2,1)}, bf16[2064,128]{1,0:T(8,128)(2,1)}, u32[]{:S(2)}, u32[]{:S(2)}) collective-permute-start(bf16[2064,128]{1,0:T(8,128)(2,1)} %get-tuple-element.58), channel_id=1, source_target_pairs={{0,12},{1,13},{2,14},{3,15},{4,0},{5,1},{6,2},{7,3},{8,4},{9,5},{1... | collective-permute-start | bytes 1585160 | tf_op jit(solution)/shard_map/ppermute | solution.py:38
  56.4 21.9 %shard_map.105 = (bf16[1024,128]{1,0:T(8,128)(2,1)}, bf16[1024,128]{1,0:T(8,128)(2,1)}, bf16[1024,128]{1,0:T(8,128)(2,1)}, bf16[1024,128]{1,0:T(8,128)(2,1)}, bf16[16,2,128,128]{3,2,1,0:T(8,128)(2,1)}) custom-call(s32[4]{0:T(128)} %pad_add_fusion.place.refs_0_, f32[2]{0:T(128)} %convert_divide_fusion.refs_1_, bf16[2064,128]{1,0:T(8,128)(2,1)} %copy-done.10, ...), custom_call_target="tpu_custom_call" | custom-call | flops 10737418240 | bytes 8388608 | tf_op jit(solution)/shard_map/pallas_call | solution.py:252
  78.3 3.8 %all-to-all-start = ((bf16[16,2,128,128]{3,2,1,0:T(8,128)(2,1)}), bf16[16,2,128,128]{3,2,1,0:T(8,128)(2,1)S(1)}, u32[]{:S(2)}, u32[]{:S(2)}) async-start(bf16[16,2,128,128]{3,2,1,0:T(8,128)(2,1)} %get-tuple-element.50), calls=%async_computation | async-start | bytes 2097152 | tf_op jit(solution)/shard_map/all_to_all | solution.py:353
  82.1 3.2 %collective-permute-start.15 = (bf16[1024,128]{1,0:T(8,128)(2,1)S(1)}, bf16[1024,128]{1,0:T(8,128)(2,1)S(1)}, u32[]{:S(2)}, u32[]{:S(2)}) collective-permute-start(bf16[1024,128]{1,0:T(8,128)(2,1)S(1)} %copy-done.19), channel_id=1, source_target_pairs={{0,12},{1,13},{2,14},{3,15},{4,0},{5,1},{6,2},{7,3},{8,4},{9,5},{1... | collective-permute-start | bytes 786440 | tf_op jit(solution)/shard_map/ppermute | solution.py:38
  85.3 0.8 collective-permute-start.16
  86.1 0.9 collective-permute-start.17
  87.0 21.8 %shard_map.107 = (bf16[1024,128]{1,0:T(8,128)(2,1)}, bf16[1024,128]{1,0:T(8,128)(2,1)}, bf16[1024,128]{1,0:T(8,128)(2,1)}, bf16[1024,128]{1,0:T(8,128)(2,1)}, bf16[16,2,128,128]{3,2,1,0:T(8,128)(2,1)}) custom-call(s32[4]{0:T(128)} %pad_add_fusion.place.refs_0_, f32[2]{0:T(128)} %convert_divide_fusion.refs_1_, ...), custom_call_target="tpu_custom_call" | custom-call | flops 10737418240 | bytes 8388608 | tf_op jit(solution)/shard_map/pallas_call | solution.py:252
  108.9 0.0 copy-start.1
  108.9 9.8 %all-to-all-start.1 = ((bf16[16,2,128,128]{3,2,1,0:T(8,128)(2,1)}), bf16[16,2,128,128]{3,2,1,0:T(8,128)(2,1)S(1)}, u32[]{:S(2)}, u32[]{:S(2)}) async-start(bf16[16,2,128,128]{3,2,1,0:T(8,128)(2,1)} %get-tuple-element.65), calls=%async_computation.1 | async-start | bytes 2097152 | tf_op jit(solution)/shard_map/all_to_all | solution.py:353
  118.7 3.1 %collective-permute-start.18 = (bf16[1024,128]{1,0:T(8,128)(2,1)}, bf16[1024,128]{1,0:T(8,128)(2,1)S(1)}, u32[]{:S(2)}, u32[]{:S(2)}) collective-permute-start(bf16[1024,128]{1,0:T(8,128)(2,1)} %get-tuple-element.68), channel_id=1, source_target_pairs={{0,12},{1,13},{2,14},{3,15},{4,0},{5,1},{6,2},{7,3},{8,4},{9,5},{1... | collective-permute-start | bytes 786440 | tf_op jit(solution)/shard_map/ppermute | solution.py:38
  121.9 0.9 collective-permute-start.19
  122.7 0.9 collective-permute-start.20
  123.6 0.6 reduce_sum.27
  124.2 6.4 %psum.7 = s32[]{:T(128)} all-reduce(s32[]{:T(128)} %reduce_sum.27), channel_id=1, replica_groups=mesh['dp'=8,'seq'=16] {'dp'}, use_global_device_ids=true, to_apply=%region_1.2 | all-reduce | flops 1 | bytes 8 | tf_op jit(solution)/shard_map/psum | solution.py:357
  131.3 1.9 %collective-permute-done.18.refs_5_ = bf16[1024,128]{1,0:T(8,128)(2,1)S(1)} collective-permute-done((bf16[1024,128]{1,0:T(8,128)(2,1)}, bf16[1024,128]{1,0:T(8,128)(2,1)S(1)}, u32[]{:S(2)}, u32[]{:S(2)}) %collective-permute-start.18) | collective-permute-done | bytes 262176 | tf_op jit(solution)/shard_map/ppermute | solution.py:38
  133.1 0.0 collective-permute-done.19.refs_6_
  133.1 2.8 %collective-permute-done.20.refs_7_ = bf16[1024,128]{1,0:T(8,128)(2,1)} collective-permute-done((bf16[1024,128]{1,0:T(8,128)(2,1)}, bf16[1024,128]{1,0:T(8,128)(2,1)}, u32[]{:S(2)}, u32[]{:S(2)}) %collective-permute-start.20) | collective-permute-done | bytes 262176 | tf_op jit(solution)/shard_map/ppermute | solution.py:38
  136.0 3.4 %shard_map.108 = bf16[2,128,4,8,128]{4,3,2,1,0:T(8,128)(2,1)} custom-call(s32[4]{0:T(128)} %pad_add_fusion.place.refs_0_, f32[1]{0:T(128)} %bitcast.9.mean_len, bf16[1024,128]{1,0:T(8,128)(2,1)} %get-tuple-element.61.refs_0_, bf16[1024,128]{1,0:T(8,128)(2,1)} %copy-done, bf16[1024,128]{1,0:T(8,128)(2,1)} %copy-done.1, bf16[1024,128]{1,0:T(8,128)(2,1)} %copy-done.2, ...), custom_call_target="tpu_custom_call" | custom-call | tf_op jit(solution)/shard_map/pallas_call | solution.py:359
  139.4 0.2 convert_reduce_fusion.1
  139.5 0.2 convert_reduce_fusion
  139.7 0.1 fusion.1
  139.9 0.9 copy.15
  140.8 0.9 copy.16
  (62 shorter events, 0.3 us)
Async XLA Ops:
  0.6 2.0 %copy-start.8 = (s32[2]{0:T(128)S(1)}, s32[2]{0:T(128)}, u32[]{:S(2)}) copy-start(s32[2]{0:T(128)} %param.13) | copy-start | bytes 28
  5.1 10.4 %collective-permute-start.3 = (bf16[2,2,128,128]{3,2,1,0:T(8,128)(2,1)}, bf16[2,2,128,128]{3,2,1,0:T(8,128)(2,1)S(1)}, u32[]{:S(2)}, u32[]{:S(2)}) collective-permute-start(bf16[2,2,128,128]{3,2,1,0:T(8,128)(2,1)} %get-tuple-element.38), channel_id=1, source_target_pairs={{0,4},{1,5},{2,6},{3,7},{4,8},{5,9},{6,10},{7,11},{8,12},{9,13},{1... | collective-permute-start | bytes 393224 | tf_op jit(solution)/shard_map/ppermute | solution.py:38
  7.0 9.8 %collective-permute-start.4 = (bf16[2,2,128,128]{3,2,1,0:T(8,128)(2,1)}, bf16[2,2,128,128]{3,2,1,0:T(8,128)(2,1)S(1)}, u32[]{:S(2)}, u32[]{:S(2)}) collective-permute-start(bf16[2,2,128,128]{3,2,1,0:T(8,128)(2,1)} %get-tuple-element.39), channel_id=1, source_target_pairs={{0,8},{1,9},{2,10},{3,11},{4,12},{5,13},{6,14},{7,15},{8,0},{9,1},... | collective-permute-start | bytes 393224 | tf_op jit(solution)/shard_map/ppermute | solution.py:38
  10.6 6.2 %collective-permute-start.5 = (bf16[2,2,128,128]{3,2,1,0:T(8,128)(2,1)}, bf16[2,2,128,128]{3,2,1,0:T(8,128)(2,1)S(1)}, u32[]{:S(2)}, u32[]{:S(2)}) collective-permute-start(bf16[2,2,128,128]{3,2,1,0:T(8,128)(2,1)} %get-tuple-element.40), channel_id=1, source_target_pairs={{0,12},{1,13},{2,14},{3,15},{4,0},{5,1},{6,2},{7,3},{8,4},{9,5},{1... | collective-permute-start | bytes 393224 | tf_op jit(solution)/shard_map/ppermute | solution.py:38
  11.6 5.3 %copy-start.7 = (bf16[2,2,128,128]{3,2,1,0:T(8,128)(2,1)S(1)}, bf16[2,2,128,128]{3,2,1,0:T(8,128)(2,1)}, u32[]{:S(2)}) copy-start(bf16[2,2,128,128]{3,2,1,0:T(8,128)(2,1)} %get-tuple-element.46) | copy-start | bytes 393220
  17.0 21.6 %copy-start.6 = (bf16[4,2,128,128]{3,2,1,0:T(8,128)(2,1)}, bf16[4,2,128,128]{3,2,1,0:T(8,128)(2,1)S(1)}, u32[]{:S(2)}) copy-start(bf16[4,2,128,128]{3,2,1,0:T(8,128)(2,1)S(1)} %pad_maximum_fusion.refs_6_) | copy-start | bytes 786436
  17.0 9.1 %collective-permute-start.6 = (bf16[4,2,128,128]{3,2,1,0:T(8,128)(2,1)S(1)}, bf16[4,2,128,128]{3,2,1,0:T(8,128)(2,1)S(1)}, u32[]{:S(2)}, u32[]{:S(2)}) collective-permute-start(bf16[4,2,128,128]{3,2,1,0:T(8,128)(2,1)S(1)} %pad_maximum_fusion.refs_6_), channel_id=1, source_target_pairs={{0,1},{1,2},{2,3},{3,0},{4,5},{5,6},{6,7},{7,4},{8,9},{9,10},{10,1... | collective-permute-start | bytes 786440 | tf_op jit(solution)/shard_map/ppermute | solution.py:38
  18.5 30.2 %collective-permute-start = (bf16[2064,128]{1,0:T(8,128)(2,1)}, bf16[2064,128]{1,0:T(8,128)(2,1)S(1)}, u32[]{:S(2)}, u32[]{:S(2)}) collective-permute-start(bf16[2064,128]{1,0:T(8,128)(2,1)} %get-tuple-element.42), channel_id=1, source_target_pairs={{0,12},{1,13},{2,14},{3,15},{4,0},{5,1},{6,2},{7,3},{8,4},{9,5},{1... | collective-permute-start | bytes 1585160 | tf_op jit(solution)/shard_map/ppermute | solution.py:38
  20.6 32.5 %collective-permute-start.1 = (bf16[2064,128]{1,0:T(8,128)(2,1)}, bf16[2064,128]{1,0:T(8,128)(2,1)S(1)}, u32[]{:S(2)}, u32[]{:S(2)}) collective-permute-start(bf16[2064,128]{1,0:T(8,128)(2,1)} %get-tuple-element.44), channel_id=1, source_target_pairs={{0,4},{1,5},{2,6},{3,7},{4,8},{5,9},{6,10},{7,11},{8,12},{9,13},{1... | collective-permute-start | bytes 1585160 | tf_op jit(solution)/shard_map/ppermute | solution.py:38
  20.6 32.7 %collective-permute-start.2 = (bf16[2064,128]{1,0:T(8,128)(2,1)}, bf16[2064,128]{1,0:T(8,128)(2,1)S(1)}, u32[]{:S(2)}, u32[]{:S(2)}) collective-permute-start(bf16[2064,128]{1,0:T(8,128)(2,1)} %get-tuple-element.45), channel_id=1, source_target_pairs={{0,8},{1,9},{2,10},{3,11},{4,12},{5,13},{6,14},{7,15},{8,0},{9,1},... | collective-permute-start | bytes 1585160 | tf_op jit(solution)/shard_map/ppermute | solution.py:38
  22.8 9.9 %collective-permute-start.7 = (bf16[4,2,128,128]{3,2,1,0:T(8,128)(2,1)S(1)}, bf16[4,2,128,128]{3,2,1,0:T(8,128)(2,1)S(1)}, u32[]{:S(2)}, u32[]{:S(2)}) collective-permute-start(bf16[4,2,128,128]{3,2,1,0:T(8,128)(2,1)S(1)} %pad_maximum_fusion.refs_6_), channel_id=1, source_target_pairs={{0,2},{1,3},{2,0},{3,1},{4,6},{5,7},{6,4},{7,5},{8,10},{9,11},{10,... | collective-permute-start | bytes 786440 | tf_op jit(solution)/shard_map/ppermute | solution.py:38
  26.0 12.6 %copy-start.14 = (bf16[4,2,128,128]{3,2,1,0:T(8,128)(2,1)}, bf16[4,2,128,128]{3,2,1,0:T(8,128)(2,1)S(1)}, u32[]{:S(2)}) copy-start(bf16[4,2,128,128]{3,2,1,0:T(8,128)(2,1)S(1)} %collective-permute-done.6.refs_7_) | copy-start | bytes 786436
  26.0 13.8 %collective-permute-start.8 = (bf16[4,2,128,128]{3,2,1,0:T(8,128)(2,1)S(1)}, bf16[4,2,128,128]{3,2,1,0:T(8,128)(2,1)S(1)}, u32[]{:S(2)}, u32[]{:S(2)}) collective-permute-start(bf16[4,2,128,128]{3,2,1,0:T(8,128)(2,1)S(1)} %pad_maximum_fusion.refs_6_), channel_id=1, source_target_pairs={{0,3},{1,0},{2,1},{3,2},{4,7},{5,4},{6,5},{7,6},{8,11},{9,8},{10,9... | collective-permute-start | bytes 786440 | tf_op jit(solution)/shard_map/ppermute | solution.py:38
  28.6 12.9 %copy-start.5 = (bf16[4,2,128,128]{3,2,1,0:T(8,128)(2,1)}, bf16[4,2,128,128]{3,2,1,0:T(8,128)(2,1)S(1)}, u32[]{:S(2)}) copy-start(bf16[4,2,128,128]{3,2,1,0:T(8,128)(2,1)S(1)} %pad_maximum_fusion.1.refs_6_) | copy-start | bytes 786436
  28.6 10.7 %copy-start.9 = (f32[2]{0:T(128)S(1)}, f32[2]{0:T(128)}, u32[]{:S(2)}) copy-start(f32[2]{0:T(128)} %constant.42.clone) | copy-start | bytes 28
  32.7 5.9 %copy-start.15 = (bf16[4,2,128,128]{3,2,1,0:T(8,128)(2,1)}, bf16[4,2,128,128]{3,2,1,0:T(8,128)(2,1)S(1)}, u32[]{:S(2)}) copy-start(bf16[4,2,128,128]{3,2,1,0:T(8,128)(2,1)S(1)} %collective-permute-done.7.refs_8_) | copy-start | bytes 786436
  32.7 8.8 %collective-permute-start.12 = (bf16[4,2,128,128]{3,2,1,0:T(8,128)(2,1)S(1)}, bf16[4,2,128,128]{3,2,1,0:T(8,128)(2,1)S(1)}, u32[]{:S(2)}, u32[]{:S(2)}) collective-permute-start(bf16[4,2,128,128]{3,2,1,0:T(8,128)(2,1)S(1)} %pad_maximum_fusion.1.refs_6_), channel_id=1, source_target_pairs={{0,1},{1,2},{2,3},{3,0},{4,5},{5,6},{6,7},{7,4},{8,9},{9,10},{10,1... | collective-permute-start | bytes 786440 | tf_op jit(solution)/shard_map/ppermute | solution.py:38
  39.9 16.5 %copy-start.16 = (bf16[4,2,128,128]{3,2,1,0:T(8,128)(2,1)}, bf16[4,2,128,128]{3,2,1,0:T(8,128)(2,1)S(1)}, u32[]{:S(2)}) copy-start(bf16[4,2,128,128]{3,2,1,0:T(8,128)(2,1)S(1)} %collective-permute-done.8.refs_9_) | copy-start | bytes 786436
  39.9 42.2 %collective-permute-start.13 = (bf16[4,2,128,128]{3,2,1,0:T(8,128)(2,1)S(1)}, bf16[4,2,128,128]{3,2,1,0:T(8,128)(2,1)}, u32[]{:S(2)}, u32[]{:S(2)}) collective-permute-start(bf16[4,2,128,128]{3,2,1,0:T(8,128)(2,1)S(1)} %pad_maximum_fusion.1.refs_6_), channel_id=1, source_target_pairs={{0,2},{1,3},{2,0},{3,1},{4,6},{5,7},{6,4},{7,5},{8,10},{9,11},{10,... | collective-permute-start | bytes 786440 | tf_op jit(solution)/shard_map/ppermute | solution.py:38
  41.5 36.7 %copy-start.13 = (bf16[4,2,128,128]{3,2,1,0:T(8,128)(2,1)}, bf16[4,2,128,128]{3,2,1,0:T(8,128)(2,1)S(1)}, u32[]{:S(2)}) copy-start(bf16[4,2,128,128]{3,2,1,0:T(8,128)(2,1)S(1)} %collective-permute-done.12.refs_7_) | copy-start | bytes 786436
  41.6 43.7 %collective-permute-start.14 = (bf16[4,2,128,128]{3,2,1,0:T(8,128)(2,1)S(1)}, bf16[4,2,128,128]{3,2,1,0:T(8,128)(2,1)}, u32[]{:S(2)}, u32[]{:S(2)}) collective-permute-start(bf16[4,2,128,128]{3,2,1,0:T(8,128)(2,1)S(1)} %pad_maximum_fusion.1.refs_6_), channel_id=1, source_target_pairs={{0,3},{1,0},{2,1},{3,2},{4,7},{5,4},{6,5},{7,6},{8,11},{9,8},{10,9... | collective-permute-start | bytes 786440 | tf_op jit(solution)/shard_map/ppermute | solution.py:38
  48.7 7.7 %copy-start.10 = (bf16[2064,128]{1,0:T(8,128)(2,1)}, bf16[2064,128]{1,0:T(8,128)(2,1)S(1)}, u32[]{:S(2)}) copy-start(bf16[2064,128]{1,0:T(8,128)(2,1)S(1)} %collective-permute-done.refs_2_) | copy-start | bytes 1585156
  48.7 37.4 %collective-permute-start.9 = (bf16[2064,128]{1,0:T(8,128)(2,1)}, bf16[2064,128]{1,0:T(8,128)(2,1)}, u32[]{:S(2)}, u32[]{:S(2)}) collective-permute-start(bf16[2064,128]{1,0:T(8,128)(2,1)} %get-tuple-element.56), channel_id=1, source_target_pairs={{0,8},{1,9},{2,10},{3,11},{4,12},{5,13},{6,14},{7,15},{8,0},{9,1},... | collective-permute-start | bytes 1585160 | tf_op jit(solution)/shard_map/ppermute | solution.py:38
  53.1 3.3 %copy-start.11 = (bf16[2064,128]{1,0:T(8,128)(2,1)}, bf16[2064,128]{1,0:T(8,128)(2,1)S(1)}, u32[]{:S(2)}) copy-start(bf16[2064,128]{1,0:T(8,128)(2,1)S(1)} %collective-permute-done.1.refs_4_) | copy-start | bytes 1585156
  53.1 33.9 %collective-permute-start.10 = (bf16[2064,128]{1,0:T(8,128)(2,1)}, bf16[2064,128]{1,0:T(8,128)(2,1)}, u32[]{:S(2)}, u32[]{:S(2)}) collective-permute-start(bf16[2064,128]{1,0:T(8,128)(2,1)} %get-tuple-element.57), channel_id=1, source_target_pairs={{0,4},{1,5},{2,6},{3,7},{4,8},{5,9},{6,10},{7,11},{8,12},{9,13},{1... | collective-permute-start | bytes 1585160 | tf_op jit(solution)/shard_map/ppermute | solution.py:38
  53.3 3.1 %copy-start.12 = (bf16[2064,128]{1,0:T(8,128)(2,1)}, bf16[2064,128]{1,0:T(8,128)(2,1)S(1)}, u32[]{:S(2)}) copy-start(bf16[2064,128]{1,0:T(8,128)(2,1)S(1)} %collective-permute-done.2.refs_5_) | copy-start | bytes 1585156
  53.3 33.7 %collective-permute-start.11 = (bf16[2064,128]{1,0:T(8,128)(2,1)}, bf16[2064,128]{1,0:T(8,128)(2,1)}, u32[]{:S(2)}, u32[]{:S(2)}) collective-permute-start(bf16[2064,128]{1,0:T(8,128)(2,1)} %get-tuple-element.58), channel_id=1, source_target_pairs={{0,12},{1,13},{2,14},{3,15},{4,0},{5,1},{6,2},{7,3},{8,4},{9,5},{1... | collective-permute-start | bytes 1585160 | tf_op jit(solution)/shard_map/ppermute | solution.py:38
  78.3 3.8 %copy-start.19 = (bf16[1024,128]{1,0:T(8,128)(2,1)S(1)}, bf16[1024,128]{1,0:T(8,128)(2,1)}, u32[]{:S(2)}) copy-start(bf16[1024,128]{1,0:T(8,128)(2,1)} %get-tuple-element.62) | copy-start | bytes 786436
  78.3 7.0 %copy-start.18 = (bf16[1024,128]{1,0:T(8,128)(2,1)S(1)}, bf16[1024,128]{1,0:T(8,128)(2,1)}, u32[]{:S(2)}) copy-start(bf16[1024,128]{1,0:T(8,128)(2,1)} %get-tuple-element.63) | copy-start | bytes 786436
  78.3 7.8 %copy-start.17 = (bf16[1024,128]{1,0:T(8,128)(2,1)S(1)}, bf16[1024,128]{1,0:T(8,128)(2,1)}, u32[]{:S(2)}) copy-start(bf16[1024,128]{1,0:T(8,128)(2,1)} %get-tuple-element.64) | copy-start | bytes 786436
  78.3 30.6 %all-to-all-start = ((bf16[16,2,128,128]{3,2,1,0:T(8,128)(2,1)}), bf16[16,2,128,128]{3,2,1,0:T(8,128)(2,1)S(1)}, u32[]{:S(2)}, u32[]{:S(2)}) async-start(bf16[16,2,128,128]{3,2,1,0:T(8,128)(2,1)} %get-tuple-element.50), calls=%async_computation | async-start | bytes 2097152 | tf_op jit(solution)/shard_map/all_to_all | solution.py:353
  82.1 26.7 %collective-permute-start.15 = (bf16[1024,128]{1,0:T(8,128)(2,1)S(1)}, bf16[1024,128]{1,0:T(8,128)(2,1)S(1)}, u32[]{:S(2)}, u32[]{:S(2)}) collective-permute-start(bf16[1024,128]{1,0:T(8,128)(2,1)S(1)} %copy-done.19), channel_id=1, source_target_pairs={{0,12},{1,13},{2,14},{3,15},{4,0},{5,1},{6,2},{7,3},{8,4},{9,5},{1... | collective-permute-start | bytes 786440 | tf_op jit(solution)/shard_map/ppermute | solution.py:38
  85.3 23.6 %collective-permute-start.16 = (bf16[1024,128]{1,0:T(8,128)(2,1)S(1)}, bf16[1024,128]{1,0:T(8,128)(2,1)S(1)}, u32[]{:S(2)}, u32[]{:S(2)}) collective-permute-start(bf16[1024,128]{1,0:T(8,128)(2,1)S(1)} %copy-done.18), channel_id=1, source_target_pairs={{0,8},{1,9},{2,10},{3,11},{4,12},{5,13},{6,14},{7,15},{8,0},{9,1},... | collective-permute-start | bytes 786440 | tf_op jit(solution)/shard_map/ppermute | solution.py:38
  86.1 22.8 %collective-permute-start.17 = (bf16[1024,128]{1,0:T(8,128)(2,1)S(1)}, bf16[1024,128]{1,0:T(8,128)(2,1)S(1)}, u32[]{:S(2)}, u32[]{:S(2)}) collective-permute-start(bf16[1024,128]{1,0:T(8,128)(2,1)S(1)} %copy-done.17), channel_id=1, source_target_pairs={{0,4},{1,5},{2,6},{3,7},{4,8},{5,9},{6,10},{7,11},{8,12},{9,13},{1... | collective-permute-start | bytes 786440 | tf_op jit(solution)/shard_map/ppermute | solution.py:38
  108.9 27.1 %copy-start = (bf16[1024,128]{1,0:T(8,128)(2,1)}, bf16[1024,128]{1,0:T(8,128)(2,1)S(1)}, u32[]{:S(2)}) copy-start(bf16[1024,128]{1,0:T(8,128)(2,1)S(1)} %collective-permute-done.15.refs_1_) | copy-start | bytes 786436
  108.9 27.1 %copy-start.1 = (bf16[1024,128]{1,0:T(8,128)(2,1)}, bf16[1024,128]{1,0:T(8,128)(2,1)S(1)}, u32[]{:S(2)}) copy-start(bf16[1024,128]{1,0:T(8,128)(2,1)S(1)} %collective-permute-done.16.refs_2_) | copy-start | bytes 786436
  108.9 27.1 %copy-start.2 = (bf16[1024,128]{1,0:T(8,128)(2,1)}, bf16[1024,128]{1,0:T(8,128)(2,1)S(1)}, u32[]{:S(2)}) copy-start(bf16[1024,128]{1,0:T(8,128)(2,1)S(1)} %collective-permute-done.17.refs_3_) | copy-start | bytes 786436
  108.9 30.6 %all-to-all-start.1 = ((bf16[16,2,128,128]{3,2,1,0:T(8,128)(2,1)}), bf16[16,2,128,128]{3,2,1,0:T(8,128)(2,1)S(1)}, u32[]{:S(2)}, u32[]{:S(2)}) async-start(bf16[16,2,128,128]{3,2,1,0:T(8,128)(2,1)} %get-tuple-element.65), calls=%async_computation.1 | async-start | bytes 2097152 | tf_op jit(solution)/shard_map/all_to_all | solution.py:353
  118.7 14.4 %collective-permute-start.18 = (bf16[1024,128]{1,0:T(8,128)(2,1)}, bf16[1024,128]{1,0:T(8,128)(2,1)S(1)}, u32[]{:S(2)}, u32[]{:S(2)}) collective-permute-start(bf16[1024,128]{1,0:T(8,128)(2,1)} %get-tuple-element.68), channel_id=1, source_target_pairs={{0,12},{1,13},{2,14},{3,15},{4,0},{5,1},{6,2},{7,3},{8,4},{9,5},{1... | collective-permute-start | bytes 786440 | tf_op jit(solution)/shard_map/ppermute | solution.py:38
  121.9 11.3 %collective-permute-start.19 = (bf16[1024,128]{1,0:T(8,128)(2,1)}, bf16[1024,128]{1,0:T(8,128)(2,1)S(1)}, u32[]{:S(2)}, u32[]{:S(2)}) collective-permute-start(bf16[1024,128]{1,0:T(8,128)(2,1)} %get-tuple-element.69), channel_id=1, source_target_pairs={{0,8},{1,9},{2,10},{3,11},{4,12},{5,13},{6,14},{7,15},{8,0},{9,1},... | collective-permute-start | bytes 786440 | tf_op jit(solution)/shard_map/ppermute | solution.py:38
  122.7 13.2 %collective-permute-start.20 = (bf16[1024,128]{1,0:T(8,128)(2,1)}, bf16[1024,128]{1,0:T(8,128)(2,1)}, u32[]{:S(2)}, u32[]{:S(2)}) collective-permute-start(bf16[1024,128]{1,0:T(8,128)(2,1)} %get-tuple-element.70), channel_id=1, source_target_pairs={{0,4},{1,5},{2,6},{3,7},{4,8},{5,9},{6,10},{7,11},{8,12},{9,13},{1... | collective-permute-start | bytes 786440 | tf_op jit(solution)/shard_map/ppermute | solution.py:38
  133.1 2.8 %copy-start.3 = (bf16[1024,128]{1,0:T(8,128)(2,1)}, bf16[1024,128]{1,0:T(8,128)(2,1)S(1)}, u32[]{:S(2)}) copy-start(bf16[1024,128]{1,0:T(8,128)(2,1)S(1)} %collective-permute-done.18.refs_5_) | copy-start | bytes 786436
  133.1 2.8 %copy-start.4 = (bf16[1024,128]{1,0:T(8,128)(2,1)}, bf16[1024,128]{1,0:T(8,128)(2,1)S(1)}, u32[]{:S(2)}) copy-start(bf16[1024,128]{1,0:T(8,128)(2,1)S(1)} %collective-permute-done.19.refs_6_) | copy-start | bytes 786436

commit v4 on v3

--- a/solution.py
+++ b/solution.py
@@ -159,24 +159,39 @@
             per = CHUNK // TOK
             rest = lax.rem(block, per) + 1
 
+            def halves(width):
+                return 2 if width % 2 == 0 else 1
+
             def scores_step(c, width, carry, masked):
+                parts = halves(width)
+                size = width // parts
+
+                def scores(j):
+                    s = lax.dot_general(
+                        k_s[pl.ds(c * per + j * size, size)].reshape(size * TOK, DIM),
+                        pk[d, 0:ROWS, :],
+                        NT,
+                        preferred_element_type=f32,
+                    )
+                    if masked:
+                        key = lax.broadcasted_iota(jnp.int32, (size * TOK, ROWS), 0)
+                        key += c * CHUNK + j * size * TOK
+                        s = jnp.where(key <= lane_token, s, -jnp.inf)
+                    return s
+
                 top, total = carry
-                k0 = pl.multiple_of(c * CHUNK, CHUNK)
-                s = lax.dot_general(
-                    k_s[pl.ds(c * per, width)].reshape(width * TOK, DIM),
-                    pk[d, 0:ROWS, :],
-                    NT,
-                    preferred_element_type=f32,
-                )
-                if masked:
-                    key = lax.broadcasted_iota(jnp.int32, (width * TOK, ROWS), 0) + k0
-                    s = jnp.where(key <= lane_token, s, -jnp.inf)
-                new = jnp.maximum(top, jnp.max(s, axis=0, keepdims=True))
-                p = jnp.exp2((s - new) * EXP2)
-                p_s[pl.ds(k0, width * TOK), :] = p
-                m_s[c] = jnp.broadcast_to(new, (8, ROWS))
-                total = total * jnp.exp2((top - new) * EXP2) + jnp.sum(p, axis=0, keepdims=True)
-                return new, total
+                held = scores(0)
+                for j in range(parts):
+                    later = scores(j + 1) if j + 1 < parts else None
+                    new = jnp.maximum(top, jnp.max(held, axis=0, keepdims=True))
+                    p = jnp.exp2((held - new) * EXP2)
+                    k0 = pl.multiple_of(c * CHUNK + j * size * TOK, TOK)
+                    p_s[pl.ds(k0, size * TOK), :] = p
+                    m_s[c * 2 + j] = jnp.broadcast_to(new, (8, ROWS))
+                    total = total * jnp.exp2((top - new) * EXP2)
+                    total += jnp.sum(p, axis=0, keepdims=True)
+                    top, held = new, later
+                return top, total
 
             carry = (jnp.full((1, ROWS), -1e30, f32), jnp.zeros((1, ROWS), f32))
             carry = lax.fori_loop(
@@ -195,18 +210,39 @@
             dqt_s[...] = jnp.zeros_like(dqt_s)
 
             def grads_step(c, width):
-                k0 = pl.multiple_of(c * CHUNK, CHUNK)
-                at = pl.ds(k0, width * TOK)
-                g = gm_s[...]
-                weight = jnp.exp2((m_s[c][0:1] - top) * EXP2) * inverse
-                dp = lax.dot_general(
-                    v_s[pl.ds(c * per, width)].reshape(width * TOK, DIM), g, NT, preferred_element_type=f32
-                )
-                prob = p_s[at, :] * weight
-                ds = (prob * (dp - delta)).astype(bf16)
-                dva[at, :] += lax.dot_general(prob.astype(bf16), g, NN, preferred_element_type=f32)
-                dka[at, :] += lax.dot_general(ds, pk[d, 0:ROWS, :], NN, preferred_element_type=f32)
-                dqt_s[...] += lax.dot_general(kt_s[:, at], ds, NN, preferred_element_type=f32)
+                parts = halves(width)
+                size = width // parts
+
+                def keys_at(j):
+                    return pl.ds(pl.multiple_of(c * CHUNK + j * size * TOK, TOK), size * TOK)
+
+                def dprob(j):
+                    return lax.dot_general(
+                        v_s[pl.ds(c * per + j * size, size)].reshape(size * TOK, DIM),
+                        gm_s[...],
+                        NT,
+                        preferred_element_type=f32,
+                    )
+
+                def add(j, low, ds):
+                    at = keys_at(j)
+                    dva[at, :] += lax.dot_general(low, gm_s[...], NN, preferred_element_type=f32)
+                    dka[at, :] += lax.dot_general(
+                        ds, pk[d, 0:ROWS, :], NN, preferred_element_type=f32
+                    )
+                    dqt_s[...] += lax.dot_general(kt_s[:, at], ds, NN, preferred_element_type=f32)
+
+                dp, ready = dprob(0), None
+                for j in range(parts):
+                    later = dprob(j + 1) if j + 1 < parts else None
+                    weight = jnp.exp2((m_s[c * 2 + j][0:1] - top) * EXP2) * inverse
+                    prob = p_s[keys_at(j), :] * weight
+                    ds = (prob * (dp - delta)).astype(bf16)
+                    low = prob.astype(bf16)
+                    if ready is not None:
+                        add(*ready)
+                    ready, dp = (j, low, ds), later
+                add(*ready)
 
             def full_step(c, _):
                 grads_step(c, per)
@@ -263,7 +299,7 @@
             pltpu.VMEM((FULL // TOK, TOK, DIM), bf16),
             pltpu.VMEM((DIM, FULL), bf16),
             pltpu.VMEM((FULL, ROWS), f32),
-            pltpu.VMEM((FULL // CHUNK, 8, ROWS), f32),
+            pltpu.VMEM((2 * FULL // CHUNK, 8, ROWS), f32),
             pltpu.VMEM((ROWS, DIM), bf16),
             pltpu.VMEM((DIM, ROWS), f32),
             pltpu.VMEM((16, ROWS), f32),

time: 140 us -> 139 us (level); the launches traced: 142 us -> 139 us
  Pallas kernels: 56.7 us -> 41.7 us
  waiting for transfers between devices: 21 us -> 35.1 us
  starting transfers between devices: 49 us -> 44.2 us
  blocking collectives: 6.41 us -> 9.16 us
    pallas_call x2, Pallas kernels: 43.7 us -> 28.7 us  [attention(): pl.pallas_call(functools.partial(attention_kernel, seq, shifts, first_cal...]
    ppermute x21, waiting for transfers between devices: 21 us -> 35.1 us  [shift(): return lax.ppermute(value, 'seq', shift_pairs(kind, by % SIDE))]
    all_to_all x2, starting transfers between devices: 13.6 us -> 8.79 us  [body(): parts = lax.all_to_all(prev, 'seq', 0, 0, tiled=True)]
    psum x1, blocking collectives: 6.41 us -> 9.16 us  [body(): total = lax.psum(jnp.sum(after(lengths, prev)), 'dp')]
  transfers between devices with their start and end apart: 23 -> 23, of which waited for: 7 -> 11; matrix products, arithmetic and copies ran while one was open for 1% -> 1% of each run, Pallas kernels for 39% -> 29%
where the time goes in v4:
time: 139 us
  starting transfers between devices  44.2 us (32%)
  Pallas kernels  41.7 us (30%)
  waiting for transfers between devices  35.1 us (25%)
  blocking collectives  9.16 us (7%)
  local copies, waits for them, and re-layouts  3.1 us (2%)
  other arithmetic  3.1 us (2%)
  between operations  2.31 us (2%)
    ppermute x21, starting transfers between devices, shift(): return lax.ppermute(value, 'seq', shift_pairs(kind, by % SIDE))  35.4 us
    ppermute x21, waiting for transfers between devices, shift(): return lax.ppermute(value, 'seq', shift_pairs(kind, by % SIDE))  35.1 us
    pallas_call x2, Pallas kernels, attention(): pl.pallas_call(functools.partial(attention_kernel, seq, shifts, first_cal...  28.7 us
    psum x1, blocking collectives, body(): total = lax.psum(jnp.sum(after(lengths, prev)), 'dp')  9.16 us
    all_to_all x2, starting transfers between devices, body(): parts = lax.all_to_all(prev, 'seq', 0, 0, tiled=True)  8.79 us
    pallas_call x2, Pallas kernels, pack(): pl.pallas_call(pack_kernel, grid=(1,), in_specs=[smem_spec()] + [spec] *...  7.74 us
    pallas_call x1, Pallas kernels, body(): pl.pallas_call(place_kernel, in_specs=[smem_spec()] * 2 + [vmem_spec()] *...  3.38 us
  transfers between devices with their start and end apart: 23, of which 11 were waited for; matrix products, arithmetic and copies ran while one was open for 1% of the time, Pallas kernels for 29%

profile of v4, /device:TPU:24, one launch (start us, length us, event | category | flops | bytes accessed | tf_op | source)
XLA Modules:
  0.0 138.6 jit_solution(5212789883895486033)
XLA Ops:
  0.7 1.1 copy_bitcast_fusion
  1.8 0.8 maximum_bitcast_fusion.kv_ref
  2.6 0.6 pad_add_fusion.place.refs_0_
  3.2 1.9 %shard_map.103 = (bf16[2,2,128,128]{3,2,1,0:T(8,128)(2,1)}, bf16[2,2,128,128]{3,2,1,0:T(8,128)(2,1)}, bf16[2,2,128,128]{3,2,1,0:T(8,128)(2,1)}, bf16[2,2,128,128]{3,2,1,0:T(8,128)(2,1)}) custom-call(s32[4]{0:T(128)} %pad_add_fusion.place.refs_0_, bf16[4,2,2,128,128]{4,3,2,1,0:T(8,128)(2,1)} %maximum_bitcast_fusion.kv_ref), custom_call_target="tpu_custom_call" | custom-call | tf_op jit(solution)/shard_map/pallas_call | solution.py:351
  5.1 1.9 %collective-permute-start.3 = (bf16[2,2,128,128]{3,2,1,0:T(8,128)(2,1)}, bf16[2,2,128,128]{3,2,1,0:T(8,128)(2,1)S(1)}, u32[]{:S(2)}, u32[]{:S(2)}) collective-permute-start(bf16[2,2,128,128]{3,2,1,0:T(8,128)(2,1)} %get-tuple-element.38), channel_id=1, source_target_pairs={{0,4},{1,5},{2,6},{3,7},{4,8},{5,9},{6,10},{7,11},{8,12},{9,13},{1... | collective-permute-start | bytes 393224 | tf_op jit(solution)/shard_map/ppermute | solution.py:38
  7.0 3.6 %collective-permute-start.4 = (bf16[2,2,128,128]{3,2,1,0:T(8,128)(2,1)}, bf16[2,2,128,128]{3,2,1,0:T(8,128)(2,1)S(1)}, u32[]{:S(2)}, u32[]{:S(2)}) collective-permute-start(bf16[2,2,128,128]{3,2,1,0:T(8,128)(2,1)} %get-tuple-element.39), channel_id=1, source_target_pairs={{0,8},{1,9},{2,10},{3,11},{4,12},{5,13},{6,14},{7,15},{8,0},{9,1},... | collective-permute-start | bytes 393224 | tf_op jit(solution)/shard_map/ppermute | solution.py:38
  10.6 1.0 collective-permute-start.5
  11.6 3.9 %shard_map.104 = (bf16[2064,128]{1,0:T(8,128)(2,1)}, bf16[2064,128]{1,0:T(8,128)(2,1)}, bf16[2064,128]{1,0:T(8,128)(2,1)}, bf16[2064,128]{1,0:T(8,128)(2,1)}) custom-call(s32[4]{0:T(128)} %pad_add_fusion.place.refs_0_, bf16[2,128,4,8,128]{4,3,2,1,0:T(8,128)(2,1)} %bitcast.28, bf16[2,128,4,8,128]{4,3,2,1,0:T(8,128)(2,1)} %bitcast.30, ...), custom_call_target="tpu_custom_call" | custom-call | tf_op jit(solution)/shard_map/pallas_call | solution.py:82
  15.5 1.3 collective-permute-done.4
  17.0 1.6 %collective-permute-start.6 = (bf16[4,2,128,128]{3,2,1,0:T(8,128)(2,1)S(1)}, bf16[4,2,128,128]{3,2,1,0:T(8,128)(2,1)S(1)}, u32[]{:S(2)}, u32[]{:S(2)}) collective-permute-start(bf16[4,2,128,128]{3,2,1,0:T(8,128)(2,1)S(1)} %pad_maximum_fusion.refs_6_), channel_id=1, source_target_pairs={{0,1},{1,2},{2,3},{3,0},{4,5},{5,6},{6,7},{7,4},{8,9},{9,10},{10,1... | collective-permute-start | bytes 786440 | tf_op jit(solution)/shard_map/ppermute | solution.py:38
  18.5 2.1 %collective-permute-start = (bf16[2064,128]{1,0:T(8,128)(2,1)}, bf16[2064,128]{1,0:T(8,128)(2,1)S(1)}, u32[]{:S(2)}, u32[]{:S(2)}) collective-permute-start(bf16[2064,128]{1,0:T(8,128)(2,1)} %get-tuple-element.42), channel_id=1, source_target_pairs={{0,12},{1,13},{2,14},{3,15},{4,0},{5,1},{6,2},{7,3},{8,4},{9,5},{1... | collective-permute-start | bytes 1585160 | tf_op jit(solution)/shard_map/ppermute | solution.py:38
  20.6 2.2 %collective-permute-start.2 = (bf16[2064,128]{1,0:T(8,128)(2,1)}, bf16[2064,128]{1,0:T(8,128)(2,1)S(1)}, u32[]{:S(2)}, u32[]{:S(2)}) collective-permute-start(bf16[2064,128]{1,0:T(8,128)(2,1)} %get-tuple-element.45), channel_id=1, source_target_pairs={{0,8},{1,9},{2,10},{3,11},{4,12},{5,13},{6,14},{7,15},{8,0},{9,1},... | collective-permute-start | bytes 1585160 | tf_op jit(solution)/shard_map/ppermute | solution.py:38
  22.8 2.7 %collective-permute-start.7 = (bf16[4,2,128,128]{3,2,1,0:T(8,128)(2,1)S(1)}, bf16[4,2,128,128]{3,2,1,0:T(8,128)(2,1)S(1)}, u32[]{:S(2)}, u32[]{:S(2)}) collective-permute-start(bf16[4,2,128,128]{3,2,1,0:T(8,128)(2,1)S(1)} %pad_maximum_fusion.refs_6_), channel_id=1, source_target_pairs={{0,2},{1,3},{2,0},{3,1},{4,6},{5,7},{6,4},{7,5},{8,10},{9,11},{10,... | collective-permute-start | bytes 786440 | tf_op jit(solution)/shard_map/ppermute | solution.py:38
  25.5 0.5 collective-permute-done.6.refs_7_
  26.0 2.5 %collective-permute-start.8 = (bf16[4,2,128,128]{3,2,1,0:T(8,128)(2,1)S(1)}, bf16[4,2,128,128]{3,2,1,0:T(8,128)(2,1)S(1)}, u32[]{:S(2)}, u32[]{:S(2)}) collective-permute-start(bf16[4,2,128,128]{3,2,1,0:T(8,128)(2,1)S(1)} %pad_maximum_fusion.refs_6_), channel_id=1, source_target_pairs={{0,3},{1,0},{2,1},{3,2},{4,7},{5,4},{6,5},{7,6},{8,11},{9,8},{10,9... | collective-permute-start | bytes 786440 | tf_op jit(solution)/shard_map/ppermute | solution.py:38
  28.6 4.1 %collective-permute-done.7.refs_8_ = bf16[4,2,128,128]{3,2,1,0:T(8,128)(2,1)S(1)} collective-permute-done((bf16[4,2,128,128]{3,2,1,0:T(8,128)(2,1)S(1)}, bf16[4,2,128,128]{3,2,1,0:T(8,128)(2,1)S(1)}, u32[]{:S(2)}, u32[]{:S(2)}) %collective-permute-start.7) | collective-permute-done | bytes 262176 | tf_op jit(solution)/shard_map/ppermute | solution.py:38
  32.7 2.0 %collective-permute-start.12 = (bf16[4,2,128,128]{3,2,1,0:T(8,128)(2,1)S(1)}, bf16[4,2,128,128]{3,2,1,0:T(8,128)(2,1)S(1)}, u32[]{:S(2)}, u32[]{:S(2)}) collective-permute-start(bf16[4,2,128,128]{3,2,1,0:T(8,128)(2,1)S(1)} %pad_maximum_fusion.1.refs_6_), channel_id=1, source_target_pairs={{0,1},{1,2},{2,3},{3,0},{4,5},{5,6},{6,7},{7,4},{8,9},{9,10},{10,1... | collective-permute-start | bytes 786440 | tf_op jit(solution)/shard_map/ppermute | solution.py:38
  34.8 3.8 %shard_map.106 = (bf16[2064,128]{1,0:T(8,128)(2,1)}, bf16[2064,128]{1,0:T(8,128)(2,1)}, bf16[2064,128]{1,0:T(8,128)(2,1)}, bf16[2064,128]{1,0:T(8,128)(2,1)}) custom-call(s32[4]{0:T(128)} %pad_add_fusion.place.refs_0_, bf16[2,128,4,8,128]{4,3,2,1,0:T(8,128)(2,1)} %bitcast.29, bf16[2,128,4,8,128]{4,3,2,1,0:T(8,128)(2,1)} %bitcast.31, ...), custom_call_target="tpu_custom_call" | custom-call | tf_op jit(solution)/shard_map/pallas_call | solution.py:82
  39.3 0.5 convert_divide_fusion.refs_1_
  39.9 1.7 %collective-permute-start.13 = (bf16[4,2,128,128]{3,2,1,0:T(8,128)(2,1)S(1)}, bf16[4,2,128,128]{3,2,1,0:T(8,128)(2,1)}, u32[]{:S(2)}, u32[]{:S(2)}) collective-permute-start(bf16[4,2,128,128]{3,2,1,0:T(8,128)(2,1)S(1)} %pad_maximum_fusion.1.refs_6_), channel_id=1, source_target_pairs={{0,2},{1,3},{2,0},{3,1},{4,6},{5,7},{6,4},{7,5},{8,10},{9,11},{10,... | collective-permute-start | bytes 786440 | tf_op jit(solution)/shard_map/ppermute | solution.py:38
  41.6 1.2 collective-permute-start.14
  42.7 6.0 %collective-permute-done.refs_2_ = bf16[2064,128]{1,0:T(8,128)(2,1)S(1)} collective-permute-done((bf16[2064,128]{1,0:T(8,128)(2,1)}, bf16[2064,128]{1,0:T(8,128)(2,1)S(1)}, u32[]{:S(2)}, u32[]{:S(2)}) %collective-permute-start) | collective-permute-done | bytes 528416 | tf_op jit(solution)/shard_map/ppermute | solution.py:38
  48.7 4.4 %collective-permute-done.1.refs_4_ = bf16[2064,128]{1,0:T(8,128)(2,1)S(1)} collective-permute-done((bf16[2064,128]{1,0:T(8,128)(2,1)}, bf16[2064,128]{1,0:T(8,128)(2,1)S(1)}, u32[]{:S(2)}, u32[]{:S(2)}) %collective-permute-start.1) | collective-permute-done | bytes 528416 | tf_op jit(solution)/shard_map/ppermute | solution.py:38
  53.1 0.2 collective-permute-start.10
  53.3 3.1 %collective-permute-start.11 = (bf16[2064,128]{1,0:T(8,128)(2,1)}, bf16[2064,128]{1,0:T(8,128)(2,1)}, u32[]{:S(2)}, u32[]{:S(2)}) collective-permute-start(bf16[2064,128]{1,0:T(8,128)(2,1)} %get-tuple-element.58), channel_id=1, source_target_pairs={{0,12},{1,13},{2,14},{3,15},{4,0},{5,1},{6,2},{7,3},{8,4},{9,5},{1... | collective-permute-start | bytes 1585160 | tf_op jit(solution)/shard_map/ppermute | solution.py:38
  56.4 14.3 %shard_map.105 = (bf16[1024,128]{1,0:T(8,128)(2,1)}, bf16[1024,128]{1,0:T(8,128)(2,1)}, bf16[1024,128]{1,0:T(8,128)(2,1)}, bf16[1024,128]{1,0:T(8,128)(2,1)}, bf16[16,2,128,128]{3,2,1,0:T(8,128)(2,1)}) custom-call(s32[4]{0:T(128)} %pad_add_fusion.place.refs_0_, f32[2]{0:T(128)} %convert_divide_fusion.refs_1_, bf16[2064,128]{1,0:T(8,128)(2,1)} %copy-done.10, ...), custom_call_target="tpu_custom_call" | custom-call | flops 10737418240 | bytes 8388608 | tf_op jit(solution)/shard_map/pallas_call | solution.py:288
  70.8 3.8 %all-to-all-start = ((bf16[16,2,128,128]{3,2,1,0:T(8,128)(2,1)}), bf16[16,2,128,128]{3,2,1,0:T(8,128)(2,1)S(1)}, u32[]{:S(2)}, u32[]{:S(2)}) async-start(bf16[16,2,128,128]{3,2,1,0:T(8,128)(2,1)} %get-tuple-element.50), calls=%async_computation | async-start | bytes 2097152 | tf_op jit(solution)/shard_map/all_to_all | solution.py:389
  74.6 3.2 %collective-permute-start.15 = (bf16[1024,128]{1,0:T(8,128)(2,1)S(1)}, bf16[1024,128]{1,0:T(8,128)(2,1)S(1)}, u32[]{:S(2)}, u32[]{:S(2)}) collective-permute-start(bf16[1024,128]{1,0:T(8,128)(2,1)S(1)} %copy-done.19), channel_id=1, source_target_pairs={{0,12},{1,13},{2,14},{3,15},{4,0},{5,1},{6,2},{7,3},{8,4},{9,5},{1... | collective-permute-start | bytes 786440 | tf_op jit(solution)/shard_map/ppermute | solution.py:38
  77.8 0.8 collective-permute-start.16
  78.6 0.9 collective-permute-start.17
  79.5 14.3 %shard_map.107 = (bf16[1024,128]{1,0:T(8,128)(2,1)}, bf16[1024,128]{1,0:T(8,128)(2,1)}, bf16[1024,128]{1,0:T(8,128)(2,1)}, bf16[1024,128]{1,0:T(8,128)(2,1)}, bf16[16,2,128,128]{3,2,1,0:T(8,128)(2,1)}) custom-call(s32[4]{0:T(128)} %pad_add_fusion.place.refs_0_, f32[2]{0:T(128)} %convert_divide_fusion.refs_1_, ...), custom_call_target="tpu_custom_call" | custom-call | flops 10737418240 | bytes 8388608 | tf_op jit(solution)/shard_map/pallas_call | solution.py:288
  93.8 1.2 collective-permute-done.15.refs_1_
  95.0 1.6 %collective-permute-done.16.refs_2_ = bf16[1024,128]{1,0:T(8,128)(2,1)S(1)} collective-permute-done((bf16[1024,128]{1,0:T(8,128)(2,1)S(1)}, bf16[1024,128]{1,0:T(8,128)(2,1)S(1)}, u32[]{:S(2)}, u32[]{:S(2)}) %collective-permute-start.16) | collective-permute-done | bytes 262176 | tf_op jit(solution)/shard_map/ppermute | solution.py:38
  96.6 5.0 %collective-permute-done.17.refs_3_ = bf16[1024,128]{1,0:T(8,128)(2,1)S(1)} collective-permute-done((bf16[1024,128]{1,0:T(8,128)(2,1)S(1)}, bf16[1024,128]{1,0:T(8,128)(2,1)S(1)}, u32[]{:S(2)}, u32[]{:S(2)}) %collective-permute-start.17) | collective-permute-done | bytes 262176 | tf_op jit(solution)/shard_map/ppermute | solution.py:38
  101.6 5.0 %all-to-all-start.1 = ((bf16[16,2,128,128]{3,2,1,0:T(8,128)(2,1)}), bf16[16,2,128,128]{3,2,1,0:T(8,128)(2,1)S(1)}, u32[]{:S(2)}, u32[]{:S(2)}) async-start(bf16[16,2,128,128]{3,2,1,0:T(8,128)(2,1)} %get-tuple-element.65), calls=%async_computation.1 | async-start | bytes 2097152 | tf_op jit(solution)/shard_map/all_to_all | solution.py:389
  106.6 3.1 %collective-permute-start.18 = (bf16[1024,128]{1,0:T(8,128)(2,1)}, bf16[1024,128]{1,0:T(8,128)(2,1)S(1)}, u32[]{:S(2)}, u32[]{:S(2)}) collective-permute-start(bf16[1024,128]{1,0:T(8,128)(2,1)} %get-tuple-element.68), channel_id=1, source_target_pairs={{0,12},{1,13},{2,14},{3,15},{4,0},{5,1},{6,2},{7,3},{8,4},{9,5},{1... | collective-permute-start | bytes 786440 | tf_op jit(solution)/shard_map/ppermute | solution.py:38
  109.8 0.9 collective-permute-start.19
  110.6 0.9 collective-permute-start.20
  111.5 0.6 reduce_sum.27
  112.1 9.2 %psum.7 = s32[]{:T(128)} all-reduce(s32[]{:T(128)} %reduce_sum.27), channel_id=1, replica_groups=mesh['dp'=8,'seq'=16] {'dp'}, use_global_device_ids=true, to_apply=%region_1.2 | all-reduce | flops 1 | bytes 8 | tf_op jit(solution)/shard_map/psum | solution.py:393
  121.9 5.3 %collective-permute-done.18.refs_5_ = bf16[1024,128]{1,0:T(8,128)(2,1)S(1)} collective-permute-done((bf16[1024,128]{1,0:T(8,128)(2,1)}, bf16[1024,128]{1,0:T(8,128)(2,1)S(1)}, u32[]{:S(2)}, u32[]{:S(2)}) %collective-permute-start.18) | collective-permute-done | bytes 262176 | tf_op jit(solution)/shard_map/ppermute | solution.py:38
  127.2 0.9 collective-permute-done.19.refs_6_
  128.1 4.8 %collective-permute-done.20.refs_7_ = bf16[1024,128]{1,0:T(8,128)(2,1)} collective-permute-done((bf16[1024,128]{1,0:T(8,128)(2,1)}, bf16[1024,128]{1,0:T(8,128)(2,1)}, u32[]{:S(2)}, u32[]{:S(2)}) %collective-permute-start.20) | collective-permute-done | bytes 262176 | tf_op jit(solution)/shard_map/ppermute | solution.py:38
  132.9 3.4 %shard_map.108 = bf16[2,128,4,8,128]{4,3,2,1,0:T(8,128)(2,1)} custom-call(s32[4]{0:T(128)} %pad_add_fusion.place.refs_0_, f32[1]{0:T(128)} %bitcast.9.mean_len, bf16[1024,128]{1,0:T(8,128)(2,1)} %get-tuple-element.61.refs_0_, bf16[1024,128]{1,0:T(8,128)(2,1)} %copy-done, bf16[1024,128]{1,0:T(8,128)(2,1)} %copy-done.1, bf16[1024,128]{1,0:T(8,128)(2,1)} %copy-done.2, ...), custom_call_target="tpu_custom_call" | custom-call | tf_op jit(solution)/shard_map/pallas_call | solution.py:395
  136.3 0.2 convert_reduce_fusion.1
  136.5 0.2 convert_reduce_fusion
  136.8 0.9 copy.15
  137.7 0.9 copy.16
  (62 shorter events, 0.4 us)
Async XLA Ops:
  0.6 2.0 %copy-start.8 = (s32[2]{0:T(128)S(1)}, s32[2]{0:T(128)}, u32[]{:S(2)}) copy-start(s32[2]{0:T(128)} %param.13) | copy-start | bytes 28
  5.1 10.4 %collective-permute-start.3 = (bf16[2,2,128,128]{3,2,1,0:T(8,128)(2,1)}, bf16[2,2,128,128]{3,2,1,0:T(8,128)(2,1)S(1)}, u32[]{:S(2)}, u32[]{:S(2)}) collective-permute-start(bf16[2,2,128,128]{3,2,1,0:T(8,128)(2,1)} %get-tuple-element.38), channel_id=1, source_target_pairs={{0,4},{1,5},{2,6},{3,7},{4,8},{5,9},{6,10},{7,11},{8,12},{9,13},{1... | collective-permute-start | bytes 393224 | tf_op jit(solution)/shard_map/ppermute | solution.py:38
  7.0 9.8 %collective-permute-start.4 = (bf16[2,2,128,128]{3,2,1,0:T(8,128)(2,1)}, bf16[2,2,128,128]{3,2,1,0:T(8,128)(2,1)S(1)}, u32[]{:S(2)}, u32[]{:S(2)}) collective-permute-start(bf16[2,2,128,128]{3,2,1,0:T(8,128)(2,1)} %get-tuple-element.39), channel_id=1, source_target_pairs={{0,8},{1,9},{2,10},{3,11},{4,12},{5,13},{6,14},{7,15},{8,0},{9,1},... | collective-permute-start | bytes 393224 | tf_op jit(solution)/shard_map/ppermute | solution.py:38
  10.6 6.2 %collective-permute-start.5 = (bf16[2,2,128,128]{3,2,1,0:T(8,128)(2,1)}, bf16[2,2,128,128]{3,2,1,0:T(8,128)(2,1)S(1)}, u32[]{:S(2)}, u32[]{:S(2)}) collective-permute-start(bf16[2,2,128,128]{3,2,1,0:T(8,128)(2,1)} %get-tuple-element.40), channel_id=1, source_target_pairs={{0,12},{1,13},{2,14},{3,15},{4,0},{5,1},{6,2},{7,3},{8,4},{9,5},{1... | collective-permute-start | bytes 393224 | tf_op jit(solution)/shard_map/ppermute | solution.py:38
  11.6 5.3 %copy-start.7 = (bf16[2,2,128,128]{3,2,1,0:T(8,128)(2,1)S(1)}, bf16[2,2,128,128]{3,2,1,0:T(8,128)(2,1)}, u32[]{:S(2)}) copy-start(bf16[2,2,128,128]{3,2,1,0:T(8,128)(2,1)} %get-tuple-element.46) | copy-start | bytes 393220
  17.0 21.6 %copy-start.6 = (bf16[4,2,128,128]{3,2,1,0:T(8,128)(2,1)}, bf16[4,2,128,128]{3,2,1,0:T(8,128)(2,1)S(1)}, u32[]{:S(2)}) copy-start(bf16[4,2,128,128]{3,2,1,0:T(8,128)(2,1)S(1)} %pad_maximum_fusion.refs_6_) | copy-start | bytes 786436
  17.0 9.1 %collective-permute-start.6 = (bf16[4,2,128,128]{3,2,1,0:T(8,128)(2,1)S(1)}, bf16[4,2,128,128]{3,2,1,0:T(8,128)(2,1)S(1)}, u32[]{:S(2)}, u32[]{:S(2)}) collective-permute-start(bf16[4,2,128,128]{3,2,1,0:T(8,128)(2,1)S(1)} %pad_maximum_fusion.refs_6_), channel_id=1, source_target_pairs={{0,1},{1,2},{2,3},{3,0},{4,5},{5,6},{6,7},{7,4},{8,9},{9,10},{10,1... | collective-permute-start | bytes 786440 | tf_op jit(solution)/shard_map/ppermute | solution.py:38
  18.5 30.2 %collective-permute-start = (bf16[2064,128]{1,0:T(8,128)(2,1)}, bf16[2064,128]{1,0:T(8,128)(2,1)S(1)}, u32[]{:S(2)}, u32[]{:S(2)}) collective-permute-start(bf16[2064,128]{1,0:T(8,128)(2,1)} %get-tuple-element.42), channel_id=1, source_target_pairs={{0,12},{1,13},{2,14},{3,15},{4,0},{5,1},{6,2},{7,3},{8,4},{9,5},{1... | collective-permute-start | bytes 1585160 | tf_op jit(solution)/shard_map/ppermute | solution.py:38
  20.6 32.5 %collective-permute-start.1 = (bf16[2064,128]{1,0:T(8,128)(2,1)}, bf16[2064,128]{1,0:T(8,128)(2,1)S(1)}, u32[]{:S(2)}, u32[]{:S(2)}) collective-permute-start(bf16[2064,128]{1,0:T(8,128)(2,1)} %get-tuple-element.44), channel_id=1, source_target_pairs={{0,4},{1,5},{2,6},{3,7},{4,8},{5,9},{6,10},{7,11},{8,12},{9,13},{1... | collective-permute-start | bytes 1585160 | tf_op jit(solution)/shard_map/ppermute | solution.py:38
  20.6 32.7 %collective-permute-start.2 = (bf16[2064,128]{1,0:T(8,128)(2,1)}, bf16[2064,128]{1,0:T(8,128)(2,1)S(1)}, u32[]{:S(2)}, u32[]{:S(2)}) collective-permute-start(bf16[2064,128]{1,0:T(8,128)(2,1)} %get-tuple-element.45), channel_id=1, source_target_pairs={{0,8},{1,9},{2,10},{3,11},{4,12},{5,13},{6,14},{7,15},{8,0},{9,1},... | collective-permute-start | bytes 1585160 | tf_op jit(solution)/shard_map/ppermute | solution.py:38
  22.8 9.9 %collective-permute-start.7 = (bf16[4,2,128,128]{3,2,1,0:T(8,128)(2,1)S(1)}, bf16[4,2,128,128]{3,2,1,0:T(8,128)(2,1)S(1)}, u32[]{:S(2)}, u32[]{:S(2)}) collective-permute-start(bf16[4,2,128,128]{3,2,1,0:T(8,128)(2,1)S(1)} %pad_maximum_fusion.refs_6_), channel_id=1, source_target_pairs={{0,2},{1,3},{2,0},{3,1},{4,6},{5,7},{6,4},{7,5},{8,10},{9,11},{10,... | collective-permute-start | bytes 786440 | tf_op jit(solution)/shard_map/ppermute | solution.py:38
  26.0 12.6 %copy-start.14 = (bf16[4,2,128,128]{3,2,1,0:T(8,128)(2,1)}, bf16[4,2,128,128]{3,2,1,0:T(8,128)(2,1)S(1)}, u32[]{:S(2)}) copy-start(bf16[4,2,128,128]{3,2,1,0:T(8,128)(2,1)S(1)} %collective-permute-done.6.refs_7_) | copy-start | bytes 786436
  26.0 13.8 %collective-permute-start.8 = (bf16[4,2,128,128]{3,2,1,0:T(8,128)(2,1)S(1)}, bf16[4,2,128,128]{3,2,1,0:T(8,128)(2,1)S(1)}, u32[]{:S(2)}, u32[]{:S(2)}) collective-permute-start(bf16[4,2,128,128]{3,2,1,0:T(8,128)(2,1)S(1)} %pad_maximum_fusion.refs_6_), channel_id=1, source_target_pairs={{0,3},{1,0},{2,1},{3,2},{4,7},{5,4},{6,5},{7,6},{8,11},{9,8},{10,9... | collective-permute-start | bytes 786440 | tf_op jit(solution)/shard_map/ppermute | solution.py:38
  28.6 12.9 %copy-start.5 = (bf16[4,2,128,128]{3,2,1,0:T(8,128)(2,1)}, bf16[4,2,128,128]{3,2,1,0:T(8,128)(2,1)S(1)}, u32[]{:S(2)}) copy-start(bf16[4,2,128,128]{3,2,1,0:T(8,128)(2,1)S(1)} %pad_maximum_fusion.1.refs_6_) | copy-start | bytes 786436
  28.6 10.7 %copy-start.9 = (f32[2]{0:T(128)S(1)}, f32[2]{0:T(128)}, u32[]{:S(2)}) copy-start(f32[2]{0:T(128)} %constant.42.clone) | copy-start | bytes 28
  32.7 5.9 %copy-start.15 = (bf16[4,2,128,128]{3,2,1,0:T(8,128)(2,1)}, bf16[4,2,128,128]{3,2,1,0:T(8,128)(2,1)S(1)}, u32[]{:S(2)}) copy-start(bf16[4,2,128,128]{3,2,1,0:T(8,128)(2,1)S(1)} %collective-permute-done.7.refs_8_) | copy-start | bytes 786436
  32.7 8.8 %collective-permute-start.12 = (bf16[4,2,128,128]{3,2,1,0:T(8,128)(2,1)S(1)}, bf16[4,2,128,128]{3,2,1,0:T(8,128)(2,1)S(1)}, u32[]{:S(2)}, u32[]{:S(2)}) collective-permute-start(bf16[4,2,128,128]{3,2,1,0:T(8,128)(2,1)S(1)} %pad_maximum_fusion.1.refs_6_), channel_id=1, source_target_pairs={{0,1},{1,2},{2,3},{3,0},{4,5},{5,6},{6,7},{7,4},{8,9},{9,10},{10,1... | collective-permute-start | bytes 786440 | tf_op jit(solution)/shard_map/ppermute | solution.py:38
  39.9 16.5 %copy-start.16 = (bf16[4,2,128,128]{3,2,1,0:T(8,128)(2,1)}, bf16[4,2,128,128]{3,2,1,0:T(8,128)(2,1)S(1)}, u32[]{:S(2)}) copy-start(bf16[4,2,128,128]{3,2,1,0:T(8,128)(2,1)S(1)} %collective-permute-done.8.refs_9_) | copy-start | bytes 786436
  39.9 34.7 %collective-permute-start.13 = (bf16[4,2,128,128]{3,2,1,0:T(8,128)(2,1)S(1)}, bf16[4,2,128,128]{3,2,1,0:T(8,128)(2,1)}, u32[]{:S(2)}, u32[]{:S(2)}) collective-permute-start(bf16[4,2,128,128]{3,2,1,0:T(8,128)(2,1)S(1)} %pad_maximum_fusion.1.refs_6_), channel_id=1, source_target_pairs={{0,2},{1,3},{2,0},{3,1},{4,6},{5,7},{6,4},{7,5},{8,10},{9,11},{10,... | collective-permute-start | bytes 786440 | tf_op jit(solution)/shard_map/ppermute | solution.py:38
  41.5 29.2 %copy-start.13 = (bf16[4,2,128,128]{3,2,1,0:T(8,128)(2,1)}, bf16[4,2,128,128]{3,2,1,0:T(8,128)(2,1)S(1)}, u32[]{:S(2)}) copy-start(bf16[4,2,128,128]{3,2,1,0:T(8,128)(2,1)S(1)} %collective-permute-done.12.refs_7_) | copy-start | bytes 786436
  41.6 36.2 %collective-permute-start.14 = (bf16[4,2,128,128]{3,2,1,0:T(8,128)(2,1)S(1)}, bf16[4,2,128,128]{3,2,1,0:T(8,128)(2,1)}, u32[]{:S(2)}, u32[]{:S(2)}) collective-permute-start(bf16[4,2,128,128]{3,2,1,0:T(8,128)(2,1)S(1)} %pad_maximum_fusion.1.refs_6_), channel_id=1, source_target_pairs={{0,3},{1,0},{2,1},{3,2},{4,7},{5,4},{6,5},{7,6},{8,11},{9,8},{10,9... | collective-permute-start | bytes 786440 | tf_op jit(solution)/shard_map/ppermute | solution.py:38
  48.7 7.7 %copy-start.10 = (bf16[2064,128]{1,0:T(8,128)(2,1)}, bf16[2064,128]{1,0:T(8,128)(2,1)S(1)}, u32[]{:S(2)}) copy-start(bf16[2064,128]{1,0:T(8,128)(2,1)S(1)} %collective-permute-done.refs_2_) | copy-start | bytes 1585156
  48.7 29.9 %collective-permute-start.9 = (bf16[2064,128]{1,0:T(8,128)(2,1)}, bf16[2064,128]{1,0:T(8,128)(2,1)}, u32[]{:S(2)}, u32[]{:S(2)}) collective-permute-start(bf16[2064,128]{1,0:T(8,128)(2,1)} %get-tuple-element.56), channel_id=1, source_target_pairs={{0,8},{1,9},{2,10},{3,11},{4,12},{5,13},{6,14},{7,15},{8,0},{9,1},... | collective-permute-start | bytes 1585160 | tf_op jit(solution)/shard_map/ppermute | solution.py:38
  53.1 3.3 %copy-start.11 = (bf16[2064,128]{1,0:T(8,128)(2,1)}, bf16[2064,128]{1,0:T(8,128)(2,1)S(1)}, u32[]{:S(2)}) copy-start(bf16[2064,128]{1,0:T(8,128)(2,1)S(1)} %collective-permute-done.1.refs_4_) | copy-start | bytes 1585156
  53.1 26.3 %collective-permute-start.10 = (bf16[2064,128]{1,0:T(8,128)(2,1)}, bf16[2064,128]{1,0:T(8,128)(2,1)}, u32[]{:S(2)}, u32[]{:S(2)}) collective-permute-start(bf16[2064,128]{1,0:T(8,128)(2,1)} %get-tuple-element.57), channel_id=1, source_target_pairs={{0,4},{1,5},{2,6},{3,7},{4,8},{5,9},{6,10},{7,11},{8,12},{9,13},{1... | collective-permute-start | bytes 1585160 | tf_op jit(solution)/shard_map/ppermute | solution.py:38
  53.3 3.1 %copy-start.12 = (bf16[2064,128]{1,0:T(8,128)(2,1)}, bf16[2064,128]{1,0:T(8,128)(2,1)S(1)}, u32[]{:S(2)}) copy-start(bf16[2064,128]{1,0:T(8,128)(2,1)S(1)} %collective-permute-done.2.refs_5_) | copy-start | bytes 1585156
  53.3 26.2 %collective-permute-start.11 = (bf16[2064,128]{1,0:T(8,128)(2,1)}, bf16[2064,128]{1,0:T(8,128)(2,1)}, u32[]{:S(2)}, u32[]{:S(2)}) collective-permute-start(bf16[2064,128]{1,0:T(8,128)(2,1)} %get-tuple-element.58), channel_id=1, source_target_pairs={{0,12},{1,13},{2,14},{3,15},{4,0},{5,1},{6,2},{7,3},{8,4},{9,5},{1... | collective-permute-start | bytes 1585160 | tf_op jit(solution)/shard_map/ppermute | solution.py:38
  70.7 3.8 %copy-start.19 = (bf16[1024,128]{1,0:T(8,128)(2,1)S(1)}, bf16[1024,128]{1,0:T(8,128)(2,1)}, u32[]{:S(2)}) copy-start(bf16[1024,128]{1,0:T(8,128)(2,1)} %get-tuple-element.62) | copy-start | bytes 786436
  70.7 7.0 %copy-start.18 = (bf16[1024,128]{1,0:T(8,128)(2,1)S(1)}, bf16[1024,128]{1,0:T(8,128)(2,1)}, u32[]{:S(2)}) copy-start(bf16[1024,128]{1,0:T(8,128)(2,1)} %get-tuple-element.63) | copy-start | bytes 786436
  70.8 7.8 %copy-start.17 = (bf16[1024,128]{1,0:T(8,128)(2,1)S(1)}, bf16[1024,128]{1,0:T(8,128)(2,1)}, u32[]{:S(2)}) copy-start(bf16[1024,128]{1,0:T(8,128)(2,1)} %get-tuple-element.64) | copy-start | bytes 786436
  70.8 30.9 %all-to-all-start = ((bf16[16,2,128,128]{3,2,1,0:T(8,128)(2,1)}), bf16[16,2,128,128]{3,2,1,0:T(8,128)(2,1)S(1)}, u32[]{:S(2)}, u32[]{:S(2)}) async-start(bf16[16,2,128,128]{3,2,1,0:T(8,128)(2,1)} %get-tuple-element.50), calls=%async_computation | async-start | bytes 2097152 | tf_op jit(solution)/shard_map/all_to_all | solution.py:389
  74.6 20.4 %collective-permute-start.15 = (bf16[1024,128]{1,0:T(8,128)(2,1)S(1)}, bf16[1024,128]{1,0:T(8,128)(2,1)S(1)}, u32[]{:S(2)}, u32[]{:S(2)}) collective-permute-start(bf16[1024,128]{1,0:T(8,128)(2,1)S(1)} %copy-done.19), channel_id=1, source_target_pairs={{0,12},{1,13},{2,14},{3,15},{4,0},{5,1},{6,2},{7,3},{8,4},{9,5},{1... | collective-permute-start | bytes 786440 | tf_op jit(solution)/shard_map/ppermute | solution.py:38
  77.8 18.8 %collective-permute-start.16 = (bf16[1024,128]{1,0:T(8,128)(2,1)S(1)}, bf16[1024,128]{1,0:T(8,128)(2,1)S(1)}, u32[]{:S(2)}, u32[]{:S(2)}) collective-permute-start(bf16[1024,128]{1,0:T(8,128)(2,1)S(1)} %copy-done.18), channel_id=1, source_target_pairs={{0,8},{1,9},{2,10},{3,11},{4,12},{5,13},{6,14},{7,15},{8,0},{9,1},... | collective-permute-start | bytes 786440 | tf_op jit(solution)/shard_map/ppermute | solution.py:38
  78.6 23.1 %collective-permute-start.17 = (bf16[1024,128]{1,0:T(8,128)(2,1)S(1)}, bf16[1024,128]{1,0:T(8,128)(2,1)S(1)}, u32[]{:S(2)}, u32[]{:S(2)}) collective-permute-start(bf16[1024,128]{1,0:T(8,128)(2,1)S(1)} %copy-done.17), channel_id=1, source_target_pairs={{0,4},{1,5},{2,6},{3,7},{4,8},{5,9},{6,10},{7,11},{8,12},{9,13},{1... | collective-permute-start | bytes 786440 | tf_op jit(solution)/shard_map/ppermute | solution.py:38
  95.0 37.9 %copy-start = (bf16[1024,128]{1,0:T(8,128)(2,1)}, bf16[1024,128]{1,0:T(8,128)(2,1)S(1)}, u32[]{:S(2)}) copy-start(bf16[1024,128]{1,0:T(8,128)(2,1)S(1)} %collective-permute-done.15.refs_1_) | copy-start | bytes 786436
  96.6 36.3 %copy-start.1 = (bf16[1024,128]{1,0:T(8,128)(2,1)}, bf16[1024,128]{1,0:T(8,128)(2,1)S(1)}, u32[]{:S(2)}) copy-start(bf16[1024,128]{1,0:T(8,128)(2,1)S(1)} %collective-permute-done.16.refs_2_) | copy-start | bytes 786436
  101.6 31.3 %copy-start.2 = (bf16[1024,128]{1,0:T(8,128)(2,1)}, bf16[1024,128]{1,0:T(8,128)(2,1)S(1)}, u32[]{:S(2)}) copy-start(bf16[1024,128]{1,0:T(8,128)(2,1)S(1)} %collective-permute-done.17.refs_3_) | copy-start | bytes 786436
  101.6 34.8 %all-to-all-start.1 = ((bf16[16,2,128,128]{3,2,1,0:T(8,128)(2,1)}), bf16[16,2,128,128]{3,2,1,0:T(8,128)(2,1)S(1)}, u32[]{:S(2)}, u32[]{:S(2)}) async-start(bf16[16,2,128,128]{3,2,1,0:T(8,128)(2,1)} %get-tuple-element.65), calls=%async_computation.1 | async-start | bytes 2097152 | tf_op jit(solution)/shard_map/all_to_all | solution.py:389
  106.6 20.6 %collective-permute-start.18 = (bf16[1024,128]{1,0:T(8,128)(2,1)}, bf16[1024,128]{1,0:T(8,128)(2,1)S(1)}, u32[]{:S(2)}, u32[]{:S(2)}) collective-permute-start(bf16[1024,128]{1,0:T(8,128)(2,1)} %get-tuple-element.68), channel_id=1, source_target_pairs={{0,12},{1,13},{2,14},{3,15},{4,0},{5,1},{6,2},{7,3},{8,4},{9,5},{1... | collective-permute-start | bytes 786440 | tf_op jit(solution)/shard_map/ppermute | solution.py:38
  109.8 18.4 %collective-permute-start.19 = (bf16[1024,128]{1,0:T(8,128)(2,1)}, bf16[1024,128]{1,0:T(8,128)(2,1)S(1)}, u32[]{:S(2)}, u32[]{:S(2)}) collective-permute-start(bf16[1024,128]{1,0:T(8,128)(2,1)} %get-tuple-element.69), channel_id=1, source_target_pairs={{0,8},{1,9},{2,10},{3,11},{4,12},{5,13},{6,14},{7,15},{8,0},{9,1},... | collective-permute-start | bytes 786440 | tf_op jit(solution)/shard_map/ppermute | solution.py:38
  110.6 22.3 %collective-permute-start.20 = (bf16[1024,128]{1,0:T(8,128)(2,1)}, bf16[1024,128]{1,0:T(8,128)(2,1)}, u32[]{:S(2)}, u32[]{:S(2)}) collective-permute-start(bf16[1024,128]{1,0:T(8,128)(2,1)} %get-tuple-element.70), channel_id=1, source_target_pairs={{0,4},{1,5},{2,6},{3,7},{4,8},{5,9},{6,10},{7,11},{8,12},{9,13},{1... | collective-permute-start | bytes 786440 | tf_op jit(solution)/shard_map/ppermute | solution.py:38
  127.2 5.7 %copy-start.3 = (bf16[1024,128]{1,0:T(8,128)(2,1)}, bf16[1024,128]{1,0:T(8,128)(2,1)S(1)}, u32[]{:S(2)}) copy-start(bf16[1024,128]{1,0:T(8,128)(2,1)S(1)} %collective-permute-done.18.refs_5_) | copy-start | bytes 786436
  128.1 4.8 %copy-start.4 = (bf16[1024,128]{1,0:T(8,128)(2,1)}, bf16[1024,128]{1,0:T(8,128)(2,1)S(1)}, u32[]{:S(2)}) copy-start(bf16[1024,128]{1,0:T(8,128)(2,1)S(1)} %collective-permute-done.19.refs_6_) | copy-start | bytes 786436
